TPU v7x, 32 devices: a whole 2x2x4 slice. The times are simulated.
32 devices in a mesh: groups: 2 (over y), row: 4 (over z), col: 2 (over x), depth: 2 (over core).
Axes of the slice: x: 2, y: 2, z: 4, core: 2. Of those that a mesh axis runs over, the one named last changes fastest.
Arguments:
- layer_input: bfloat16 [2, 1024, 4096], P('depth', ('groups', 'row'), 'col'), parts along dimension 1, may hold values from -6 to 6
- out_grad: bfloat16 [2, 1024, 4096], P('depth', ('groups', 'row'), 'col'), parts along dimension 1, may hold values from -0.1875 to 0.1875
- down_codes: bfloat16 [4096, 14336], P('col', 'row'), may hold values from -0.09375 to 0.09375
- down_scales: float32 [32, 112], P('col', 'row'), may hold values from 0.3 to 3
- gate_pre: bfloat16 [2, 1024, 14336], P('depth', ('groups', 'col'), 'row'), parts along dimension 1, may hold values from -8 to 8
- up_pre: bfloat16 [2, 1024, 14336], P('depth', ('groups', 'col'), 'row'), parts along dimension 1, may hold values from -6 to 6
Outputs:
- grad_gate: float32 [28672, 4096], P(('groups', 'row'), ('col', 'depth')), parts along dimension 0
- grad_up: float32 [28672, 4096], P(('groups', 'row'), ('col', 'depth')), parts along dimension 0
There are 2 independent parts, one for each index of `groups`. A program takes and returns all parts, laid end to end along the dimension named above; an argument that names none is the same for every part. Nothing has to cross between parts.
All inputs are finite; a program needn't handle non-finite values.
Results may differ from a plain program's by a relative error of at most 0.0095.
Values may be sent and summed in bfloat16 or wider, within the bound.
No kernel may reach another device: no remote copies, remote signals or barrier semaphores. Data moves between devices by JAX's collectives and lax.ppermute only.
A program may use at most 256 MiB of HBM per device.

v0:
```python
import jax
import jax.numpy as jnp
from jax import lax
from jax.sharding import PartitionSpec as P


def from_partner(shard, axis, apart):
    return lax.ppermute(shard, axis, [(i, i ^ 1 << apart) for i in range(lax.axis_size(axis))])


def contract_tokens(left, right):
    return lax.dot_general(
        left, right, (((0,), (0,)), ((), ())), preferred_element_type=jnp.float32
    )


def on_device(layer_input, out_grad, down_codes, down_scales, gate_pre, up_pre):
    feature_rows, hidden_cols = down_codes.shape
    blocks_feat, blocks_hidden = down_scales.shape
    block_side = feature_rows // blocks_feat
    scaled = down_codes.astype(jnp.float32).reshape(
        blocks_feat, block_side, blocks_hidden, block_side
    )
    scaled = scaled * down_scales[:, None, :, None]
    down_weight = scaled.reshape(feature_rows, hidden_cols).astype(jnp.bfloat16)
    grads_all, inputs_all = (
        lax.all_gather(out_grad, "row", axis=1, tiled=True),
        lax.all_gather(layer_input, "row", axis=1, tiled=True),
    )
    grad_rows = grads_all[0]
    selected = grad_rows
    hidden_grad = lax.psum_scatter(
        jnp.dot(selected, down_weight, preferred_element_type=jnp.float32).astype(jnp.bfloat16),
        "col",
        scatter_dimension=0,
        tiled=True,
    ).astype(jnp.float32)
    gates = gate_pre[0].astype(jnp.float32)
    ups = up_pre[0].astype(jnp.float32)
    sigmoid_gate = 1.0 / (1.0 + jnp.exp(-gates))
    d_gate = (hidden_grad * ups * sigmoid_gate * (1.0 + gates * (1.0 - sigmoid_gate))).astype(
        jnp.bfloat16
    )
    d_up = (hidden_grad * gates * sigmoid_gate).astype(jnp.bfloat16)
    input_rows = inputs_all[0]
    selected = input_rows
    gate_terms = contract_tokens(lax.all_gather(d_gate, "col", axis=0, tiled=True), selected)
    up_terms = contract_tokens(lax.all_gather(d_up, "col", axis=0, tiled=True), selected)
    half_cols = gate_terms.shape[1] // 2
    depth_index = lax.axis_index("depth")
    keep_start = depth_index * half_cols
    send_start = (1 - depth_index) * half_cols
    keep_gate = lax.dynamic_slice_in_dim(gate_terms, keep_start, half_cols, 1)
    keep_up = lax.dynamic_slice_in_dim(up_terms, keep_start, half_cols, 1)
    send_gate = lax.dynamic_slice_in_dim(gate_terms, send_start, half_cols, 1)
    send_up = lax.dynamic_slice_in_dim(up_terms, send_start, half_cols, 1)
    other_gate, other_up = (
        from_partner(send_gate.astype(jnp.bfloat16), "depth", 0).astype(send_gate.dtype),
        from_partner(send_up.astype(jnp.bfloat16), "depth", 0).astype(send_up.dtype),
    )
    return (keep_gate + other_gate, keep_up + other_up)


def solution(mesh):
    in_specs = (
        P("depth", ("groups", "row"), "col"),
        P("depth", ("groups", "row"), "col"),
        P("col", "row"),
        P("col", "row"),
        P("depth", ("groups", "col"), "row"),
        P("depth", ("groups", "col"), "row"),
    )
    out_specs = (P(("groups", "row"), ("col", "depth")), P(("groups", "row"), ("col", "depth")))
    return jax.shard_map(
        on_device, mesh=mesh, in_specs=in_specs, out_specs=out_specs, check_vma=False
    )
```

profile of v0, /device:TPU:0, one launch (start us, length us, event | category | flops | bytes accessed | tf_op | source)
XLA Modules:
  0.0 355.0 jit_solution(6338483432105480138)
XLA Ops:
  7.2 0.0 all-gather.5.cloned.1.call-start
  7.2 0.7 all-gather.5.cloned.1.call-update
  7.9 0.0 reduce-scatter.2.cloned.1.call-start
  7.9 0.8 copy.11
  8.7 20.3 %copy.10 = bf16[2048,3584]{0,1:T(8,128)(2,1)} copy(bf16[2048,3584]{1,0:T(8,128)(2,1)} %param.8) | data formatting | bytes 29360128 | tf_op args[2]
  29.0 29.2 %all-gather.5.cloned.1.call-done = bf16[1,512,2048]{2,1,0:T(8,128)(2,1)} async-done(((bf16[1,128,2048]{2,1,0:T(8,128)(2,1)}), bf16[1,512,2048]{2,1,0:T(8,128)(2,1)}) %all-gather.5.cloned.1.call-update) | async-done | bytes 2097168 | tf_op jit(solution)/shard_map/all_gather | solution.py:27
  58.2 0.0 copy-start.2
  58.2 11.6 %mul.35 = f32[16,128,28,128]{1,0,3,2:T(8,128)} broadcast(f32[16,28]{0,1:T(8,128)S(1)} %copy.11), dimensions={0,2} | broadcast | bytes 29361920 | tf_op jit(solution)/shard_map/mul | solution.py:24
  69.9 0.0 copy-done.2
  69.9 22.4 %fusion.6 = bf16[512,3584]{0,1:T(8,128)(2,1)} fusion(f32[448,8,16,128]{3,2,1,0:T(8,128)} %bitcast.32, bf16[2048,3584]{0,1:T(8,128)(2,1)} %copy.10, bf16[1,512,2048]{2,1,0:T(8,128)(2,1)S(1)} %copy-done.2), kind=kOutput, calls=%fused_computation.11 | convolution fusion | flops 7540047872 | bytes 49807360 | tf_op jit(solution)/shard_map/dot_general | solution.py:33
  92.3 0.0 reduce-scatter.2.cloned.1.call-update
  92.3 0.0 all-gather.9.cloned.1.call-start
  92.4 0.7 all-gather.9.cloned.1.call-update
  93.1 0.0 all-gather.7.cloned.1.call-start
  93.1 2.9 copy.13
  96.0 4.0 %copy.12 = bf16[1,256,3584]{1,2,0:T(8,128)(2,1)} copy(bf16[1,256,3584]{2,1,0:T(8,128)(2,1)} %param.11) | data formatting | bytes 3670016 | tf_op args[5]
  100.0 40.3 %reduce-scatter.2.cloned.1.call-done = bf16[256,3584]{0,1:T(8,128)(2,1)} async-done(((bf16[512,3584]{0,1:T(8,128)(2,1)}), bf16[256,3584]{0,1:T(8,128)(2,1)}) %reduce-scatter.2.cloned.1.call-update) | async-done | bytes 1835024 | tf_op jit(solution)/shard_map/reduce_scatter | solution.py:32
  140.3 4.6 %fusion.17 = (bf16[256,3584]{0,1:T(8,128)(2,1)}, bf16[256,3584]{0,1:T(8,128)(2,1)}) fusion(bf16[256,3584]{0,1:T(8,128)(2,1)} %reduce-scatter.2.cloned.1.call-done, bf16[1,256,3584]{1,2,0:T(8,128)(2,1)S(1)} %copy.13, bf16[1,256,3584]{1,2,0:T(8,128)(2,1)} %copy.12), kind=kLoop, calls=%fused_computation.21 | loop fusion | flops 14680064 | bytes 9175040 | tf_op jit(solution)/shard_map/convert_element_type | solution.py:44
  144.9 0.0 all-gather.7.cloned.1.call-update
  144.9 0.2 all-gather.11.cloned.1.call-start
  145.2 0.4 all-gather.11.cloned.1.call-update
  145.5 42.4 %all-gather.9.cloned.1.call-done = bf16[1,512,2048]{2,1,0:T(8,128)(2,1)} async-done(((bf16[1,128,2048]{2,1,0:T(8,128)(2,1)}), bf16[1,512,2048]{2,1,0:T(8,128)(2,1)}) %all-gather.9.cloned.1.call-update) | async-done | bytes 2097168 | tf_op jit(solution)/shard_map/all_gather | solution.py:28
  187.9 51.6 %all-gather.7.cloned.1.call-done = bf16[512,3584]{0,1:T(8,128)(2,1)} async-done(((bf16[256,3584]{0,1:T(8,128)(2,1)}), bf16[512,3584]{0,1:T(8,128)(2,1)}) %all-gather.7.cloned.1.call-update) | async-done | bytes 3670032 | tf_op jit(solution)/shard_map/all_gather | solution.py:47
  239.5 17.0 %fusion.20 = f32[3584,2048]{1,0:T(8,128)} fusion(bf16[512,3584]{0,1:T(8,128)(2,1)} %all-gather.7.cloned.1.call-done, bf16[1,512,2048]{2,1,0:T(8,128)(2,1)} %all-gather.9.cloned.1.call-done), kind=kOutput, calls=%fused_computation.24 | convolution fusion | flops 7516192768 | bytes 35127296 | tf_op jit(solution)/shard_map/dot_general | solution.py:12
  256.5 0.0 copy-start.1
  256.5 9.8 %dynamic-slice_convert_fusion.1 = bf16[3584,1024]{1,0:T(8,128)(2,1)} fusion(f32[3584,2048]{1,0:T(8,128)} %fusion.20, s32[]{:T(128)S(6)} %select_n.9), kind=kLoop, calls=%fused_computation.6 | loop fusion | bytes 14680068 | tf_op jit(solution)/shard_map/convert_element_type | solution.py:58
  266.3 0.0 collective-permute-start
  266.3 26.1 %all-gather.11.cloned.1.call-done = bf16[512,3584]{0,1:T(8,128)(2,1)} async-done(((bf16[256,3584]{0,1:T(8,128)(2,1)}), bf16[512,3584]{0,1:T(8,128)(2,1)}) %all-gather.11.cloned.1.call-update) | async-done | bytes 3670032 | tf_op jit(solution)/shard_map/all_gather | solution.py:48
  292.4 0.0 copy-done.1
  292.4 15.6 %fusion.18 = f32[3584,2048]{1,0:T(8,128)} fusion(bf16[512,3584]{0,1:T(8,128)(2,1)} %all-gather.11.cloned.1.call-done, bf16[1,512,2048]{2,1,0:T(8,128)(2,1)S(1)} %copy-done.1), kind=kOutput, calls=%fused_computation.22 | convolution fusion | flops 7516192768 | bytes 35127296 | tf_op jit(solution)/shard_map/dot_general | solution.py:12
  308.0 9.5 %dynamic-slice_convert_fusion = bf16[3584,1024]{1,0:T(8,128)(2,1)} fusion(f32[3584,2048]{1,0:T(8,128)} %fusion.18, s32[]{:T(128)S(6)} %select_n.9), kind=kLoop, calls=%fused_computation.4 | loop fusion | bytes 14680068 | tf_op jit(solution)/shard_map/convert_element_type | solution.py:59
  317.5 0.0 collective-permute-start.1
  317.5 0.0 collective-permute-done
  317.5 0.0 copy-start
  317.5 13.7 %convert_add_fusion.1 = f32[3584,1024]{1,0:T(8,128)} fusion(bf16[3584,1024]{1,0:T(8,128)(2,1)} %collective-permute-done, f32[3584,2048]{1,0:T(8,128)} %fusion.20, s32[]{:T(128)S(6)} %select_n.8), kind=kLoop, calls=%fused_computation.5 | loop fusion | flops 7340032 | bytes 36700164 | tf_op jit(solution)/shard_map/add | solution.py:61
  331.2 0.0 collective-permute-done.1
  331.2 7.3 %copy-done = f32[3584,2048]{1,0:T(8,128)S(1)} copy-done((f32[3584,2048]{1,0:T(8,128)S(1)}, f32[3584,2048]{1,0:T(8,128)}, u32[]{:S(2)}) %copy-start) | copy-done | bytes 29360152
  338.5 10.0 %convert_add_fusion = f32[3584,1024]{1,0:T(8,128)} fusion(bf16[3584,1024]{1,0:T(8,128)(2,1)} %collective-permute-done.1, f32[3584,2048]{1,0:T(8,128)S(1)} %copy-done, s32[]{:T(128)S(6)} %select_n.8), kind=kLoop, calls=%fused_computation.3 | loop fusion | flops 7340032 | bytes 36700164 | tf_op jit(solution)/shard_map/add | solution.py:61
Async XLA Ops:
  7.2 51.1 %all-gather.5.cloned.1.call-start = ((), (), s32[]{:S(2)}) async-start(), calls=%async_computation.1 | async-start | bytes 2621440 | tf_op jit(solution)/shard_map/all_gather | solution.py:27
  7.9 132.4 %reduce-scatter.2.cloned.1.call-start = ((), (), s32[]{:S(2)}) async-start(), calls=%async_computation.2 | async-start | bytes 5505024 | tf_op jit(solution)/shard_map/reduce_scatter | solution.py:32
  58.2 11.6 %copy-start.2 = (bf16[1,512,2048]{2,1,0:T(8,128)(2,1)S(1)}, bf16[1,512,2048]{2,1,0:T(8,128)(2,1)}, u32[]{:S(2)}) copy-start(bf16[1,512,2048]{2,1,0:T(8,128)(2,1)} %all-gather.5.cloned.1.call-done) | copy-start | bytes 6291460
  92.3 95.6 %all-gather.9.cloned.1.call-start = ((), (), s32[]{:S(2)}) async-start(), calls=%async_computation.4 | async-start | bytes 2621440 | tf_op jit(solution)/shard_map/all_gather | solution.py:28
  93.1 146.4 %all-gather.7.cloned.1.call-start = ((), (), s32[]{:S(2)}) async-start(), calls=%async_computation.3 | async-start | bytes 5505024 | tf_op jit(solution)/shard_map/all_gather | solution.py:47
  144.9 147.5 %all-gather.11.cloned.1.call-start = ((), (), s32[]{:S(2)}) async-start(), calls=%async_computation.5 | async-start | bytes 5505024 | tf_op jit(solution)/shard_map/all_gather | solution.py:48
  256.5 35.9 %copy-start.1 = (bf16[1,512,2048]{2,1,0:T(8,128)(2,1)S(1)}, bf16[1,512,2048]{2,1,0:T(8,128)(2,1)}, u32[]{:S(2)}) copy-start(bf16[1,512,2048]{2,1,0:T(8,128)(2,1)} %all-gather.9.cloned.1.call-done) | copy-start | bytes 6291460
  266.3 51.2 %collective-permute-start = (bf16[3584,1024]{1,0:T(8,128)(2,1)}, bf16[3584,1024]{1,0:T(8,128)(2,1)}, u32[]{:S(2)}, u32[]{:S(2)}) collective-permute-start(bf16[3584,1024]{1,0:T(8,128)(2,1)} %dynamic-slice_convert_fusion.1), channel_id=1, source_target_pairs={{0,1},{1,0},{2,3},{3,2},{4,5},{5,4},{6,7},{7,6},{8,9},{9,8},{10,11... | collective-permute-start | bytes 22020104 | tf_op jit(solution)/shard_map/ppermute | solution.py:8
  317.5 13.7 %collective-permute-start.1 = (bf16[3584,1024]{1,0:T(8,128)(2,1)}, bf16[3584,1024]{1,0:T(8,128)(2,1)}, u32[]{:S(2)}, u32[]{:S(2)}) collective-permute-start(bf16[3584,1024]{1,0:T(8,128)(2,1)} %dynamic-slice_convert_fusion), channel_id=1, source_target_pairs={{0,1},{1,0},{2,3},{3,2},{4,5},{5,4},{6,7},{7,6},{8,9},{9,8},{10,11... | collective-permute-start | bytes 22020104 | tf_op jit(solution)/shard_map/ppermute | solution.py:8
  317.5 21.0 %copy-start = (f32[3584,2048]{1,0:T(8,128)S(1)}, f32[3584,2048]{1,0:T(8,128)}, u32[]{:S(2)}) copy-start(f32[3584,2048]{1,0:T(8,128)} %fusion.18) | copy-start | bytes 88080384
Sparse Core Ops, SparseCore 0:
  9.6 48.6 all-gather.4
  92.4 47.8 reduce-scatter.1
  142.0 45.8 all-gather.8
  189.9 49.5 all-gather.6
  241.5 50.7 all-gather.10
where the time goes:
time: 356 us; the launch traced here: 355 us
  waiting for transfers between devices  191 us (54%)
  local copies, waits for them, and re-layouts  66.1 us (19%)
  matrix products  55.1 us (15%)
  other arithmetic  28.3 us (8%)
  between operations  13.8 us (4%)
    all_gather x1, waiting for transfers between devices, on_device(): lax.all_gather(d_gate, 'col', axis=0, tiled=True)  51.6 us
    all_gather x1, waiting for transfers between devices, on_device(): lax.all_gather(layer_input, 'row', axis=1, tiled=True)  42.4 us
    reduce_scatter x1, waiting for transfers between devices, on_device(): lax.psum_scatter(jnp.dot(selected, down_weight, preferred_element_type=jn...  40.3 us
    unnamed x10, local copies, waits for them, and re-layouts  35.2 us
    dot_general x2, matrix products, contract_tokens(): lax.dot_general(left, right, (((0,), (0,)), ((), ())), preferred_element_...  32.7 us
    all_gather x1, waiting for transfers between devices, on_device(): lax.all_gather(out_grad, 'row', axis=1, tiled=True)  29.2 us
    all_gather x1, waiting for transfers between devices, on_device(): lax.all_gather(d_up, 'col', axis=0, tiled=True)  26.1 us
    add x2, other arithmetic, on_device(): return (keep_gate + other_gate, keep_up + other_up)  23.7 us
  transfers between devices with their start and end apart: 7, of which 5 were waited for; matrix products, arithmetic and copies ran while one was open for 28% of the time, Pallas kernels for 0%

commit v1 on v0

v1 whole, which is shorter than its diff:
```python
import functools

import jax
import jax.numpy as jnp
from jax import lax
from jax.experimental import pallas as pl
from jax.experimental.pallas import tpu as pltpu
from jax.sharding import PartitionSpec as P

VMEM_LIMIT = 48 * 1024 * 1024
LANES = 256


def swap(value, axis):
    return lax.ppermute(value, axis, [(0, 1), (1, 0)])


def swap_neighbours(value, axis):
    return lax.ppermute(value, axis, [(i, i ^ 1) for i in range(lax.axis_size(axis))])


def contract_tokens(left, right):
    return lax.dot_general(
        left, right, (((0,), (0,)), ((), ())), preferred_element_type=jnp.float32
    )


def d_gate_and_up(hidden_grad, gates, ups):
    sigmoid_gate = 1.0 / (1.0 + jnp.exp(-gates))
    d_gate = hidden_grad * ups * sigmoid_gate * (1.0 + gates * (1.0 - sigmoid_gate))
    d_up = hidden_grad * gates * sigmoid_gate
    return d_gate.astype(jnp.bfloat16), d_up.astype(jnp.bfloat16)


def ring_gather(shard, axis, turn, stack_axis):
    n = lax.axis_size(axis)
    me = lax.axis_index(axis)
    up = [(i, i + 1) for i in range(n - 1)]
    down = [(i + 1, i) for i in range(n - 1)]
    ups, downs = [shard], [shard]
    for _ in range(n - 1):
        ups.append(lax.ppermute(ups[-1], axis, up))
        downs.append(lax.ppermute(downs[-1], axis, down))
    shape = shard.shape[:stack_axis] + (n,) + shard.shape[stack_axis:]
    out = jnp.zeros(shape, shard.dtype)
    for k in range(n):
        piece = shard if k == 0 else jnp.where(me >= k, ups[k], downs[n - k])
        slot = lax.rem(me - k - turn + 2 * n, n)
        out = lax.dynamic_update_index_in_dim(out, piece, slot, stack_axis)
    return out


def partial_kernel(block_side, first_block, grads, codes, scales, own, partner, weight):
    feature_rows = codes.shape[0]
    lanes = codes.shape[1]
    base = first_block + pl.program_id(0) * (lanes // block_side)
    for i in range(feature_rows // block_side):
        for j in range(lanes // block_side):
            rows = slice(i * block_side, (i + 1) * block_side)
            cols = slice(j * block_side, (j + 1) * block_side)
            scaled = codes[rows, cols].astype(jnp.float32) * scales[i, base + j]
            weight[rows, cols] = scaled.astype(jnp.bfloat16)
    product = jnp.dot(grads[...], weight[...], preferred_element_type=jnp.float32)
    half = own.shape[0]
    own[...] = product[:half].astype(jnp.bfloat16)
    partner[...] = product[half:].astype(jnp.bfloat16)


def partial_products(grads, codes, scales, start, width):
    tokens, features = grads.shape
    block_side = features // scales.shape[0]
    half = tokens // 2
    offset = start // LANES
    out = jax.ShapeDtypeStruct((half, width), jnp.bfloat16)
    out_spec = pl.BlockSpec((half, LANES), lambda i: (0, i))
    return pl.pallas_call(
        functools.partial(partial_kernel, block_side, start // block_side),
        grid=(width // LANES,),
        in_specs=[
            pl.BlockSpec((tokens, features), lambda i: (0, 0)),
            pl.BlockSpec((features, LANES), lambda i: (0, offset + i)),
            pl.BlockSpec(memory_space=pltpu.SMEM),
        ],
        out_specs=[out_spec, out_spec],
        out_shape=[out, out],
        scratch_shapes=[pltpu.VMEM((features, LANES), jnp.bfloat16)],
        compiler_params=pltpu.CompilerParams(vmem_limit_bytes=VMEM_LIMIT),
        cost_estimate=pl.CostEstimate(
            flops=2 * tokens * features * width,
            bytes_accessed=2 * (features * width + tokens * features + tokens * width),
            transcendentals=0,
        ),
    )(grads, codes, scales)


def activation_kernel(own, other, gates, ups, out):
    hidden_grad = own[...].astype(jnp.float32) + other[...].astype(jnp.float32)
    d_gate, d_up = d_gate_and_up(
        hidden_grad, gates[0].astype(jnp.float32), ups[0].astype(jnp.float32)
    )
    out[0] = d_gate
    out[1] = d_up


def activation_grads(own, other, gate_pre, up_pre, start):
    tokens, width = own.shape
    offset = start // LANES
    piece = pl.BlockSpec((tokens, LANES), lambda i: (0, i))
    saved = pl.BlockSpec((1, tokens, LANES), lambda i: (0, 0, offset + i))
    return pl.pallas_call(
        activation_kernel,
        grid=(width // LANES,),
        in_specs=[piece, piece, saved, saved],
        out_specs=pl.BlockSpec((2, tokens, LANES), lambda i: (0, 0, i)),
        out_shape=jax.ShapeDtypeStruct((2, tokens, width), jnp.bfloat16),
        compiler_params=pltpu.CompilerParams(vmem_limit_bytes=VMEM_LIMIT),
        cost_estimate=pl.CostEstimate(
            flops=16 * tokens * width,
            bytes_accessed=12 * tokens * width,
            transcendentals=tokens * width,
        ),
    )(own, other, gate_pre, up_pre)


def weight_kernel(a, b, c, d, inputs, *refs):
    gate_out, up_out = refs[-2:]
    for which, out in ((0, gate_out), (1, up_out)):
        left = jnp.concatenate([a[which], b[which], c[which], d[which]], axis=0)
        out[...] = contract_tokens(left, inputs[...])


def weight_grads(pieces, inputs, start, outs, hidden):
    _, quarter, width = pieces[0].shape
    tokens, features = inputs.shape
    offset = start // LANES
    piece = pl.BlockSpec((2, quarter, LANES), lambda i: (0, 0, i))
    out_spec = pl.BlockSpec((LANES, features), lambda i: (offset + i, 0))
    out = jax.ShapeDtypeStruct((hidden, features), jnp.float32)
    in_specs = [piece] * 4 + [pl.BlockSpec((tokens, features), lambda i: (0, 0))]
    operands = list(pieces) + [inputs]
    aliases = {}
    if outs is not None:
        in_specs += [pl.BlockSpec(memory_space=pl.ANY)] * 2
        operands += list(outs)
        aliases = {5: 0, 6: 1}
    return pl.pallas_call(
        weight_kernel,
        grid=(width // LANES,),
        in_specs=in_specs,
        out_specs=[out_spec, out_spec],
        out_shape=[out, out],
        input_output_aliases=aliases,
        compiler_params=pltpu.CompilerParams(vmem_limit_bytes=VMEM_LIMIT),
        cost_estimate=pl.CostEstimate(
            flops=4 * tokens * features * width,
            bytes_accessed=4 * tokens * width + 2 * tokens * features + 8 * width * features,
            transcendentals=0,
        ),
    )(*operands)


def chunk_bounds(hidden):
    pieces = 7
    width = hidden // pieces
    return [(i * width, width) for i in range(pieces)]


def on_pairs(layer_input, out_grad, down_codes, down_scales, gate_pre, up_pre):
    hidden = down_codes.shape[1]
    col = lax.axis_index("col")
    depth = lax.axis_index("depth")
    n_row = lax.axis_size("row")
    turn = col * (n_row // 2)
    shard_tokens, features = out_grad.shape[1:]
    half_features = features // 2

    grads = ring_gather(out_grad[0], "row", turn, 0).reshape(n_row * shard_tokens, features)

    keep = lax.dynamic_slice_in_dim(layer_input, depth * half_features, half_features, 2)
    send = lax.dynamic_slice_in_dim(layer_input, (1 - depth) * half_features, half_features, 2)
    both = jnp.concatenate([keep, swap(send, "depth")], axis=0)
    inputs = ring_gather(both, "row", turn, 1).reshape(2 * n_row * shard_tokens, half_features)

    outs = None
    for start, width in chunk_bounds(hidden):
        own, partner = partial_products(grads, down_codes, down_scales, start, width)
        other = swap(partner, "col")
        mine = activation_grads(own, other, gate_pre, up_pre, start)
        theirs = swap(mine, "col")
        pieces = (mine, theirs, swap(mine, "depth"), swap(theirs, "depth"))
        outs = weight_grads(pieces, inputs, start, outs, hidden)
    return tuple(outs)


def on_many(layer_input, out_grad, down_codes, down_scales, gate_pre, up_pre):
    feature_rows, hidden_cols = down_codes.shape
    blocks_feat, blocks_hidden = down_scales.shape
    block_side = feature_rows // blocks_feat
    scaled = down_codes.astype(jnp.float32).reshape(
        blocks_feat, block_side, blocks_hidden, block_side
    )
    scaled = scaled * down_scales[:, None, :, None]
    down_weight = scaled.reshape(feature_rows, hidden_cols).astype(jnp.bfloat16)
    grads = lax.all_gather(out_grad, "row", axis=1, tiled=True)[0]
    half_features = feature_rows // 2
    depth = lax.axis_index("depth")
    keep = lax.dynamic_slice_in_dim(layer_input, depth * half_features, half_features, 2)
    send = lax.dynamic_slice_in_dim(layer_input, (1 - depth) * half_features, half_features, 2)
    both = jnp.concatenate([keep, swap_neighbours(send, "depth")], axis=0)
    inputs = lax.all_gather(both, "row", axis=1, tiled=True)
    hidden_grad = lax.psum_scatter(
        jnp.dot(grads, down_weight, preferred_element_type=jnp.float32).astype(jnp.bfloat16),
        "col",
        scatter_dimension=0,
        tiled=True,
    ).astype(jnp.float32)
    d_gate, d_up = d_gate_and_up(
        hidden_grad, gate_pre[0].astype(jnp.float32), up_pre[0].astype(jnp.float32)
    )
    results = []
    for mine in (d_gate, d_up):
        gathered = lax.all_gather(mine, "col", axis=0, tiled=True)
        other = swap_neighbours(gathered, "depth")
        results.append(
            contract_tokens(
                jnp.concatenate([gathered, other], axis=0),
                inputs.reshape(-1, half_features),
            )
        )
    return tuple(results)


def solution(mesh):
    in_specs = (
        P("depth", ("groups", "row"), "col"),
        P("depth", ("groups", "row"), "col"),
        P("col", "row"),
        P("col", "row"),
        P("depth", ("groups", "col"), "row"),
        P("depth", ("groups", "col"), "row"),
    )
    out_specs = (P(("groups", "row"), ("col", "depth")), P(("groups", "row"), ("col", "depth")))
    pairs = mesh.shape["col"] == 2 and mesh.shape["row"] % 2 == 0
    return jax.shard_map(
        on_pairs if pairs else on_many,
        mesh=mesh,
        in_specs=in_specs,
        out_specs=out_specs,
        check_vma=False,
    )
```

time: 356 us -> 206 us (0.58)
  waiting for transfers between devices: 191 us -> 93.6 us
  local copies, waits for them, and re-layouts: 66.1 us -> 2.7 us
  matrix products: 55.1 us -> 0 us
  starting transfers between devices: 0.38 us -> 52.8 us
  Pallas kernels: 0 us -> 50.8 us
  other arithmetic: 28.3 us -> 4.23 us
  between operations: 13.8 us -> 1.18 us
    all_gather x4 -> x0, waiting for transfers between devices: 149 us -> none  [the longest x1 51.6 us: on_device(): lax.all_gather(d_gate, 'col', axis=0, tiled=True)]
    ppermute x2 -> x41, waiting for transfers between devices: 0.01 us -> 93.6 us  [the longest x29 62.8 us: swap(): return lax.ppermute(value, axis, [(0, 1), (1, 0)])]
    dot_general x3 -> x0, matrix products: 55.1 us -> none  [the longest x2 32.7 us: contract_tokens(): lax.dot_general(left, right, (((0,), (0,)), ((), ())), preferred_element_...]
    ppermute x2 -> x41, starting transfers between devices: 0.01 us -> 52.8 us  [the longest x6 28.3 us: ring_gather(): ups.append(lax.ppermute(ups[-1], axis, up))]
    pallas_call x0 -> x21, Pallas kernels: none -> 50.8 us  [the longest x7 26.1 us: weight_grads(): pl.pallas_call(weight_kernel, grid=(width // LANES,), in_specs=in_specs,...]
    reduce_scatter x1 -> x0, waiting for transfers between devices: 40.3 us -> none  [on_device(): lax.psum_scatter(jnp.dot(selected, down_weight, preferred_element_type=jn...]
    unnamed x10 -> x32, local copies, waits for them, and re-layouts: 35.2 us -> 1.03 us
    add x2 -> x0, other arithmetic: 23.7 us -> none  [on_device(): return (keep_gate + other_gate, keep_up + other_up)]
  transfers between devices with their start and end apart: 7 -> 41, of which waited for: 5 -> 17; matrix products, arithmetic and copies ran while one was open for 28% -> 3% of each run, Pallas kernels for 0% -> 23%
where the time goes in v1:
time: 206 us; the launch traced here: 205 us
  waiting for transfers between devices  93.6 us (45%)
  starting transfers between devices  52.8 us (26%)
  Pallas kernels  50.8 us (25%)
  other arithmetic  4.23 us (2%)
  local copies, waits for them, and re-layouts  2.7 us (1%)
    ppermute x29, waiting for transfers between devices, swap(): return lax.ppermute(value, axis, [(0, 1), (1, 0)])  62.8 us
    ppermute x6, waiting for transfers between devices, ring_gather(): downs.append(lax.ppermute(downs[-1], axis, down))  28.5 us
    ppermute x6, starting transfers between devices, ring_gather(): ups.append(lax.ppermute(ups[-1], axis, up))  28.3 us
    pallas_call x7, Pallas kernels, weight_grads(): pl.pallas_call(weight_kernel, grid=(width // LANES,), in_specs=in_specs,...  26.1 us
    pallas_call x7, Pallas kernels, partial_products(): pl.pallas_call(functools.partial(partial_kernel, block_side, start // blo...  21.1 us
    ppermute x29, starting transfers between devices, swap(): return lax.ppermute(value, axis, [(0, 1), (1, 0)])  16.8 us
    ppermute x6, starting transfers between devices, ring_gather(): downs.append(lax.ppermute(downs[-1], axis, down))  7.71 us
    dynamic_update_slice x7, other arithmetic, ring_gather(): out = lax.dynamic_update_index_in_dim(out, piece, slot, stack_axis)  4.18 us
  transfers between devices with their start and end apart: 41, of which 17 were waited for; matrix products, arithmetic and copies ran while one was open for 3% of the time, Pallas kernels for 23%

profile of v1, /device:TPU:0, one launch (start us, length us, event | category | flops | bytes accessed | tf_op | source)
XLA Modules:
  0.0 205.3 jit_solution(4524517453614199894)
XLA Ops:
  0.6 1.3 collective-permute-start.1
  3.6 5.9 %collective-permute-start = (bf16[128,2048]{1,0:T(8,128)(2,1)}, bf16[128,2048]{1,0:T(8,128)(2,1)}, u32[]{:S(2)}, u32[]{:S(2)}) collective-permute-start(bf16[128,2048]{1,0:T(8,128)(2,1)} %bitcast.40), channel_id=1, source_target_pairs={{0,4},{4,8},{8,12},{1,5},{5,9},{9,13},{2,6},{6,10},{10,14},{3,7},{... | collective-permute-start | bytes 1572872 | tf_op jit(solution)/shard_map/ppermute | solution.py:42
  10.3 1.3 collective-permute-start.12
  11.6 6.9 %collective-permute-done.1 = bf16[128,2048]{1,0:T(8,128)(2,1)S(1)} collective-permute-done((bf16[128,2048]{1,0:T(8,128)(2,1)}, bf16[128,2048]{1,0:T(8,128)(2,1)S(1)}, u32[]{:S(2)}, u32[]{:S(2)}) %collective-permute-start.1) | collective-permute-done | bytes 524320 | tf_op jit(solution)/shard_map/ppermute | solution.py:43
  18.5 1.3 collective-permute-start.2
  19.8 4.6 %collective-permute-start.11 = (bf16[2,128,1024]{2,1,0:T(8,128)(2,1)S(1)}, bf16[2,128,1024]{2,1,0:T(8,128)(2,1)S(1)}, u32[]{:S(2)}, u32[]{:S(2)}) collective-permute-start(bf16[2,128,1024]{2,1,0:T(8,128)(2,1)S(1)} %pad_maximum_fusion), channel_id=1, source_target_pairs={{0,4},{4,8},{8,12},{1,5},{5,9},{9,13},{2,6},{6,10},{10,14},{3,7},{... | collective-permute-start | bytes 1572872 | tf_op jit(solution)/shard_map/ppermute | solution.py:42
  24.4 4.7 %collective-permute-start.4 = (bf16[128,2048]{1,0:T(8,128)(2,1)}, bf16[128,2048]{1,0:T(8,128)(2,1)}, u32[]{:S(2)}, u32[]{:S(2)}) collective-permute-start(bf16[128,2048]{1,0:T(8,128)(2,1)} %collective-permute-done), channel_id=1, source_target_pairs={{0,4},{4,8},{8,12},{1,5},{5,9},{9,13},{2,6},{6,10},{10,14},{3,7},{... | collective-permute-start | bytes 1572872 | tf_op jit(solution)/shard_map/ppermute | solution.py:42
  29.8 1.3 collective-permute-start.13
  31.0 10.0 %collective-permute-done.2 = bf16[128,2048]{1,0:T(8,128)(2,1)} collective-permute-done((bf16[128,2048]{1,0:T(8,128)(2,1)S(1)}, bf16[128,2048]{1,0:T(8,128)(2,1)}, u32[]{:S(2)}, u32[]{:S(2)}) %collective-permute-start.2) | collective-permute-done | bytes 524320 | tf_op jit(solution)/shard_map/ppermute | solution.py:43
  41.1 1.3 collective-permute-start.3
  42.8 4.6 %collective-permute-start.15 = (bf16[2,128,1024]{2,1,0:T(8,128)(2,1)S(1)}, bf16[2,128,1024]{2,1,0:T(8,128)(2,1)S(1)}, u32[]{:S(2)}, u32[]{:S(2)}) collective-permute-start(bf16[2,128,1024]{2,1,0:T(8,128)(2,1)S(1)} %collective-permute-done.11), channel_id=1, source_target_pairs={{0,4},{4,8},{8,12},{1,5},{5,9},{9,13},{2,6},{6,10},{10,14},{3,7},{... | collective-permute-start | bytes 1572872 | tf_op jit(solution)/shard_map/ppermute | solution.py:42
  47.4 3.9 %collective-permute-start.5 = (bf16[128,2048]{1,0:T(8,128)(2,1)}, bf16[128,2048]{1,0:T(8,128)(2,1)S(1)}, u32[]{:S(2)}, u32[]{:S(2)}) collective-permute-start(bf16[128,2048]{1,0:T(8,128)(2,1)} %collective-permute-done.4), channel_id=1, source_target_pairs={{0,4},{4,8},{8,12},{1,5},{5,9},{9,13},{2,6},{6,10},{10,14},{3,7},{... | collective-permute-start | bytes 1572872 | tf_op jit(solution)/shard_map/ppermute | solution.py:42
  52.3 1.3 collective-permute-start.14
  53.6 9.9 %collective-permute-done.3 = bf16[128,2048]{1,0:T(8,128)(2,1)} collective-permute-done((bf16[128,2048]{1,0:T(8,128)(2,1)}, bf16[128,2048]{1,0:T(8,128)(2,1)}, u32[]{:S(2)}, u32[]{:S(2)}) %collective-permute-start.3) | collective-permute-done | bytes 524320 | tf_op jit(solution)/shard_map/ppermute | solution.py:43
  63.6 1.2 bitcast_dynamic-update-slice_fusion.6
  64.8 1.2 bitcast_dynamic-update-slice_fusion.5
  66.0 2.2 %collective-permute-done.5 = bf16[128,2048]{1,0:T(8,128)(2,1)S(1)} collective-permute-done((bf16[128,2048]{1,0:T(8,128)(2,1)}, bf16[128,2048]{1,0:T(8,128)(2,1)S(1)}, u32[]{:S(2)}, u32[]{:S(2)}) %collective-permute-start.5) | collective-permute-done | bytes 524320 | tf_op jit(solution)/shard_map/ppermute | solution.py:42
  68.3 3.0 %shard_map.89 = (bf16[256,512]{1,0:T(8,128)(2,1)S(1)}, bf16[256,512]{1,0:T(8,128)(2,1)S(1)}) custom-call(bf16[512,2048]{1,0:T(8,128)(2,1)S(1)} %bitcast.25, bf16[2048,3584]{1,0:T(8,128)(2,1)} %codes.13, f32[16,28]{1,0:T(8,128)S(1)} %copy-done.2), custom_call_target="tpu_custom_call" | custom-call | flops 1073741824 | bytes 4718592 | tf_op jit(solution)/shard_map/pallas_call | solution.py:76
  71.3 1.4 collective-permute-start.37
  72.7 3.0 %shard_map.87 = (bf16[256,512]{1,0:T(8,128)(2,1)S(1)}, bf16[256,512]{1,0:T(8,128)(2,1)S(1)}) custom-call(bf16[512,2048]{1,0:T(8,128)(2,1)S(1)} %bitcast.26, bf16[2048,3584]{1,0:T(8,128)(2,1)} %codes.13, f32[16,28]{1,0:T(8,128)S(1)} %copy-done.2), custom_call_target="tpu_custom_call" | custom-call | flops 1073741824 | bytes 4718592 | tf_op jit(solution)/shard_map/pallas_call | solution.py:76
  76.4 3.0 %shard_map.85 = (bf16[256,512]{1,0:T(8,128)(2,1)S(1)}, bf16[256,512]{1,0:T(8,128)(2,1)S(1)}) custom-call(bf16[512,2048]{1,0:T(8,128)(2,1)S(1)} %bitcast.27, bf16[2048,3584]{1,0:T(8,128)(2,1)} %codes.13, f32[16,28]{1,0:T(8,128)S(1)} %copy-done.2), custom_call_target="tpu_custom_call" | custom-call | flops 1073741824 | bytes 4718592 | tf_op jit(solution)/shard_map/pallas_call | solution.py:76
  79.4 1.4 collective-permute-start.29
  80.8 3.0 %shard_map.83 = (bf16[256,512]{1,0:T(8,128)(2,1)S(1)}, bf16[256,512]{1,0:T(8,128)(2,1)S(1)}) custom-call(bf16[512,2048]{1,0:T(8,128)(2,1)S(1)} %bitcast.28, bf16[2048,3584]{1,0:T(8,128)(2,1)} %codes.13, f32[16,28]{1,0:T(8,128)S(1)} %copy-done.2), custom_call_target="tpu_custom_call" | custom-call | flops 1073741824 | bytes 4718592 | tf_op jit(solution)/shard_map/pallas_call | solution.py:76
  83.8 3.0 %shard_map.81 = (bf16[256,512]{1,0:T(8,128)(2,1)S(1)}, bf16[256,512]{1,0:T(8,128)(2,1)S(1)}) custom-call(bf16[512,2048]{1,0:T(8,128)(2,1)S(1)} %bitcast.29, bf16[2048,3584]{1,0:T(8,128)(2,1)} %codes.13, f32[16,28]{1,0:T(8,128)S(1)} %copy-done.2), custom_call_target="tpu_custom_call" | custom-call | flops 1073741824 | bytes 4718592 | tf_op jit(solution)/shard_map/pallas_call | solution.py:76
  86.8 3.0 %shard_map.79 = (bf16[256,512]{1,0:T(8,128)(2,1)S(1)}, bf16[256,512]{1,0:T(8,128)(2,1)S(1)}) custom-call(bf16[512,2048]{1,0:T(8,128)(2,1)S(1)} %bitcast.30, bf16[2048,3584]{1,0:T(8,128)(2,1)} %codes.13, f32[16,28]{1,0:T(8,128)S(1)} %copy-done.2), custom_call_target="tpu_custom_call" | custom-call | flops 1073741824 | bytes 4718592 | tf_op jit(solution)/shard_map/pallas_call | solution.py:76
  90.6 1.4 collective-permute-start.21
  92.6 3.3 %shard_map.77 = (bf16[256,512]{1,0:T(8,128)(2,1)S(1)}, bf16[256,512]{1,0:T(8,128)(2,1)S(1)}) custom-call(bf16[512,2048]{1,0:T(8,128)(2,1)S(1)} %bitcast.31, bf16[2048,3584]{1,0:T(8,128)(2,1)} %codes.13, f32[16,28]{1,0:T(8,128)S(1)} %copy-done.2), custom_call_target="tpu_custom_call" | custom-call | flops 1073741824 | bytes 4718592 | tf_op jit(solution)/shard_map/pallas_call | solution.py:76
  97.5 1.6 collective-permute-done.25.other
  99.1 4.5 %collective-permute-start.16 = (bf16[2,128,1024]{2,1,0:T(8,128)(2,1)S(1)}, bf16[2,128,1024]{2,1,0:T(8,128)(2,1)S(1)}, u32[]{:S(2)}, u32[]{:S(2)}) collective-permute-start(bf16[2,128,1024]{2,1,0:T(8,128)(2,1)S(1)} %collective-permute-done.15), channel_id=1, source_target_pairs={{0,4},{4,8},{8,12},{1,5},{5,9},{9,13},{2,6},{6,10},{10,14},{3,7},{... | collective-permute-start | bytes 1572872 | tf_op jit(solution)/shard_map/ppermute | solution.py:42
  103.6 1.1 collective-permute-done.21.other
  105.4 4.9 %collective-permute-done.17.other = bf16[256,512]{1,0:T(8,128)(2,1)S(1)} collective-permute-done((bf16[256,512]{1,0:T(8,128)(2,1)S(1)}, bf16[256,512]{1,0:T(8,128)(2,1)S(1)}, u32[]{:S(2)}, u32[]{:S(2)}) %collective-permute-start.17) | collective-permute-done | bytes 262176 | tf_op jit(solution)/shard_map/ppermute | solution.py:15
  110.9 5.1 %collective-permute-done.6.other = bf16[256,512]{1,0:T(8,128)(2,1)S(1)} collective-permute-done((bf16[256,512]{1,0:T(8,128)(2,1)S(1)}, bf16[256,512]{1,0:T(8,128)(2,1)S(1)}, u32[]{:S(2)}, u32[]{:S(2)}) %collective-permute-start.6) | collective-permute-done | bytes 262176 | tf_op jit(solution)/shard_map/ppermute | solution.py:15
  118.0 1.4 collective-permute-start.30
  119.4 7.8 %collective-permute-done.38.b = bf16[2,256,512]{2,1,0:T(8,128)(2,1)S(1)} collective-permute-done((bf16[2,256,512]{2,1,0:T(8,128)(2,1)S(1)}, bf16[2,256,512]{2,1,0:T(8,128)(2,1)S(1)}, u32[]{:S(2)}, u32[]{:S(2)}) %collective-permute-start.38) | collective-permute-done | bytes 524320 | tf_op jit(solution)/shard_map/ppermute | solution.py:15
  129.9 8.6 %collective-permute-done.34.b = bf16[2,256,512]{2,1,0:T(8,128)(2,1)S(1)} collective-permute-done((bf16[2,256,512]{2,1,0:T(8,128)(2,1)S(1)}, bf16[2,256,512]{2,1,0:T(8,128)(2,1)S(1)}, u32[]{:S(2)}, u32[]{:S(2)}) %collective-permute-start.34) | collective-permute-done | bytes 524320 | tf_op jit(solution)/shard_map/ppermute | solution.py:15
  139.3 10.4 %collective-permute-done.30.b = bf16[2,256,512]{2,1,0:T(8,128)(2,1)S(1)} collective-permute-done((bf16[2,256,512]{2,1,0:T(8,128)(2,1)S(1)}, bf16[2,256,512]{2,1,0:T(8,128)(2,1)S(1)}, u32[]{:S(2)}, u32[]{:S(2)}) %collective-permute-start.30) | collective-permute-done | bytes 524320 | tf_op jit(solution)/shard_map/ppermute | solution.py:15
  150.2 10.7 %collective-permute-done.26.b = bf16[2,256,512]{2,1,0:T(8,128)(2,1)S(1)} collective-permute-done((bf16[2,256,512]{2,1,0:T(8,128)(2,1)S(1)}, bf16[2,256,512]{2,1,0:T(8,128)(2,1)S(1)}, u32[]{:S(2)}, u32[]{:S(2)}) %collective-permute-start.26) | collective-permute-done | bytes 524320 | tf_op jit(solution)/shard_map/ppermute | solution.py:15
  160.9 1.2 bitcast_dynamic-update-slice_fusion.1
  162.9 6.4 %collective-permute-done.22.b = bf16[2,256,512]{2,1,0:T(8,128)(2,1)S(1)} collective-permute-done((bf16[2,256,512]{2,1,0:T(8,128)(2,1)S(1)}, bf16[2,256,512]{2,1,0:T(8,128)(2,1)S(1)}, u32[]{:S(2)}, u32[]{:S(2)}) %collective-permute-start.22) | collective-permute-done | bytes 524320 | tf_op jit(solution)/shard_map/ppermute | solution.py:15
  169.6 2.0 collective-permute-start.7
  171.8 3.7 %shard_map.91 = (f32[3584,1024]{1,0:T(8,128)}, f32[3584,1024]{1,0:T(8,128)}) custom-call(bf16[2,256,512]{2,1,0:T(8,128)(2,1)S(1)} %shard_map.90.a, bf16[2,256,512]{2,1,0:T(8,128)(2,1)S(1)} %collective-permute-done.38.b, bf16[2,256,512]{2,1,0:T(8,128)(2,1)S(1)} %collective-permute-done.39.c, bf16[2,256,512]{2,1,0:T(8,128)(2,1)S(1)} %collective-permute-done.40.d, ...), custom_call_target="tpu_custom_call" | custom-call | flops 2147483648 | bytes 8388608 | tf_op jit(solution)/shard_map/pallas_call | solution.py:146
  175.8 3.7 %shard_map.92 = (f32[3584,1024]{1,0:T(8,128)}, f32[3584,1024]{1,0:T(8,128)}) custom-call(bf16[2,256,512]{2,1,0:T(8,128)(2,1)S(1)} %shard_map.88.a, bf16[2,256,512]{2,1,0:T(8,128)(2,1)S(1)} %collective-permute-done.34.b, bf16[2,256,512]{2,1,0:T(8,128)(2,1)S(1)} %collective-permute-done.35.c, ...), custom_call_target="tpu_custom_call", output_to_operand_aliasing={{0}: (5, {}), {1}: (6, {})} | custom-call | flops 2147483648 | bytes 8388608 | tf_op jit(solution)/shard_map/pallas_call | solution.py:146
  181.1 3.7 %shard_map.93 = (f32[3584,1024]{1,0:T(8,128)}, f32[3584,1024]{1,0:T(8,128)}) custom-call(bf16[2,256,512]{2,1,0:T(8,128)(2,1)S(1)} %shard_map.86.a, bf16[2,256,512]{2,1,0:T(8,128)(2,1)S(1)} %collective-permute-done.30.b, bf16[2,256,512]{2,1,0:T(8,128)(2,1)S(1)} %collective-permute-done.31.c, ...), custom_call_target="tpu_custom_call", output_to_operand_aliasing={{0}: (5, {}), {1}: (6, {})} | custom-call | flops 2147483648 | bytes 8388608 | tf_op jit(solution)/shard_map/pallas_call | solution.py:146
  184.8 5.0 %collective-permute-done.7.b = bf16[2,256,512]{2,1,0:T(8,128)(2,1)S(1)} collective-permute-done((bf16[2,256,512]{2,1,0:T(8,128)(2,1)S(1)}, bf16[2,256,512]{2,1,0:T(8,128)(2,1)S(1)}, u32[]{:S(2)}, u32[]{:S(2)}) %collective-permute-start.7) | collective-permute-done | bytes 524320 | tf_op jit(solution)/shard_map/ppermute | solution.py:15
  190.4 3.7 %shard_map.94 = (f32[3584,1024]{1,0:T(8,128)}, f32[3584,1024]{1,0:T(8,128)}) custom-call(bf16[2,256,512]{2,1,0:T(8,128)(2,1)S(1)} %shard_map.84.a, bf16[2,256,512]{2,1,0:T(8,128)(2,1)S(1)} %collective-permute-done.26.b, bf16[2,256,512]{2,1,0:T(8,128)(2,1)S(1)} %collective-permute-done.27.c, ...), custom_call_target="tpu_custom_call", output_to_operand_aliasing={{0}: (5, {}), {1}: (6, {})} | custom-call | flops 2147483648 | bytes 8388608 | tf_op jit(solution)/shard_map/pallas_call | solution.py:146
  194.1 3.7 %shard_map.95 = (f32[3584,1024]{1,0:T(8,128)}, f32[3584,1024]{1,0:T(8,128)}) custom-call(bf16[2,256,512]{2,1,0:T(8,128)(2,1)S(1)} %shard_map.82.a, bf16[2,256,512]{2,1,0:T(8,128)(2,1)S(1)} %collective-permute-done.22.b, bf16[2,256,512]{2,1,0:T(8,128)(2,1)S(1)} %collective-permute-done.23.c, ...), custom_call_target="tpu_custom_call", output_to_operand_aliasing={{0}: (5, {}), {1}: (6, {})} | custom-call | flops 2147483648 | bytes 8388608 | tf_op jit(solution)/shard_map/pallas_call | solution.py:146
  197.8 3.7 %shard_map.96 = (f32[3584,1024]{1,0:T(8,128)}, f32[3584,1024]{1,0:T(8,128)}) custom-call(bf16[2,256,512]{2,1,0:T(8,128)(2,1)S(1)} %shard_map.80.a, bf16[2,256,512]{2,1,0:T(8,128)(2,1)S(1)} %collective-permute-done.18.b, bf16[2,256,512]{2,1,0:T(8,128)(2,1)S(1)} %collective-permute-done.19.c, ...), custom_call_target="tpu_custom_call", output_to_operand_aliasing={{0}: (5, {}), {1}: (6, {})} | custom-call | flops 2147483648 | bytes 8388608 | tf_op jit(solution)/shard_map/pallas_call | solution.py:146
  201.6 3.7 %shard_map.97 = (f32[3584,1024]{1,0:T(8,128)}, f32[3584,1024]{1,0:T(8,128)}) custom-call(bf16[2,256,512]{2,1,0:T(8,128)(2,1)S(1)} %shard_map.78.a, bf16[2,256,512]{2,1,0:T(8,128)(2,1)S(1)} %collective-permute-done.7.b, bf16[2,256,512]{2,1,0:T(8,128)(2,1)S(1)} %collective-permute-done.8.c, ...), custom_call_target="tpu_custom_call", output_to_operand_aliasing={{0}: (5, {}), {1}: (6, {})} | custom-call | flops 2147483648 | bytes 8388608 | tf_op jit(solution)/shard_map/pallas_call | solution.py:146
  (99 shorter events, 18.9 us)
Async XLA Ops:
  0.6 17.9 %collective-permute-start.1 = (bf16[128,2048]{1,0:T(8,128)(2,1)}, bf16[128,2048]{1,0:T(8,128)(2,1)S(1)}, u32[]{:S(2)}, u32[]{:S(2)}) collective-permute-start(bf16[128,2048]{1,0:T(8,128)(2,1)} %bitcast.39), channel_id=1, source_target_pairs={{4,0},{8,4},{12,8},{5,1},{9,5},{13,9},{6,2},{10,6},{14,10},{7,3},{... | collective-permute-start | bytes 1572872 | tf_op jit(solution)/shard_map/ppermute | solution.py:43
  1.9 40.7 %copy-start.5 = (bf16[1,128,2048]{2,1,0:T(8,128)(2,1)S(1)}, bf16[1,128,2048]{2,1,0:T(8,128)(2,1)}, u32[]{:S(2)}) copy-start(bf16[1,128,2048]{2,1,0:T(8,128)(2,1)} %param.7) | copy-start | bytes 1572868
  3.1 6.5 %collective-permute-start.10 = (bf16[1,128,1024]{2,1,0:T(8,128)(2,1)S(1)}, bf16[1,128,1024]{2,1,0:T(8,128)(2,1)S(1)}, u32[]{:S(2)}, u32[]{:S(2)}) collective-permute-start(bf16[1,128,1024]{2,1,0:T(8,128)(2,1)S(1)} %get-tuple-element.55), channel_id=1, source_target_pairs={{0,1},{1,0},{2,3},{3,2},{4,5},{5,4},{6,7},{7,6},{8,9},{9,8},{10,11... | collective-permute-start | bytes 786440 | tf_op jit(solution)/shard_map/ppermute | solution.py:15
  3.6 20.8 %collective-permute-start = (bf16[128,2048]{1,0:T(8,128)(2,1)}, bf16[128,2048]{1,0:T(8,128)(2,1)}, u32[]{:S(2)}, u32[]{:S(2)}) collective-permute-start(bf16[128,2048]{1,0:T(8,128)(2,1)} %bitcast.40), channel_id=1, source_target_pairs={{0,4},{4,8},{8,12},{1,5},{5,9},{9,13},{2,6},{6,10},{10,14},{3,7},{... | collective-permute-start | bytes 1572872 | tf_op jit(solution)/shard_map/ppermute | solution.py:42
  10.3 19.5 %collective-permute-start.12 = (bf16[2,128,1024]{2,1,0:T(8,128)(2,1)S(1)}, bf16[2,128,1024]{2,1,0:T(8,128)(2,1)S(1)}, u32[]{:S(2)}, u32[]{:S(2)}) collective-permute-start(bf16[2,128,1024]{2,1,0:T(8,128)(2,1)S(1)} %pad_maximum_fusion), channel_id=1, source_target_pairs={{4,0},{8,4},{12,8},{5,1},{9,5},{13,9},{6,2},{10,6},{14,10},{7,3},{... | collective-permute-start | bytes 1572872 | tf_op jit(solution)/shard_map/ppermute | solution.py:43
  18.5 22.6 %collective-permute-start.2 = (bf16[128,2048]{1,0:T(8,128)(2,1)S(1)}, bf16[128,2048]{1,0:T(8,128)(2,1)}, u32[]{:S(2)}, u32[]{:S(2)}) collective-permute-start(bf16[128,2048]{1,0:T(8,128)(2,1)S(1)} %collective-permute-done.1), channel_id=1, source_target_pairs={{4,0},{8,4},{12,8},{5,1},{9,5},{13,9},{6,2},{10,6},{14,10},{7,3},{... | collective-permute-start | bytes 1572872 | tf_op jit(solution)/shard_map/ppermute | solution.py:43
  19.8 22.9 %collective-permute-start.11 = (bf16[2,128,1024]{2,1,0:T(8,128)(2,1)S(1)}, bf16[2,128,1024]{2,1,0:T(8,128)(2,1)S(1)}, u32[]{:S(2)}, u32[]{:S(2)}) collective-permute-start(bf16[2,128,1024]{2,1,0:T(8,128)(2,1)S(1)} %pad_maximum_fusion), channel_id=1, source_target_pairs={{0,4},{4,8},{8,12},{1,5},{5,9},{9,13},{2,6},{6,10},{10,14},{3,7},{... | collective-permute-start | bytes 1572872 | tf_op jit(solution)/shard_map/ppermute | solution.py:42
  24.4 23.0 %collective-permute-start.4 = (bf16[128,2048]{1,0:T(8,128)(2,1)}, bf16[128,2048]{1,0:T(8,128)(2,1)}, u32[]{:S(2)}, u32[]{:S(2)}) collective-permute-start(bf16[128,2048]{1,0:T(8,128)(2,1)} %collective-permute-done), channel_id=1, source_target_pairs={{0,4},{4,8},{8,12},{1,5},{5,9},{9,13},{2,6},{6,10},{10,14},{3,7},{... | collective-permute-start | bytes 1572872 | tf_op jit(solution)/shard_map/ppermute | solution.py:42
  29.8 35.0 %copy-start.6 = (bf16[2,128,1024]{2,1,0:T(8,128)(2,1)}, bf16[2,128,1024]{2,1,0:T(8,128)(2,1)S(1)}, u32[]{:S(2)}) copy-start(bf16[2,128,1024]{2,1,0:T(8,128)(2,1)S(1)} %collective-permute-done.12) | copy-start | bytes 1572868
  29.8 22.6 %collective-permute-start.13 = (bf16[2,128,1024]{2,1,0:T(8,128)(2,1)S(1)}, bf16[2,128,1024]{2,1,0:T(8,128)(2,1)}, u32[]{:S(2)}, u32[]{:S(2)}) collective-permute-start(bf16[2,128,1024]{2,1,0:T(8,128)(2,1)S(1)} %collective-permute-done.12), channel_id=1, source_target_pairs={{4,0},{8,4},{12,8},{5,1},{9,5},{13,9},{6,2},{10,6},{14,10},{7,3},{... | collective-permute-start | bytes 1572872 | tf_op jit(solution)/shard_map/ppermute | solution.py:43
  41.1 22.5 %collective-permute-start.3 = (bf16[128,2048]{1,0:T(8,128)(2,1)}, bf16[128,2048]{1,0:T(8,128)(2,1)}, u32[]{:S(2)}, u32[]{:S(2)}) collective-permute-start(bf16[128,2048]{1,0:T(8,128)(2,1)} %collective-permute-done.2), channel_id=1, source_target_pairs={{4,0},{8,4},{12,8},{5,1},{9,5},{13,9},{6,2},{10,6},{14,10},{7,3},{... | collective-permute-start | bytes 1572872 | tf_op jit(solution)/shard_map/ppermute | solution.py:43
  42.7 25.6 %copy-start.2 = (f32[16,28]{1,0:T(8,128)S(1)}, f32[16,28]{1,0:T(8,128)}, u32[]{:S(2)}) copy-start(f32[16,28]{1,0:T(8,128)} %scales.13) | copy-start | bytes 5380
  42.8 25.6 %copy-start.8 = (bf16[2,128,1024]{2,1,0:T(8,128)(2,1)}, bf16[2,128,1024]{2,1,0:T(8,128)(2,1)S(1)}, u32[]{:S(2)}) copy-start(bf16[2,128,1024]{2,1,0:T(8,128)(2,1)S(1)} %collective-permute-done.11) | copy-start | bytes 1572868
  42.8 47.0 %collective-permute-start.15 = (bf16[2,128,1024]{2,1,0:T(8,128)(2,1)S(1)}, bf16[2,128,1024]{2,1,0:T(8,128)(2,1)S(1)}, u32[]{:S(2)}, u32[]{:S(2)}) collective-permute-start(bf16[2,128,1024]{2,1,0:T(8,128)(2,1)S(1)} %collective-permute-done.11), channel_id=1, source_target_pairs={{0,4},{4,8},{8,12},{1,5},{5,9},{9,13},{2,6},{6,10},{10,14},{3,7},{... | collective-permute-start | bytes 1572872 | tf_op jit(solution)/shard_map/ppermute | solution.py:42
  47.4 20.8 %collective-permute-start.5 = (bf16[128,2048]{1,0:T(8,128)(2,1)}, bf16[128,2048]{1,0:T(8,128)(2,1)S(1)}, u32[]{:S(2)}, u32[]{:S(2)}) collective-permute-start(bf16[128,2048]{1,0:T(8,128)(2,1)} %collective-permute-done.4), channel_id=1, source_target_pairs={{0,4},{4,8},{8,12},{1,5},{5,9},{9,13},{2,6},{6,10},{10,14},{3,7},{... | collective-permute-start | bytes 1572872 | tf_op jit(solution)/shard_map/ppermute | solution.py:42
  52.3 64.3 %collective-permute-start.14 = (bf16[2,128,1024]{2,1,0:T(8,128)(2,1)}, bf16[2,128,1024]{2,1,0:T(8,128)(2,1)S(1)}, u32[]{:S(2)}, u32[]{:S(2)}) collective-permute-start(bf16[2,128,1024]{2,1,0:T(8,128)(2,1)} %collective-permute-done.13), channel_id=1, source_target_pairs={{4,0},{8,4},{12,8},{5,1},{9,5},{13,9},{6,2},{10,6},{14,10},{7,3},{... | collective-permute-start | bytes 1572872 | tf_op jit(solution)/shard_map/ppermute | solution.py:43
  71.3 19.2 %collective-permute-start.37 = (bf16[256,512]{1,0:T(8,128)(2,1)S(1)}, bf16[256,512]{1,0:T(8,128)(2,1)S(1)}, u32[]{:S(2)}, u32[]{:S(2)}) collective-permute-start(bf16[256,512]{1,0:T(8,128)(2,1)S(1)} %get-tuple-element.41), channel_id=1, source_target_pairs={{0,2},{2,0},{1,3},{3,1},{4,6},{6,4},{5,7},{7,5},{8,10},{10,8},{9,1... | collective-permute-start | bytes 786440 | tf_op jit(solution)/shard_map/ppermute | solution.py:15
  75.7 16.2 %collective-permute-start.33 = (bf16[256,512]{1,0:T(8,128)(2,1)S(1)}, bf16[256,512]{1,0:T(8,128)(2,1)S(1)}, u32[]{:S(2)}, u32[]{:S(2)}) collective-permute-start(bf16[256,512]{1,0:T(8,128)(2,1)S(1)} %get-tuple-element.39), channel_id=1, source_target_pairs={{0,2},{2,0},{1,3},{3,1},{4,6},{6,4},{5,7},{7,5},{8,10},{10,8},{9,1... | collective-permute-start | bytes 786440 | tf_op jit(solution)/shard_map/ppermute | solution.py:15
  79.4 16.5 %collective-permute-start.29 = (bf16[256,512]{1,0:T(8,128)(2,1)S(1)}, bf16[256,512]{1,0:T(8,128)(2,1)S(1)}, u32[]{:S(2)}, u32[]{:S(2)}) collective-permute-start(bf16[256,512]{1,0:T(8,128)(2,1)S(1)} %get-tuple-element.37), channel_id=1, source_target_pairs={{0,2},{2,0},{1,3},{3,1},{4,6},{6,4},{5,7},{7,5},{8,10},{10,8},{9,1... | collective-permute-start | bytes 786440 | tf_op jit(solution)/shard_map/ppermute | solution.py:15
  89.8 9.3 %collective-permute-start.25 = (bf16[256,512]{1,0:T(8,128)(2,1)S(1)}, bf16[256,512]{1,0:T(8,128)(2,1)S(1)}, u32[]{:S(2)}, u32[]{:S(2)}) collective-permute-start(bf16[256,512]{1,0:T(8,128)(2,1)S(1)} %get-tuple-element.35), channel_id=1, source_target_pairs={{0,2},{2,0},{1,3},{3,1},{4,6},{6,4},{5,7},{7,5},{8,10},{10,8},{9,1... | collective-permute-start | bytes 786440 | tf_op jit(solution)/shard_map/ppermute | solution.py:15
  90.6 14.2 %collective-permute-start.21 = (bf16[256,512]{1,0:T(8,128)(2,1)S(1)}, bf16[256,512]{1,0:T(8,128)(2,1)S(1)}, u32[]{:S(2)}, u32[]{:S(2)}) collective-permute-start(bf16[256,512]{1,0:T(8,128)(2,1)S(1)} %get-tuple-element.33), channel_id=1, source_target_pairs={{0,2},{2,0},{1,3},{3,1},{4,6},{6,4},{5,7},{7,5},{8,10},{10,8},{9,1... | collective-permute-start | bytes 786440 | tf_op jit(solution)/shard_map/ppermute | solution.py:15
  91.9 18.4 %collective-permute-start.17 = (bf16[256,512]{1,0:T(8,128)(2,1)S(1)}, bf16[256,512]{1,0:T(8,128)(2,1)S(1)}, u32[]{:S(2)}, u32[]{:S(2)}) collective-permute-start(bf16[256,512]{1,0:T(8,128)(2,1)S(1)} %get-tuple-element.31), channel_id=1, source_target_pairs={{0,2},{2,0},{1,3},{3,1},{4,6},{6,4},{5,7},{7,5},{8,10},{10,8},{9,1... | collective-permute-start | bytes 786440 | tf_op jit(solution)/shard_map/ppermute | solution.py:15
  95.9 20.1 %collective-permute-start.6 = (bf16[256,512]{1,0:T(8,128)(2,1)S(1)}, bf16[256,512]{1,0:T(8,128)(2,1)S(1)}, u32[]{:S(2)}, u32[]{:S(2)}) collective-permute-start(bf16[256,512]{1,0:T(8,128)(2,1)S(1)} %get-tuple-element.29), channel_id=1, source_target_pairs={{0,2},{2,0},{1,3},{3,1},{4,6},{6,4},{5,7},{7,5},{8,10},{10,8},{9,1... | collective-permute-start | bytes 786440 | tf_op jit(solution)/shard_map/ppermute | solution.py:15
  99.1 18.8 %collective-permute-start.16 = (bf16[2,128,1024]{2,1,0:T(8,128)(2,1)S(1)}, bf16[2,128,1024]{2,1,0:T(8,128)(2,1)S(1)}, u32[]{:S(2)}, u32[]{:S(2)}) collective-permute-start(bf16[2,128,1024]{2,1,0:T(8,128)(2,1)S(1)} %collective-permute-done.15), channel_id=1, source_target_pairs={{0,4},{4,8},{8,12},{1,5},{5,9},{9,13},{2,6},{6,10},{10,14},{3,7},{... | collective-permute-start | bytes 1572872 | tf_op jit(solution)/shard_map/ppermute | solution.py:42
  104.7 22.5 %collective-permute-start.38 = (bf16[2,256,512]{2,1,0:T(8,128)(2,1)S(1)}, bf16[2,256,512]{2,1,0:T(8,128)(2,1)S(1)}, u32[]{:S(2)}, u32[]{:S(2)}) collective-permute-start(bf16[2,256,512]{2,1,0:T(8,128)(2,1)S(1)} %shard_map.90.a), channel_id=1, source_target_pairs={{0,2},{2,0},{1,3},{3,1},{4,6},{6,4},{5,7},{7,5},{8,10},{10,8},{9,1... | collective-permute-start | bytes 1572872 | tf_op jit(solution)/shard_map/ppermute | solution.py:15
  110.4 16.9 %collective-permute-start.39 = (bf16[2,256,512]{2,1,0:T(8,128)(2,1)S(1)}, bf16[2,256,512]{2,1,0:T(8,128)(2,1)S(1)}, u32[]{:S(2)}, u32[]{:S(2)}) collective-permute-start(bf16[2,256,512]{2,1,0:T(8,128)(2,1)S(1)} %shard_map.90.a), channel_id=1, source_target_pairs={{0,1},{1,0},{2,3},{3,2},{4,5},{5,4},{6,7},{7,6},{8,9},{9,8},{10,11... | collective-permute-start | bytes 1572872 | tf_op jit(solution)/shard_map/ppermute | solution.py:15
  116.0 22.5 %collective-permute-start.34 = (bf16[2,256,512]{2,1,0:T(8,128)(2,1)S(1)}, bf16[2,256,512]{2,1,0:T(8,128)(2,1)S(1)}, u32[]{:S(2)}, u32[]{:S(2)}) collective-permute-start(bf16[2,256,512]{2,1,0:T(8,128)(2,1)S(1)} %shard_map.88.a), channel_id=1, source_target_pairs={{0,2},{2,0},{1,3},{3,1},{4,6},{6,4},{5,7},{7,5},{8,10},{10,8},{9,1... | collective-permute-start | bytes 1572872 | tf_op jit(solution)/shard_map/ppermute | solution.py:15
  116.7 21.8 %collective-permute-start.35 = (bf16[2,256,512]{2,1,0:T(8,128)(2,1)S(1)}, bf16[2,256,512]{2,1,0:T(8,128)(2,1)S(1)}, u32[]{:S(2)}, u32[]{:S(2)}) collective-permute-start(bf16[2,256,512]{2,1,0:T(8,128)(2,1)S(1)} %shard_map.88.a), channel_id=1, source_target_pairs={{0,1},{1,0},{2,3},{3,2},{4,5},{5,4},{6,7},{7,6},{8,9},{9,8},{10,11... | collective-permute-start | bytes 1572872 | tf_op jit(solution)/shard_map/ppermute | solution.py:15
  118.0 31.7 %collective-permute-start.30 = (bf16[2,256,512]{2,1,0:T(8,128)(2,1)S(1)}, bf16[2,256,512]{2,1,0:T(8,128)(2,1)S(1)}, u32[]{:S(2)}, u32[]{:S(2)}) collective-permute-start(bf16[2,256,512]{2,1,0:T(8,128)(2,1)S(1)} %shard_map.86.a), channel_id=1, source_target_pairs={{0,2},{2,0},{1,3},{3,1},{4,6},{6,4},{5,7},{7,5},{8,10},{10,8},{9,1... | collective-permute-start | bytes 1572872 | tf_op jit(solution)/shard_map/ppermute | solution.py:15
  127.2 22.5 %collective-permute-start.31 = (bf16[2,256,512]{2,1,0:T(8,128)(2,1)S(1)}, bf16[2,256,512]{2,1,0:T(8,128)(2,1)S(1)}, u32[]{:S(2)}, u32[]{:S(2)}) collective-permute-start(bf16[2,256,512]{2,1,0:T(8,128)(2,1)S(1)} %shard_map.86.a), channel_id=1, source_target_pairs={{0,1},{1,0},{2,3},{3,2},{4,5},{5,4},{6,7},{7,6},{8,9},{9,8},{10,11... | collective-permute-start | bytes 1572872 | tf_op jit(solution)/shard_map/ppermute | solution.py:15
  127.2 33.7 %collective-permute-start.26 = (bf16[2,256,512]{2,1,0:T(8,128)(2,1)S(1)}, bf16[2,256,512]{2,1,0:T(8,128)(2,1)S(1)}, u32[]{:S(2)}, u32[]{:S(2)}) collective-permute-start(bf16[2,256,512]{2,1,0:T(8,128)(2,1)S(1)} %shard_map.84.a), channel_id=1, source_target_pairs={{0,2},{2,0},{1,3},{3,1},{4,6},{6,4},{5,7},{7,5},{8,10},{10,8},{9,1... | collective-permute-start | bytes 1572872 | tf_op jit(solution)/shard_map/ppermute | solution.py:15
  129.3 31.6 %copy-start.11 = (bf16[2,128,1024]{2,1,0:T(8,128)(2,1)S(1)}, bf16[2,128,1024]{2,1,0:T(8,128)(2,1)}, u32[]{:S(2)}) copy-start(bf16[2,128,1024]{2,1,0:T(8,128)(2,1)} %copy-done.10) | copy-start | bytes 1572868
  129.8 39.5 %copy-start.7 = (bf16[2,128,1024]{2,1,0:T(8,128)(2,1)S(1)}, bf16[2,128,1024]{2,1,0:T(8,128)(2,1)}, u32[]{:S(2)}) copy-start(bf16[2,128,1024]{2,1,0:T(8,128)(2,1)} %copy-done.6) | copy-start | bytes 1572868
  129.9 39.5 %copy-start.15 = (bf16[2,128,1024]{2,1,0:T(8,128)(2,1)S(1)}, bf16[2,128,1024]{2,1,0:T(8,128)(2,1)}, u32[]{:S(2)}) copy-start(bf16[2,128,1024]{2,1,0:T(8,128)(2,1)} %copy-done.14) | copy-start | bytes 1572868
  138.4 23.7 %collective-permute-start.27 = (bf16[2,256,512]{2,1,0:T(8,128)(2,1)S(1)}, bf16[2,256,512]{2,1,0:T(8,128)(2,1)S(1)}, u32[]{:S(2)}, u32[]{:S(2)}) collective-permute-start(bf16[2,256,512]{2,1,0:T(8,128)(2,1)S(1)} %shard_map.84.a), channel_id=1, source_target_pairs={{0,1},{1,0},{2,3},{3,2},{4,5},{5,4},{6,7},{7,6},{8,9},{9,8},{10,11... | collective-permute-start | bytes 1572872 | tf_op jit(solution)/shard_map/ppermute | solution.py:15
  138.5 30.9 %collective-permute-start.22 = (bf16[2,256,512]{2,1,0:T(8,128)(2,1)S(1)}, bf16[2,256,512]{2,1,0:T(8,128)(2,1)S(1)}, u32[]{:S(2)}, u32[]{:S(2)}) collective-permute-start(bf16[2,256,512]{2,1,0:T(8,128)(2,1)S(1)} %shard_map.82.a), channel_id=1, source_target_pairs={{0,2},{2,0},{1,3},{3,1},{4,6},{6,4},{5,7},{7,5},{8,10},{10,8},{9,1... | collective-permute-start | bytes 1572872 | tf_op jit(solution)/shard_map/ppermute | solution.py:15
  149.7 19.9 %collective-permute-start.23 = (bf16[2,256,512]{2,1,0:T(8,128)(2,1)S(1)}, bf16[2,256,512]{2,1,0:T(8,128)(2,1)S(1)}, u32[]{:S(2)}, u32[]{:S(2)}) collective-permute-start(bf16[2,256,512]{2,1,0:T(8,128)(2,1)S(1)} %shard_map.82.a), channel_id=1, source_target_pairs={{0,1},{1,0},{2,3},{3,2},{4,5},{5,4},{6,7},{7,6},{8,9},{9,8},{10,11... | collective-permute-start | bytes 1572872 | tf_op jit(solution)/shard_map/ppermute | solution.py:15
  149.7 21.9 %collective-permute-start.40 = (bf16[2,256,512]{2,1,0:T(8,128)(2,1)S(1)}, bf16[2,256,512]{2,1,0:T(8,128)(2,1)S(1)}, u32[]{:S(2)}, u32[]{:S(2)}) collective-permute-start(bf16[2,256,512]{2,1,0:T(8,128)(2,1)S(1)} %collective-permute-done.38.b), channel_id=1, source_target_pairs={{0,1},{1,0},{2,3},{3,2},{4,5},{5,4},{6,7},{7,6},{8,9},{9,8},{10,11... | collective-permute-start | bytes 1572872 | tf_op jit(solution)/shard_map/ppermute | solution.py:15
  160.9 14.6 %collective-permute-start.36 = (bf16[2,256,512]{2,1,0:T(8,128)(2,1)S(1)}, bf16[2,256,512]{2,1,0:T(8,128)(2,1)S(1)}, u32[]{:S(2)}, u32[]{:S(2)}) collective-permute-start(bf16[2,256,512]{2,1,0:T(8,128)(2,1)S(1)} %collective-permute-done.34.b), channel_id=1, source_target_pairs={{0,1},{1,0},{2,3},{3,2},{4,5},{5,4},{6,7},{7,6},{8,9},{9,8},{10,11... | collective-permute-start | bytes 1572872 | tf_op jit(solution)/shard_map/ppermute | solution.py:15
  162.2 18.4 %collective-permute-start.18 = (bf16[2,256,512]{2,1,0:T(8,128)(2,1)S(1)}, bf16[2,256,512]{2,1,0:T(8,128)(2,1)S(1)}, u32[]{:S(2)}, u32[]{:S(2)}) collective-permute-start(bf16[2,256,512]{2,1,0:T(8,128)(2,1)S(1)} %shard_map.80.a), channel_id=1, source_target_pairs={{0,2},{2,0},{1,3},{3,1},{4,6},{6,4},{5,7},{7,5},{8,10},{10,8},{9,1... | collective-permute-start | bytes 1572872 | tf_op jit(solution)/shard_map/ppermute | solution.py:15
  169.3 11.2 %collective-permute-start.32 = (bf16[2,256,512]{2,1,0:T(8,128)(2,1)S(1)}, bf16[2,256,512]{2,1,0:T(8,128)(2,1)S(1)}, u32[]{:S(2)}, u32[]{:S(2)}) collective-permute-start(bf16[2,256,512]{2,1,0:T(8,128)(2,1)S(1)} %collective-permute-done.30.b), channel_id=1, source_target_pairs={{0,1},{1,0},{2,3},{3,2},{4,5},{5,4},{6,7},{7,6},{8,9},{9,8},{10,11... | collective-permute-start | bytes 1572872 | tf_op jit(solution)/shard_map/ppermute | solution.py:15
  169.6 20.3 %collective-permute-start.7 = (bf16[2,256,512]{2,1,0:T(8,128)(2,1)S(1)}, bf16[2,256,512]{2,1,0:T(8,128)(2,1)S(1)}, u32[]{:S(2)}, u32[]{:S(2)}) collective-permute-start(bf16[2,256,512]{2,1,0:T(8,128)(2,1)S(1)} %shard_map.78.a), channel_id=1, source_target_pairs={{0,2},{2,0},{1,3},{3,1},{4,6},{6,4},{5,7},{7,5},{8,10},{10,8},{9,1... | collective-permute-start | bytes 1572872 | tf_op jit(solution)/shard_map/ppermute | solution.py:15
  171.5 18.3 %collective-permute-start.28 = (bf16[2,256,512]{2,1,0:T(8,128)(2,1)S(1)}, bf16[2,256,512]{2,1,0:T(8,128)(2,1)S(1)}, u32[]{:S(2)}, u32[]{:S(2)}) collective-permute-start(bf16[2,256,512]{2,1,0:T(8,128)(2,1)S(1)} %collective-permute-done.26.b), channel_id=1, source_target_pairs={{0,1},{1,0},{2,3},{3,2},{4,5},{5,4},{6,7},{7,6},{8,9},{9,8},{10,11... | collective-permute-start | bytes 1572872 | tf_op jit(solution)/shard_map/ppermute | solution.py:15
  175.5 18.6 %collective-permute-start.24 = (bf16[2,256,512]{2,1,0:T(8,128)(2,1)S(1)}, bf16[2,256,512]{2,1,0:T(8,128)(2,1)S(1)}, u32[]{:S(2)}, u32[]{:S(2)}) collective-permute-start(bf16[2,256,512]{2,1,0:T(8,128)(2,1)S(1)} %collective-permute-done.22.b), channel_id=1, source_target_pairs={{0,1},{1,0},{2,3},{3,2},{4,5},{5,4},{6,7},{7,6},{8,9},{9,8},{10,11... | collective-permute-start | bytes 1572872 | tf_op jit(solution)/shard_map/ppermute | solution.py:15
  180.6 17.2 %collective-permute-start.19 = (bf16[2,256,512]{2,1,0:T(8,128)(2,1)S(1)}, bf16[2,256,512]{2,1,0:T(8,128)(2,1)S(1)}, u32[]{:S(2)}, u32[]{:S(2)}) collective-permute-start(bf16[2,256,512]{2,1,0:T(8,128)(2,1)S(1)} %shard_map.80.a), channel_id=1, source_target_pairs={{0,1},{1,0},{2,3},{3,2},{4,5},{5,4},{6,7},{7,6},{8,9},{9,8},{10,11... | collective-permute-start | bytes 1572872 | tf_op jit(solution)/shard_map/ppermute | solution.py:15
  180.6 17.2 %collective-permute-start.20 = (bf16[2,256,512]{2,1,0:T(8,128)(2,1)S(1)}, bf16[2,256,512]{2,1,0:T(8,128)(2,1)S(1)}, u32[]{:S(2)}, u32[]{:S(2)}) collective-permute-start(bf16[2,256,512]{2,1,0:T(8,128)(2,1)S(1)} %collective-permute-done.18.b), channel_id=1, source_target_pairs={{0,1},{1,0},{2,3},{3,2},{4,5},{5,4},{6,7},{7,6},{8,9},{9,8},{10,11... | collective-permute-start | bytes 1572872 | tf_op jit(solution)/shard_map/ppermute | solution.py:15
  189.8 11.7 %collective-permute-start.8 = (bf16[2,256,512]{2,1,0:T(8,128)(2,1)S(1)}, bf16[2,256,512]{2,1,0:T(8,128)(2,1)S(1)}, u32[]{:S(2)}, u32[]{:S(2)}) collective-permute-start(bf16[2,256,512]{2,1,0:T(8,128)(2,1)S(1)} %shard_map.78.a), channel_id=1, source_target_pairs={{0,1},{1,0},{2,3},{3,2},{4,5},{5,4},{6,7},{7,6},{8,9},{9,8},{10,11... | collective-permute-start | bytes 1572872 | tf_op jit(solution)/shard_map/ppermute | solution.py:15
  189.8 11.7 %collective-permute-start.9 = (bf16[2,256,512]{2,1,0:T(8,128)(2,1)S(1)}, bf16[2,256,512]{2,1,0:T(8,128)(2,1)S(1)}, u32[]{:S(2)}, u32[]{:S(2)}) collective-permute-start(bf16[2,256,512]{2,1,0:T(8,128)(2,1)S(1)} %collective-permute-done.7.b), channel_id=1, source_target_pairs={{0,1},{1,0},{2,3},{3,2},{4,5},{5,4},{6,7},{7,6},{8,9},{9,8},{10,11... | collective-permute-start | bytes 1572872 | tf_op jit(solution)/shard_map/ppermute | solution.py:15
  (9 other events, 52.3 us)

commit v2 on v1

v2 whole, which is shorter than its diff:
```python
import functools

import jax
import jax.numpy as jnp
from jax import lax
from jax.experimental import pallas as pl
from jax.experimental.pallas import tpu as pltpu
from jax.sharding import PartitionSpec as P

VMEM_LIMIT = 24 * 1024 * 1024
LANES = 256


def swap_neighbours(value, axis):
    return lax.ppermute(value, axis, [(i, i ^ 1) for i in range(lax.axis_size(axis))])


def contract_tokens(left, right):
    return lax.dot_general(
        left, right, (((0,), (0,)), ((), ())), preferred_element_type=jnp.float32
    )


def d_gate_and_up(hidden_grad, gates, ups):
    sigmoid_gate = 1.0 / (1.0 + jnp.exp(-gates))
    d_gate = hidden_grad * ups * sigmoid_gate * (1.0 + gates * (1.0 - sigmoid_gate))
    d_up = hidden_grad * gates * sigmoid_gate
    return d_gate.astype(jnp.bfloat16), d_up.astype(jnp.bfloat16)


def call(kernel, grid, in_specs, out_specs, out_shape, operands, prefetch=0, scratch=(), aliases=None):
    return pl.pallas_call(
        kernel,
        grid_spec=pltpu.PrefetchScalarGridSpec(
            num_scalar_prefetch=prefetch,
            grid=grid,
            in_specs=in_specs,
            out_specs=out_specs,
            scratch_shapes=scratch,
        ),
        out_shape=out_shape,
        input_output_aliases=aliases or {},
        compiler_params=pltpu.CompilerParams(vmem_limit_bytes=VMEM_LIMIT),
        cost_estimate=pl.CostEstimate(flops=1, bytes_accessed=1, transcendentals=0),
    )(*operands)


def scale_kernel(block_side, first_block, codes, scales, weight):
    feature_rows, lanes = codes.shape
    base = first_block + pl.program_id(0) * (lanes // block_side)
    for i in range(feature_rows // block_side):
        for j in range(lanes // block_side):
            rows = slice(i * block_side, (i + 1) * block_side)
            cols = slice(j * block_side, (j + 1) * block_side)
            scaled = codes[rows, cols].astype(jnp.float32) * scales[i, base + j]
            weight[0, rows, cols] = scaled.astype(jnp.bfloat16)


def scaled_weight(codes, scales, start, width):
    features = codes.shape[0]
    block_side = features // scales.shape[0]
    offset = start // LANES
    return call(
        functools.partial(scale_kernel, block_side, start // block_side),
        (width // LANES,),
        [
            pl.BlockSpec((features, LANES), lambda i: (0, offset + i)),
            pl.BlockSpec(memory_space=pltpu.SMEM),
        ],
        pl.BlockSpec((1, features, LANES), lambda i: (i, 0, 0)),
        jax.ShapeDtypeStruct((width // LANES, features, LANES), jnp.bfloat16),
        [codes, scales],
    )


def arrange_kernel(places, own, buddy, across, middle, outward, out):
    for k, shard in enumerate((own, buddy, across)):
        out[:, pl.ds(places[k], 1)] = shard[...][:, None]

    @pl.when(places[4] == 1)
    def _():
        out[:, pl.ds(places[3], 1)] = middle[...][:, None]

    @pl.when(places[4] == 0)
    def _():
        out[:, pl.ds(places[3], 1)] = outward[...][:, None]


def arranged(places, shards):
    lead, tokens, features = shards[0].shape
    shape = (lead, 4, tokens, features)
    return call(
        arrange_kernel,
        (1,),
        [pl.BlockSpec((lead, tokens, features), lambda i, f: (0, 0, 0))] * 5,
        pl.BlockSpec(shape, lambda i, f: (0, 0, 0, 0)),
        jax.ShapeDtypeStruct(shape, shards[0].dtype),
        [places, *shards],
        prefetch=1,
    )


def partial_kernel(parts, grads, weight, *outs):
    step = pl.program_id(0)
    product = jnp.dot(grads[...], weight[0], preferred_element_type=jnp.float32)
    product = product.astype(jnp.bfloat16)
    first = 0
    for count, split in parts:

        @pl.when(jnp.logical_and(step >= first, step < first + count))
        def _():
            rows = outs[0].shape[0]
            for k in range(1 + split):
                outs[k][...] = product[k * rows : (k + 1) * rows]

        outs = outs[1 + split :]
        first += count


def partial_products(grads, weight, parts):
    tokens, features = grads.shape
    outs, out_specs, first = [], [], 0
    for count, split in parts:
        rows = tokens // (1 + split)

        def place(i, first=first, count=count):
            return 0, jnp.clip(i - first, 0, count - 1)

        outs += [jax.ShapeDtypeStruct((rows, count * LANES), jnp.bfloat16)] * (1 + split)
        out_specs += [pl.BlockSpec((rows, LANES), place)] * (1 + split)
        first += count
    return call(
        functools.partial(partial_kernel, parts),
        (first,),
        [
            pl.BlockSpec((tokens, features), lambda i: (0, 0)),
            pl.BlockSpec((1, features, LANES), lambda i: (i, 0, 0)),
        ],
        out_specs,
        outs,
        [grads, weight],
    )


def touch_kernel(value, out):
    pass


def touched(value):
    return call(
        touch_kernel,
        (1,),
        [pl.BlockSpec(memory_space=pl.ANY)],
        pl.BlockSpec(memory_space=pl.ANY),
        jax.ShapeDtypeStruct(value.shape, value.dtype),
        [value],
        aliases={0: 0},
    )


def activation_kernel(own, other, gates, ups, out):
    hidden_grad = own[...].astype(jnp.float32) + other[...].astype(jnp.float32)
    d_gate, d_up = d_gate_and_up(
        hidden_grad, gates[0].astype(jnp.float32), ups[0].astype(jnp.float32)
    )
    out[0] = d_gate
    out[1] = d_up


def activation_grads(own, other, gate_pre, up_pre, piece_start, start, width):
    tokens = own.shape[0]
    offset = start // LANES
    inner = (start - piece_start) // LANES
    piece = pl.BlockSpec((tokens, LANES), lambda i: (0, inner + i))
    saved = pl.BlockSpec((1, tokens, LANES), lambda i: (0, 0, offset + i))
    return call(
        activation_kernel,
        (width // LANES,),
        [piece, piece, saved, saved],
        pl.BlockSpec((2, tokens, LANES), lambda i: (0, 0, i)),
        jax.ShapeDtypeStruct((2, tokens, width), jnp.bfloat16),
        [own, other, gate_pre, up_pre],
    )


def both_kernel(own, other, gates, ups, other_gates, other_ups, mine, theirs):
    half = gates.shape[1]
    for k, (gate, up, out) in enumerate(((gates, ups, mine), (other_gates, other_ups, theirs))):
        here = slice(k * half, (k + 1) * half)
        there = slice((1 - k) * half, (2 - k) * half)
        hidden_grad = own[here].astype(jnp.float32) + other[there].astype(jnp.float32)
        d_gate, d_up = d_gate_and_up(
            hidden_grad, gate[0].astype(jnp.float32), up[0].astype(jnp.float32)
        )
        out[0] = d_gate
        out[1] = d_up


def both_activation_grads(own, other, gate_pre, up_pre, other_gates, other_ups, start, inner):
    tokens, width = own.shape
    offset = start // LANES
    inner = inner // LANES
    piece = pl.BlockSpec((tokens, LANES), lambda i: (0, i))
    saved = pl.BlockSpec((1, tokens // 2, LANES), lambda i: (0, 0, offset + i))
    swapped = pl.BlockSpec((1, tokens // 2, LANES), lambda i: (0, 0, inner + i))
    out = jax.ShapeDtypeStruct((2, tokens // 2, width), jnp.bfloat16)
    out_spec = pl.BlockSpec((2, tokens // 2, LANES), lambda i: (0, 0, i))
    return call(
        both_kernel,
        (width // LANES,),
        [piece, piece, saved, saved, swapped, swapped],
        [out_spec, out_spec],
        [out, out],
        [own, other, gate_pre, up_pre, other_gates, other_ups],
    )


def weight_kernel(inputs, mine, theirs, mine_far, theirs_far, *refs):
    for which, out in enumerate(refs[-2:]):
        pieces = [piece[which] for piece in (mine, theirs, mine_far, theirs_far)]
        out[...] = contract_tokens(jnp.concatenate(pieces, axis=0), inputs[...])


def weight_grads(inputs, pieces, start, outs, hidden):
    _, quarter, width = pieces[0].shape
    tokens, features = inputs.shape
    offset = start // LANES
    piece = pl.BlockSpec((2, quarter, LANES), lambda i: (0, 0, i))
    out_spec = pl.BlockSpec((LANES, features), lambda i: (offset + i, 0))
    out = jax.ShapeDtypeStruct((hidden, features), jnp.float32)
    in_specs = [pl.BlockSpec((tokens, features), lambda i: (0, 0))] + [piece] * 4
    operands = [inputs, *pieces]
    aliases = {}
    if outs is not None:
        in_specs += [pl.BlockSpec(memory_space=pl.ANY)] * 2
        aliases = {5: 0, 6: 1}
        operands += list(outs)
    return call(
        weight_kernel,
        (width // LANES,),
        in_specs,
        [out_spec, out_spec],
        [out, out],
        operands,
        aliases=aliases,
    )


class Chain:
    def __init__(self):
        self.last = ()

    def __call__(self, value):
        return lax.optimization_barrier((value, *self.last))[0]

    def done(self, value):
        self.last = (value,)

    def wait(self, value):
        self.last += (value,)


def on_pairs(layer_input, out_grad, down_codes, down_scales, gate_pre, up_pre):
    hidden = down_codes.shape[1]
    unit = hidden // 7
    row = lax.axis_index("row")
    col = lax.axis_index("col")
    depth = lax.axis_index("depth")
    shard_tokens, features = out_grad.shape[1:]
    half_features = features // 2
    chain = Chain()

    shared = 4 * unit
    other_gates = swap_neighbours(gate_pre[:, :, shared:], "col")
    other_ups = swap_neighbours(up_pre[:, :, shared:], "col")

    def gather_near(shard):
        buddy = lax.ppermute(shard, "row", [(0, 1), (1, 0), (2, 3), (3, 2)])
        across = lax.ppermute(shard, "row", [(0, 3), (3, 0), (1, 2), (2, 1)])
        return buddy, across

    def gather_far(buddy, across):
        outward = lax.ppermute(across, "row", [(1, 0), (2, 3)])
        middle = lax.ppermute(buddy, "row", [(1, 2), (2, 1)])
        return middle, outward

    is_inner = jnp.logical_or(row == 1, row == 2).astype(jnp.int32)
    shards = [row, row ^ 1, 3 - row, (3 - row) ^ 1]
    places = jnp.stack([*(lax.rem(s + 4 - 2 * col, 4) for s in shards), is_inner])
    places = places.astype(jnp.int32)

    near = gather_near(out_grad)
    lead = 2 * unit
    first_weight = scaled_weight(down_codes, down_scales, 0, lead)
    chain.done(first_weight)
    far = gather_far(*(chain(part) for part in near))
    weight = scaled_weight(chain(down_codes), down_scales, lead, hidden - lead)
    chain.done(weight)

    keep = lax.dynamic_slice_in_dim(layer_input, depth * half_features, half_features, 2)
    send = lax.dynamic_slice_in_dim(layer_input, (1 - depth) * half_features, half_features, 2)
    both = jnp.concatenate([keep, swap_neighbours(send, "depth")], axis=0)

    outward = lax.optimization_barrier((far[1], other_gates, other_ups))[0]
    grads = arranged(chain(places), [out_grad, *near, far[0], outward])
    chain.done(grads)
    grads = grads.reshape(4 * shard_tokens, features)

    starts = {f"p{k}": k * unit for k in range(4)}
    starts.update({f"s{k}": shared + k * unit for k in range(3)})
    own_part, other_part, mine, theirs, mine_far, theirs_far = {}, {}, {}, {}, {}, {}
    blocks = unit // LANES

    def send_step(names, kept, sent):
        received = swap_neighbours(sent, "col")
        for name in names:
            own_part[name] = (kept, starts[names[0]])
            other_part[name] = received

    def touch_step(name):
        value = touched(chain(shared_parts[name]))
        chain.done(value)
        send_step([name], value, value)

    def activation_step(name):
        kept, piece_start = own_part[name]
        operands = (chain(kept), other_part[name], gate_pre, up_pre)
        if name[0] == "p":
            mine[name] = activation_grads(*operands, piece_start, starts[name], unit)
            theirs[name] = swap_neighbours(mine[name], "col")
        else:
            mine[name], theirs[name] = both_activation_grads(
                *operands, other_gates, other_ups, starts[name], starts[name] - shared
            )
        chain.done(mine[name])

    def far_step(name):
        mine_far[name] = swap_neighbours(chain(mine[name]), "depth")
        theirs_far[name] = swap_neighbours(chain(theirs[name]), "depth")

    def weight_step(name, outs):
        pieces = [part[name] for part in (mine, theirs, mine_far, theirs_far)]
        outs = weight_grads(chain(inputs), pieces, starts[name], outs, hidden)
        chain.done(outs[0])
        return outs

    outs = None
    kept, sent = partial_products(chain(grads), first_weight, [(2 * blocks, True)])
    chain.done(sent)
    send_step(["p0", "p1"], kept, sent)
    kept, sent, *rest = partial_products(
        chain(grads), weight, [(2 * blocks, True)] + [(blocks, False)] * 3
    )
    chain.done(sent)
    send_step(["p2", "p3"], kept, sent)
    shared_parts = {f"s{k}": part for k, part in enumerate(rest)}
    input_near = gather_near(chain(both))
    activation_step("p0")
    chain.wait(other_part["p2"])
    touch_step("s0")
    input_far = gather_far(*(chain(part) for part in input_near))
    far_step("p0")
    chain.wait(theirs["p0"])
    touch_step("s1")
    activation_step("s0")
    inputs = arranged(chain(places), [both, *input_near, *input_far])
    chain.done(inputs)
    inputs = inputs.reshape(-1, half_features)
    outs = weight_step("p0", outs)
    far_step("s0")
    touch_step("s2")
    activation_step("s1")
    outs = weight_step("s0", outs)
    far_step("s1")
    activation_step("p1")
    activation_step("s2")
    outs = weight_step("s1", outs)
    far_step("s2")
    activation_step("p2")
    chain.wait(theirs["p1"])
    outs = weight_step("s2", outs)
    far_step("p1")
    activation_step("p3")
    chain.wait(theirs["p2"])
    outs = weight_step("p1", outs)
    far_step("p2")
    chain.wait(theirs["p3"])
    far_step("p3")
    outs = weight_step("p2", outs)
    outs = weight_step("p3", outs)
    return tuple(outs)


def on_many(layer_input, out_grad, down_codes, down_scales, gate_pre, up_pre):
    feature_rows, hidden_cols = down_codes.shape
    blocks_feat, blocks_hidden = down_scales.shape
    block_side = feature_rows // blocks_feat
    scaled = down_codes.astype(jnp.float32).reshape(
        blocks_feat, block_side, blocks_hidden, block_side
    )
    scaled = scaled * down_scales[:, None, :, None]
    down_weight = scaled.reshape(feature_rows, hidden_cols).astype(jnp.bfloat16)
    grads = lax.all_gather(out_grad, "row", axis=1, tiled=True)[0]
    half_features = feature_rows // 2
    depth = lax.axis_index("depth")
    keep = lax.dynamic_slice_in_dim(layer_input, depth * half_features, half_features, 2)
    send = lax.dynamic_slice_in_dim(layer_input, (1 - depth) * half_features, half_features, 2)
    both = jnp.concatenate([keep, swap_neighbours(send, "depth")], axis=0)
    inputs = lax.all_gather(both, "row", axis=1, tiled=True)
    hidden_grad = lax.psum_scatter(
        jnp.dot(grads, down_weight, preferred_element_type=jnp.float32).astype(jnp.bfloat16),
        "col",
        scatter_dimension=0,
        tiled=True,
    ).astype(jnp.float32)
    d_gate, d_up = d_gate_and_up(
        hidden_grad, gate_pre[0].astype(jnp.float32), up_pre[0].astype(jnp.float32)
    )
    results = []
    for mine in (d_gate, d_up):
        gathered = lax.all_gather(mine, "col", axis=0, tiled=True)
        other = swap_neighbours(gathered, "depth")
        results.append(
            contract_tokens(
                jnp.concatenate([gathered, other], axis=0),
                inputs.reshape(-1, half_features),
            )
        )
    return tuple(results)


def solution(mesh):
    in_specs = (
        P("depth", ("groups", "row"), "col"),
        P("depth", ("groups", "row"), "col"),
        P("col", "row"),
        P("col", "row"),
        P("depth", ("groups", "col"), "row"),
        P("depth", ("groups", "col"), "row"),
    )
    out_specs = (P(("groups", "row"), ("col", "depth")), P(("groups", "row"), ("col", "depth")))
    pairs = mesh.shape["col"] == 2 and mesh.shape["row"] == 4
    return jax.shard_map(
        on_pairs if pairs else on_many,
        mesh=mesh,
        in_specs=in_specs,
        out_specs=out_specs,
        check_vma=False,
    )
```

time: 206 us -> 177 us (0.86)
  waiting for transfers between devices: 93.6 us -> 62 us
  local copies, waits for them, and re-layouts: 2.7 us -> 29.4 us
  starting transfers between devices: 52.8 us -> 30.5 us
  other arithmetic: 4.23 us -> 0.05 us
  Pallas kernels: 50.8 us -> 53.2 us
    ppermute x41 -> x34, waiting for transfers between devices: 93.6 us -> 62 us  [the longest x26 37.7 us: swap_neighbours(): lax.ppermute(value, axis, [(i, i ^ 1) for i in range(lax.axis_size(axis))])]
    unnamed x32 -> x26, local copies, waits for them, and re-layouts: 1.03 us -> 23.9 us
    ppermute x41 -> x34, starting transfers between devices: 52.8 us -> 30.5 us  [the longest x26 16.1 us: swap_neighbours(): lax.ppermute(value, axis, [(i, i ^ 1) for i in range(lax.axis_size(axis))])]
    dynamic_update_slice x7 -> x0, other arithmetic: 4.18 us -> none  [ring_gather(): out = lax.dynamic_update_index_in_dim(out, piece, slot, stack_axis)]
    slice x0 -> x2, local copies, waits for them, and re-layouts: none -> 4.16 us  [the longest x1 2.1 us: on_pairs(): other_gates = swap_neighbours(gate_pre[:, :, shared:], 'col')]
    pallas_call x21 -> x23, Pallas kernels: 50.8 us -> 53.2 us  [call(): pl.pallas_call(kernel, grid_spec=pltpu.PrefetchScalarGridSpec(num_scalar_...]
  transfers between devices with their start and end apart: 41 -> 34, of which waited for: 17 -> 11; matrix products, arithmetic and copies ran while one was open for 3% -> 3% of each run, Pallas kernels for 23% -> 25%
where the time goes in v2:
time: 177 us; the launch traced here: 176 us
  waiting for transfers between devices  62 us (35%)
  Pallas kernels  53.2 us (30%)
  starting transfers between devices  30.5 us (17%)
  local copies, waits for them, and re-layouts  29.4 us (17%)
    pallas_call x23, Pallas kernels, call(): pl.pallas_call(kernel, grid_spec=pltpu.PrefetchScalarGridSpec(num_scalar_...  53.2 us
    ppermute x26, waiting for transfers between devices, swap_neighbours(): lax.ppermute(value, axis, [(i, i ^ 1) for i in range(lax.axis_size(axis))])  37.7 us
    unnamed x26, local copies, waits for them, and re-layouts  23.9 us
    ppermute x26, starting transfers between devices, swap_neighbours(): lax.ppermute(value, axis, [(i, i ^ 1) for i in range(lax.axis_size(axis))])  16.1 us
    ppermute x2, waiting for transfers between devices, gather_near(): across = lax.ppermute(shard, 'row', [(0, 3), (3, 0), (1, 2), (2, 1)])  12.6 us
    ppermute x2, starting transfers between devices, gather_near(): across = lax.ppermute(shard, 'row', [(0, 3), (3, 0), (1, 2), (2, 1)])  7.41 us
    ppermute x2, waiting for transfers between devices, gather_near(): buddy = lax.ppermute(shard, 'row', [(0, 1), (1, 0), (2, 3), (3, 2)])  6.4 us
    ppermute x2, waiting for transfers between devices, gather_far(): outward = lax.ppermute(across, 'row', [(1, 0), (2, 3)])  5.32 us
  transfers between devices with their start and end apart: 34, of which 11 were waited for; matrix products, arithmetic and copies ran while one was open for 3% of the time, Pallas kernels for 25%

profile of v2, /device:TPU:0, one launch (start us, length us, event | category | flops | bytes accessed | tf_op | source)
XLA Modules:
  0.0 176.1 jit_solution(17186056535719160764)
XLA Ops:
  0.6 5.1 %collective-permute-start.1 = (bf16[1,128,2048]{2,1,0:T(8,128)(2,1)}, bf16[1,128,2048]{2,1,0:T(8,128)(2,1)}, u32[]{:S(2)}, u32[]{:S(2)}) collective-permute-start(bf16[1,128,2048]{2,1,0:T(8,128)(2,1)} %own.1), channel_id=1, source_target_pairs={{0,12},{12,0},{4,8},{8,4},{1,13},{13,1},{5,9},{9,5},{2,14},{14,2},... | collective-permute-start | bytes 1572872 | tf_op jit(solution)/shard_map/ppermute | solution.py:279
  5.7 2.1 %slice.6 = bf16[1,256,1536]{2,1,0:T(8,128)(2,1)} slice(bf16[1,256,3584]{2,1,0:T(8,128)(2,1)} %gates.13), slice={[0:1], [0:256], [2048:3584]} | slice | bytes 1572864 | tf_op jit(solution)/shard_map/slice | solution.py:274
  7.8 1.5 collective-permute-start.4
  9.3 2.1 %slice.7 = bf16[1,256,1536]{2,1,0:T(8,128)(2,1)} slice(bf16[1,256,3584]{2,1,0:T(8,128)(2,1)} %ups.13), slice={[0:1], [0:256], [2048:3584]} | slice | bytes 1572864 | tf_op jit(solution)/shard_map/slice | solution.py:275
  11.9 5.2 %copy-done.2 = bf16[2048,3584]{1,0:T(8,128)(2,1)S(1)} copy-done((bf16[2048,3584]{1,0:T(8,128)(2,1)S(1)}, bf16[2048,3584]{1,0:T(8,128)(2,1)}, u32[]{:S(2)}) %copy-start.2) | copy-done | bytes 14680088
  17.8 1.8 %shard_map.77.weight = bf16[4,2048,256]{2,1,0:T(8,128)(2,1)S(1)} custom-call(bf16[2048,3584]{1,0:T(8,128)(2,1)S(1)} %copy-done.2, f32[16,28]{1,0:T(8,128)S(1)} %copy-done.12), custom_call_target="tpu_custom_call" | custom-call | flops 1 | bytes 1 | tf_op jit(solution)/shard_map/pallas_call | solution.py:32
  19.6 2.0 %copy-done.7 = bf16[4,2048,256]{2,1,0:T(8,128)(2,1)} copy-done((bf16[4,2048,256]{2,1,0:T(8,128)(2,1)}, bf16[4,2048,256]{2,1,0:T(8,128)(2,1)S(1)}, u32[]{:S(2)}) %copy-start.7) | copy-done | bytes 4194328
  21.6 1.3 collective-permute-start.3
  22.9 6.4 %collective-permute-done.buddy = bf16[1,128,2048]{2,1,0:T(8,128)(2,1)} collective-permute-done((bf16[1,128,2048]{2,1,0:T(8,128)(2,1)}, bf16[1,128,2048]{2,1,0:T(8,128)(2,1)}, u32[]{:S(2)}, u32[]{:S(2)}) %collective-permute-start) | collective-permute-done | bytes 524320 | tf_op jit(solution)/shard_map/ppermute | solution.py:278
  29.3 1.5 collective-permute-start.2
  30.8 3.6 %shard_map.78.weight = bf16[10,2048,256]{2,1,0:T(8,128)(2,1)S(1)} custom-call(bf16[2048,3584]{1,0:T(8,128)(2,1)S(1)} %copy-done.2, f32[16,28]{1,0:T(8,128)S(1)} %copy-done.12), custom_call_target="tpu_custom_call" | custom-call | flops 1 | bytes 1 | tf_op jit(solution)/shard_map/pallas_call | solution.py:32
  34.4 4.1 %copy-done.3 = bf16[10,2048,256]{2,1,0:T(8,128)(2,1)} copy-done((bf16[10,2048,256]{2,1,0:T(8,128)(2,1)}, bf16[10,2048,256]{2,1,0:T(8,128)(2,1)S(1)}, u32[]{:S(2)}) %copy-start.3) | copy-done | bytes 10485784
  38.6 5.3 %collective-permute-done.5.other_ups = bf16[1,256,1536]{2,1,0:T(8,128)(2,1)S(1)} collective-permute-done((bf16[1,256,1536]{2,1,0:T(8,128)(2,1)}, bf16[1,256,1536]{2,1,0:T(8,128)(2,1)S(1)}, u32[]{:S(2)}, u32[]{:S(2)}) %collective-permute-start.5) | collective-permute-done | bytes 786464 | tf_op jit(solution)/shard_map/ppermute | solution.py:15
  43.9 1.0 copy-done.11
  45.0 2.2 %shard_map.79 = bf16[1,4,128,2048]{3,2,1,0:T(8,128)(2,1)S(1)} custom-call(s32[5]{0:T(128)S(1)} %stack.27.places, bf16[1,128,2048]{2,1,0:T(8,128)(2,1)S(1)} %copy-done.11, bf16[1,128,2048]{2,1,0:T(8,128)(2,1)} %collective-permute-done.buddy, bf16[1,128,2048]{2,1,0:T(8,128)(2,1)} %collective-permute-done.1.across, ...), custom_call_target="tpu_custom_call" | custom-call | flops 1 | bytes 1 | tf_op jit(solution)/shard_map/pallas_call | solution.py:32
  47.2 2.2 %copy-done.8 = bf16[4,2048,256]{2,1,0:T(8,128)(2,1)S(1)} copy-done((bf16[4,2048,256]{2,1,0:T(8,128)(2,1)S(1)}, bf16[4,2048,256]{2,1,0:T(8,128)(2,1)}, u32[]{:S(2)}) %copy-start.8) | copy-done | bytes 4194328
  49.4 3.7 %shard_map.80 = (bf16[256,1024]{1,0:T(8,128)(2,1)S(1)}, bf16[256,1024]{1,0:T(8,128)(2,1)}) custom-call(bf16[512,2048]{1,0:T(8,128)(2,1)S(1)} %bitcast.14, bf16[4,2048,256]{2,1,0:T(8,128)(2,1)S(1)} %copy-done.8), custom_call_target="tpu_custom_call" | custom-call | flops 1 | bytes 1 | tf_op jit(solution)/shard_map/pallas_call | solution.py:32
  53.1 1.3 copy-done.5
  55.2 1.5 collective-permute-start.6
  56.7 1.2 constant_dynamic-slice_fusion.1
  58.0 4.0 %copy-done.4 = bf16[10,2048,256]{2,1,0:T(8,128)(2,1)S(1)} copy-done((bf16[10,2048,256]{2,1,0:T(8,128)(2,1)S(1)}, bf16[10,2048,256]{2,1,0:T(8,128)(2,1)}, u32[]{:S(2)}) %copy-start.4) | copy-done | bytes 10485784
  62.0 1.6 copy-done.6
  63.6 8.2 %shard_map.81 = (bf16[256,1024]{1,0:T(8,128)(2,1)S(1)}, bf16[256,1024]{1,0:T(8,128)(2,1)S(1)}, bf16[512,512]{1,0:T(8,128)(2,1)S(1)}, bf16[512,512]{1,0:T(8,128)(2,1)S(1)}, bf16[512,512]{1,0:T(8,128)(2,1)S(1)}) custom-call(bf16[512,2048]{1,0:T(8,128)(2,1)S(1)} %bitcast.15, bf16[10,2048,256]{2,1,0:T(8,128)(2,1)S(1)} %copy-done.4), custom_call_target="tpu_custom_call" | custom-call | flops 1 | bytes 1 | tf_op jit(solution)/shard_map/pallas_call | solution.py:32
  72.4 2.3 %collective-permute-start.11 = (bf16[2,128,1024]{2,1,0:T(8,128)(2,1)S(1)}, bf16[2,128,1024]{2,1,0:T(8,128)(2,1)S(1)}, u32[]{:S(2)}, u32[]{:S(2)}) collective-permute-start(bf16[2,128,1024]{2,1,0:T(8,128)(2,1)S(1)} %pad_maximum_fusion.own), channel_id=1, source_target_pairs={{0,4},{4,0},{8,12},{12,8},{1,5},{5,1},{9,13},{13,9},{2,6},{6,2},{1... | collective-permute-start | bytes 1572872 | tf_op jit(solution)/shard_map/ppermute | solution.py:278
  74.7 2.3 %collective-permute-start.12 = (bf16[2,128,1024]{2,1,0:T(8,128)(2,1)S(1)}, bf16[2,128,1024]{2,1,0:T(8,128)(2,1)S(1)}, u32[]{:S(2)}, u32[]{:S(2)}) collective-permute-start(bf16[2,128,1024]{2,1,0:T(8,128)(2,1)S(1)} %pad_maximum_fusion.own), channel_id=1, source_target_pairs={{0,12},{12,0},{4,8},{8,4},{1,13},{13,1},{5,9},{9,5},{2,14},{14,2},... | collective-permute-start | bytes 1572872 | tf_op jit(solution)/shard_map/ppermute | solution.py:279
  78.0 1.3 shard_map.82.mine
  79.4 1.6 collective-permute-start.8
  80.9 5.6 %collective-permute-done.7.other = bf16[256,1024]{1,0:T(8,128)(2,1)S(1)} collective-permute-done((bf16[256,1024]{1,0:T(8,128)(2,1)S(1)}, bf16[256,1024]{1,0:T(8,128)(2,1)S(1)}, u32[]{:S(2)}, u32[]{:S(2)}) %collective-permute-start.7) | collective-permute-done | bytes 524320 | tf_op jit(solution)/shard_map/ppermute | solution.py:15
  87.7 12.6 %collective-permute-done.12.across = bf16[2,128,1024]{2,1,0:T(8,128)(2,1)S(1)} collective-permute-done((bf16[2,128,1024]{2,1,0:T(8,128)(2,1)S(1)}, bf16[2,128,1024]{2,1,0:T(8,128)(2,1)S(1)}, u32[]{:S(2)}, u32[]{:S(2)}) %collective-permute-start.12) | collective-permute-done | bytes 524320 | tf_op jit(solution)/shard_map/ppermute | solution.py:279
  100.3 1.3 collective-permute-start.14
  102.2 6.4 %collective-permute-done.9.other = bf16[512,512]{1,0:T(8,128)(2,1)S(1)} collective-permute-done((bf16[512,512]{1,0:T(8,128)(2,1)S(1)}, bf16[512,512]{1,0:T(8,128)(2,1)S(1)}, u32[]{:S(2)}, u32[]{:S(2)}) %collective-permute-start.9) | collective-permute-done | bytes 524320 | tf_op jit(solution)/shard_map/ppermute | solution.py:15
  110.1 5.3 %collective-permute-done.14.outward = bf16[2,128,1024]{2,1,0:T(8,128)(2,1)S(1)} collective-permute-done((bf16[2,128,1024]{2,1,0:T(8,128)(2,1)S(1)}, bf16[2,128,1024]{2,1,0:T(8,128)(2,1)S(1)}, u32[]{:S(2)}, u32[]{:S(2)}) %collective-permute-start.14) | collective-permute-done | bytes 524320 | tf_op jit(solution)/shard_map/ppermute | solution.py:283
  116.3 3.7 %shard_map.87 = (f32[3584,1024]{1,0:T(8,128)}, f32[3584,1024]{1,0:T(8,128)}) custom-call(bf16[1024,1024]{1,0:T(8,128)(2,1)S(1)} %bitcast.7, bf16[2,256,512]{2,1,0:T(8,128)(2,1)S(1)} %shard_map.82.mine, bf16[2,256,512]{2,1,0:T(8,128)(2,1)S(1)} %collective-permute-done.8.theirs, bf16[2,256,512]{2,1,0:T(8,128)(2,1)S(1)} %collective-permute-done.15.mine_far, ...), custom_call_target="tpu_custom_call" | custom-call | flops 1 | bytes 1 | tf_op jit(solution)/shard_map/pallas_call | solution.py:32
  120.5 1.5 collective-permute-start.20
  123.1 3.8 %shard_map.90 = (f32[3584,1024]{1,0:T(8,128)}, f32[3584,1024]{1,0:T(8,128)}) custom-call(bf16[1024,1024]{1,0:T(8,128)(2,1)S(1)} %bitcast.8, bf16[2,256,512]{2,1,0:T(8,128)(2,1)S(1)} %get-tuple-element.101.mine, bf16[2,256,512]{2,1,0:T(8,128)(2,1)S(1)} %get-tuple-element.102.theirs, ...), custom_call_target="tpu_custom_call", output_to_operand_aliasing={{0}: (5, {}), {1}: (6, {})} | custom-call | flops 1 | bytes 1 | tf_op jit(solution)/shard_map/pallas_call | solution.py:32
  127.4 1.3 shard_map.91.mine
  128.7 1.1 collective-permute-start.23
  129.8 5.5 %collective-permute-done.20.other = bf16[512,512]{1,0:T(8,128)(2,1)S(1)} collective-permute-done((bf16[512,512]{1,0:T(8,128)(2,1)S(1)}, bf16[512,512]{1,0:T(8,128)(2,1)S(1)}, u32[]{:S(2)}, u32[]{:S(2)}) %collective-permute-start.20) | collective-permute-done | bytes 524320 | tf_op jit(solution)/shard_map/ppermute | solution.py:15
  136.3 3.7 %shard_map.93 = (f32[3584,1024]{1,0:T(8,128)}, f32[3584,1024]{1,0:T(8,128)}) custom-call(bf16[1024,1024]{1,0:T(8,128)(2,1)S(1)} %bitcast.9, bf16[2,256,512]{2,1,0:T(8,128)(2,1)S(1)} %get-tuple-element.110.mine, bf16[2,256,512]{2,1,0:T(8,128)(2,1)S(1)} %get-tuple-element.111.theirs, ...), custom_call_target="tpu_custom_call", output_to_operand_aliasing={{0}: (5, {}), {1}: (6, {})} | custom-call | flops 1 | bytes 1 | tf_op jit(solution)/shard_map/pallas_call | solution.py:32
  141.1 1.6 collective-permute-start.26
  142.7 3.9 %collective-permute-done.23.theirs = bf16[2,256,512]{2,1,0:T(8,128)(2,1)S(1)} collective-permute-done((bf16[2,256,512]{2,1,0:T(8,128)(2,1)S(1)}, bf16[2,256,512]{2,1,0:T(8,128)(2,1)S(1)}, u32[]{:S(2)}, u32[]{:S(2)}) %collective-permute-start.23) | collective-permute-done | bytes 524320 | tf_op jit(solution)/shard_map/ppermute | solution.py:15
  146.6 3.7 %shard_map.95 = (f32[3584,1024]{1,0:T(8,128)}, f32[3584,1024]{1,0:T(8,128)}) custom-call(bf16[1024,1024]{1,0:T(8,128)(2,1)S(1)} %bitcast.10, bf16[2,256,512]{2,1,0:T(8,128)(2,1)S(1)} %get-tuple-element.117.mine, bf16[2,256,512]{2,1,0:T(8,128)(2,1)S(1)} %get-tuple-element.118.theirs, ...), custom_call_target="tpu_custom_call", output_to_operand_aliasing={{0}: (5, {}), {1}: (6, {})} | custom-call | flops 1 | bytes 1 | tf_op jit(solution)/shard_map/pallas_call | solution.py:32
  151.4 1.6 collective-permute-start.29
  152.9 4.9 %collective-permute-done.26.theirs = bf16[2,256,512]{2,1,0:T(8,128)(2,1)S(1)} collective-permute-done((bf16[2,256,512]{2,1,0:T(8,128)(2,1)S(1)}, bf16[2,256,512]{2,1,0:T(8,128)(2,1)S(1)}, u32[]{:S(2)}, u32[]{:S(2)}) %collective-permute-start.26) | collective-permute-done | bytes 524320 | tf_op jit(solution)/shard_map/ppermute | solution.py:15
  157.8 3.7 %shard_map.97 = (f32[3584,1024]{1,0:T(8,128)}, f32[3584,1024]{1,0:T(8,128)}) custom-call(bf16[1024,1024]{1,0:T(8,128)(2,1)S(1)} %bitcast.11, bf16[2,256,512]{2,1,0:T(8,128)(2,1)S(1)} %shard_map.91.mine, bf16[2,256,512]{2,1,0:T(8,128)(2,1)S(1)} %collective-permute-done.23.theirs, ...), custom_call_target="tpu_custom_call", output_to_operand_aliasing={{0}: (5, {}), {1}: (6, {})} | custom-call | flops 1 | bytes 1 | tf_op jit(solution)/shard_map/pallas_call | solution.py:32
  162.0 6.0 %collective-permute-done.29.theirs = bf16[2,256,512]{2,1,0:T(8,128)(2,1)S(1)} collective-permute-done((bf16[2,256,512]{2,1,0:T(8,128)(2,1)S(1)}, bf16[2,256,512]{2,1,0:T(8,128)(2,1)S(1)}, u32[]{:S(2)}, u32[]{:S(2)}) %collective-permute-start.29) | collective-permute-done | bytes 524320 | tf_op jit(solution)/shard_map/ppermute | solution.py:15
  168.6 3.7 %shard_map.98 = (f32[3584,1024]{1,0:T(8,128)}, f32[3584,1024]{1,0:T(8,128)}) custom-call(bf16[1024,1024]{1,0:T(8,128)(2,1)S(1)} %bitcast.12, bf16[2,256,512]{2,1,0:T(8,128)(2,1)S(1)} %shard_map.94.mine, bf16[2,256,512]{2,1,0:T(8,128)(2,1)S(1)} %collective-permute-done.26.theirs, ...), custom_call_target="tpu_custom_call", output_to_operand_aliasing={{0}: (5, {}), {1}: (6, {})} | custom-call | flops 1 | bytes 1 | tf_op jit(solution)/shard_map/pallas_call | solution.py:32
  172.3 3.7 %shard_map.99 = (f32[3584,1024]{1,0:T(8,128)}, f32[3584,1024]{1,0:T(8,128)}) custom-call(bf16[1024,1024]{1,0:T(8,128)(2,1)S(1)} %bitcast.13, bf16[2,256,512]{2,1,0:T(8,128)(2,1)S(1)} %shard_map.96.mine, bf16[2,256,512]{2,1,0:T(8,128)(2,1)S(1)} %collective-permute-done.29.theirs, ...), custom_call_target="tpu_custom_call", output_to_operand_aliasing={{0}: (5, {}), {1}: (6, {})} | custom-call | flops 1 | bytes 1 | tf_op jit(solution)/shard_map/pallas_call | solution.py:32
  (74 shorter events, 14.3 us)
Async XLA Ops:
  0.6 21.0 %collective-permute-start.1 = (bf16[1,128,2048]{2,1,0:T(8,128)(2,1)}, bf16[1,128,2048]{2,1,0:T(8,128)(2,1)}, u32[]{:S(2)}, u32[]{:S(2)}) collective-permute-start(bf16[1,128,2048]{2,1,0:T(8,128)(2,1)} %own.1), channel_id=1, source_target_pairs={{0,12},{12,0},{4,8},{8,4},{1,13},{13,1},{5,9},{9,5},{2,14},{14,2},... | collective-permute-start | bytes 1572872 | tf_op jit(solution)/shard_map/ppermute | solution.py:279
  5.7 23.6 %collective-permute-start = (bf16[1,128,2048]{2,1,0:T(8,128)(2,1)}, bf16[1,128,2048]{2,1,0:T(8,128)(2,1)}, u32[]{:S(2)}, u32[]{:S(2)}) collective-permute-start(bf16[1,128,2048]{2,1,0:T(8,128)(2,1)} %own.1), channel_id=1, source_target_pairs={{0,4},{4,0},{8,12},{12,8},{1,5},{5,1},{9,13},{13,9},{2,6},{6,2},{1... | collective-permute-start | bytes 1572872 | tf_op jit(solution)/shard_map/ppermute | solution.py:278
  7.8 30.7 %collective-permute-start.4 = (bf16[1,256,1536]{2,1,0:T(8,128)(2,1)}, bf16[1,256,1536]{2,1,0:T(8,128)(2,1)S(1)}, u32[]{:S(2)}, u32[]{:S(2)}) collective-permute-start(bf16[1,256,1536]{2,1,0:T(8,128)(2,1)} %slice.6), channel_id=1, source_target_pairs={{0,2},{2,0},{1,3},{3,1},{4,6},{6,4},{5,7},{7,5},{8,10},{10,8},{9,1... | collective-permute-start | bytes 2359304 | tf_op jit(solution)/shard_map/ppermute | solution.py:15
  11.4 32.5 %collective-permute-start.5 = (bf16[1,256,1536]{2,1,0:T(8,128)(2,1)}, bf16[1,256,1536]{2,1,0:T(8,128)(2,1)S(1)}, u32[]{:S(2)}, u32[]{:S(2)}) collective-permute-start(bf16[1,256,1536]{2,1,0:T(8,128)(2,1)} %slice.7), channel_id=1, source_target_pairs={{0,2},{2,0},{1,3},{3,1},{4,6},{6,4},{5,7},{7,5},{8,10},{10,8},{9,1... | collective-permute-start | bytes 2359304 | tf_op jit(solution)/shard_map/ppermute | solution.py:15
  11.9 5.2 %copy-start.2 = (bf16[2048,3584]{1,0:T(8,128)(2,1)S(1)}, bf16[2048,3584]{1,0:T(8,128)(2,1)}, u32[]{:S(2)}) copy-start(bf16[2048,3584]{1,0:T(8,128)(2,1)} %codes.2) | copy-start | bytes 44040196
  17.1 0.7 copy-start.12
  19.6 2.0 %copy-start.7 = (bf16[4,2048,256]{2,1,0:T(8,128)(2,1)}, bf16[4,2048,256]{2,1,0:T(8,128)(2,1)S(1)}, u32[]{:S(2)}) copy-start(bf16[4,2048,256]{2,1,0:T(8,128)(2,1)S(1)} %shard_map.77.weight) | copy-start | bytes 12582916
  21.6 22.3 %collective-permute-start.3 = (bf16[1,128,2048]{2,1,0:T(8,128)(2,1)}, bf16[1,128,2048]{2,1,0:T(8,128)(2,1)}, u32[]{:S(2)}, u32[]{:S(2)}) collective-permute-start(bf16[1,128,2048]{2,1,0:T(8,128)(2,1)} %collective-permute-done.1.across), channel_id=1, source_target_pairs={{4,0},{8,12},{5,1},{9,13},{6,2},{10,14},{7,3},{11,15},{20,16},{24,... | collective-permute-start | bytes 1572872 | tf_op jit(solution)/shard_map/ppermute | solution.py:283
  29.3 14.6 %collective-permute-start.2 = (bf16[1,128,2048]{2,1,0:T(8,128)(2,1)}, bf16[1,128,2048]{2,1,0:T(8,128)(2,1)}, u32[]{:S(2)}, u32[]{:S(2)}) collective-permute-start(bf16[1,128,2048]{2,1,0:T(8,128)(2,1)} %collective-permute-done.buddy), channel_id=1, source_target_pairs={{4,8},{8,4},{5,9},{9,5},{6,10},{10,6},{7,11},{11,7},{20,24},{24,20... | collective-permute-start | bytes 1572872 | tf_op jit(solution)/shard_map/ppermute | solution.py:284
  34.4 4.1 %copy-start.3 = (bf16[10,2048,256]{2,1,0:T(8,128)(2,1)}, bf16[10,2048,256]{2,1,0:T(8,128)(2,1)S(1)}, u32[]{:S(2)}) copy-start(bf16[10,2048,256]{2,1,0:T(8,128)(2,1)S(1)} %shard_map.78.weight) | copy-start | bytes 31457284
  38.5 38.5 %copy-start = (bf16[1,256,3584]{2,1,0:T(8,128)(2,1)S(1)}, bf16[1,256,3584]{2,1,0:T(8,128)(2,1)}, u32[]{:S(2)}) copy-start(bf16[1,256,3584]{2,1,0:T(8,128)(2,1)} %gates.13) | copy-start | bytes 5505028
  43.9 1.0 copy-start.11
  47.2 2.2 %copy-start.8 = (bf16[4,2048,256]{2,1,0:T(8,128)(2,1)S(1)}, bf16[4,2048,256]{2,1,0:T(8,128)(2,1)}, u32[]{:S(2)}) copy-start(bf16[4,2048,256]{2,1,0:T(8,128)(2,1)} %copy-done.7) | copy-start | bytes 12582916
  53.1 1.3 copy-start.5
  54.4 0.8 copy-start.9
  55.2 21.8 %collective-permute-start.6 = (bf16[256,1024]{1,0:T(8,128)(2,1)}, bf16[256,1024]{1,0:T(8,128)(2,1)}, u32[]{:S(2)}, u32[]{:S(2)}) collective-permute-start(bf16[256,1024]{1,0:T(8,128)(2,1)} %get-tuple-element.75), channel_id=1, source_target_pairs={{0,2},{2,0},{1,3},{3,1},{4,6},{6,4},{5,7},{7,5},{8,10},{10,8},{9,1... | collective-permute-start | bytes 1572872 | tf_op jit(solution)/shard_map/ppermute | solution.py:15
  56.7 20.3 %copy-start.1 = (bf16[1,256,3584]{2,1,0:T(8,128)(2,1)S(1)}, bf16[1,256,3584]{2,1,0:T(8,128)(2,1)}, u32[]{:S(2)}) copy-start(bf16[1,256,3584]{2,1,0:T(8,128)(2,1)} %ups.13) | copy-start | bytes 5505028
  57.9 14.4 %collective-permute-start.10 = (bf16[1,128,1024]{2,1,0:T(8,128)(2,1)S(1)}, bf16[1,128,1024]{2,1,0:T(8,128)(2,1)S(1)}, u32[]{:S(2)}, u32[]{:S(2)}) collective-permute-start(bf16[1,128,1024]{2,1,0:T(8,128)(2,1)S(1)} %get-tuple-element.137), channel_id=1, source_target_pairs={{0,1},{1,0},{2,3},{3,2},{4,5},{5,4},{6,7},{7,6},{8,9},{9,8},{10,11... | collective-permute-start | bytes 786440 | tf_op jit(solution)/shard_map/ppermute | solution.py:15
  58.0 4.0 %copy-start.4 = (bf16[10,2048,256]{2,1,0:T(8,128)(2,1)S(1)}, bf16[10,2048,256]{2,1,0:T(8,128)(2,1)}, u32[]{:S(2)}) copy-start(bf16[10,2048,256]{2,1,0:T(8,128)(2,1)} %copy-done.3) | copy-start | bytes 31457284
  62.0 1.6 copy-start.6
  71.7 14.8 %collective-permute-start.7 = (bf16[256,1024]{1,0:T(8,128)(2,1)S(1)}, bf16[256,1024]{1,0:T(8,128)(2,1)S(1)}, u32[]{:S(2)}, u32[]{:S(2)}) collective-permute-start(bf16[256,1024]{1,0:T(8,128)(2,1)S(1)} %get-tuple-element.79), channel_id=1, source_target_pairs={{0,2},{2,0},{1,3},{3,1},{4,6},{6,4},{5,7},{7,5},{8,10},{10,8},{9,1... | collective-permute-start | bytes 1572872 | tf_op jit(solution)/shard_map/ppermute | solution.py:15
  72.4 14.7 %collective-permute-start.11 = (bf16[2,128,1024]{2,1,0:T(8,128)(2,1)S(1)}, bf16[2,128,1024]{2,1,0:T(8,128)(2,1)S(1)}, u32[]{:S(2)}, u32[]{:S(2)}) collective-permute-start(bf16[2,128,1024]{2,1,0:T(8,128)(2,1)S(1)} %pad_maximum_fusion.own), channel_id=1, source_target_pairs={{0,4},{4,0},{8,12},{12,8},{1,5},{5,1},{9,13},{13,9},{2,6},{6,2},{1... | collective-permute-start | bytes 1572872 | tf_op jit(solution)/shard_map/ppermute | solution.py:278
  74.7 25.7 %collective-permute-start.12 = (bf16[2,128,1024]{2,1,0:T(8,128)(2,1)S(1)}, bf16[2,128,1024]{2,1,0:T(8,128)(2,1)S(1)}, u32[]{:S(2)}, u32[]{:S(2)}) collective-permute-start(bf16[2,128,1024]{2,1,0:T(8,128)(2,1)S(1)} %pad_maximum_fusion.own), channel_id=1, source_target_pairs={{0,12},{12,0},{4,8},{8,4},{1,13},{13,1},{5,9},{9,5},{2,14},{14,2},... | collective-permute-start | bytes 1572872 | tf_op jit(solution)/shard_map/ppermute | solution.py:279
  77.0 1.0 copy-start.10
  79.4 22.3 %collective-permute-start.8 = (bf16[2,256,512]{2,1,0:T(8,128)(2,1)S(1)}, bf16[2,256,512]{2,1,0:T(8,128)(2,1)S(1)}, u32[]{:S(2)}, u32[]{:S(2)}) collective-permute-start(bf16[2,256,512]{2,1,0:T(8,128)(2,1)S(1)} %shard_map.82.mine), channel_id=1, source_target_pairs={{0,2},{2,0},{1,3},{3,1},{4,6},{6,4},{5,7},{7,5},{8,10},{10,8},{9,1... | collective-permute-start | bytes 1572872 | tf_op jit(solution)/shard_map/ppermute | solution.py:15
  86.5 22.1 %collective-permute-start.9 = (bf16[512,512]{1,0:T(8,128)(2,1)S(1)}, bf16[512,512]{1,0:T(8,128)(2,1)S(1)}, u32[]{:S(2)}, u32[]{:S(2)}) collective-permute-start(bf16[512,512]{1,0:T(8,128)(2,1)S(1)} %shard_map.83.own), channel_id=1, source_target_pairs={{0,2},{2,0},{1,3},{3,1},{4,6},{6,4},{5,7},{7,5},{8,10},{10,8},{9,1... | collective-permute-start | bytes 1572872 | tf_op jit(solution)/shard_map/ppermute | solution.py:15
  87.0 23.0 %collective-permute-start.13 = (bf16[2,128,1024]{2,1,0:T(8,128)(2,1)S(1)}, bf16[2,128,1024]{2,1,0:T(8,128)(2,1)S(1)}, u32[]{:S(2)}, u32[]{:S(2)}) collective-permute-start(bf16[2,128,1024]{2,1,0:T(8,128)(2,1)S(1)} %collective-permute-done.11.buddy), channel_id=1, source_target_pairs={{4,8},{8,4},{5,9},{9,5},{6,10},{10,6},{7,11},{11,7},{20,24},{24,20... | collective-permute-start | bytes 1572872 | tf_op jit(solution)/shard_map/ppermute | solution.py:284
  100.3 15.0 %collective-permute-start.14 = (bf16[2,128,1024]{2,1,0:T(8,128)(2,1)S(1)}, bf16[2,128,1024]{2,1,0:T(8,128)(2,1)S(1)}, u32[]{:S(2)}, u32[]{:S(2)}) collective-permute-start(bf16[2,128,1024]{2,1,0:T(8,128)(2,1)S(1)} %collective-permute-done.12.across), channel_id=1, source_target_pairs={{4,0},{8,12},{5,1},{9,13},{6,2},{10,14},{7,3},{11,15},{20,16},{24,... | collective-permute-start | bytes 1572872 | tf_op jit(solution)/shard_map/ppermute | solution.py:283
  101.6 14.6 %collective-permute-start.15 = (bf16[2,256,512]{2,1,0:T(8,128)(2,1)S(1)}, bf16[2,256,512]{2,1,0:T(8,128)(2,1)S(1)}, u32[]{:S(2)}, u32[]{:S(2)}) collective-permute-start(bf16[2,256,512]{2,1,0:T(8,128)(2,1)S(1)} %shard_map.82.mine), channel_id=1, source_target_pairs={{0,1},{1,0},{2,3},{3,2},{4,5},{5,4},{6,7},{7,6},{8,9},{9,8},{10,11... | collective-permute-start | bytes 1572872 | tf_op jit(solution)/shard_map/ppermute | solution.py:15
  101.7 14.6 %collective-permute-start.16 = (bf16[2,256,512]{2,1,0:T(8,128)(2,1)S(1)}, bf16[2,256,512]{2,1,0:T(8,128)(2,1)S(1)}, u32[]{:S(2)}, u32[]{:S(2)}) collective-permute-start(bf16[2,256,512]{2,1,0:T(8,128)(2,1)S(1)} %collective-permute-done.8.theirs), channel_id=1, source_target_pairs={{0,1},{1,0},{2,3},{3,2},{4,5},{5,4},{6,7},{7,6},{8,9},{9,8},{10,11... | collective-permute-start | bytes 1572872 | tf_op jit(solution)/shard_map/ppermute | solution.py:15
  108.6 13.5 %collective-permute-start.17 = (bf16[512,512]{1,0:T(8,128)(2,1)S(1)}, bf16[512,512]{1,0:T(8,128)(2,1)S(1)}, u32[]{:S(2)}, u32[]{:S(2)}) collective-permute-start(bf16[512,512]{1,0:T(8,128)(2,1)S(1)} %shard_map.84.own), channel_id=1, source_target_pairs={{0,2},{2,0},{1,3},{3,1},{4,6},{6,4},{5,7},{7,5},{8,10},{10,8},{9,1... | collective-permute-start | bytes 1572872 | tf_op jit(solution)/shard_map/ppermute | solution.py:15
  120.0 3.1 %collective-permute-start.18 = (bf16[2,256,512]{2,1,0:T(8,128)(2,1)S(1)}, bf16[2,256,512]{2,1,0:T(8,128)(2,1)S(1)}, u32[]{:S(2)}, u32[]{:S(2)}) collective-permute-start(bf16[2,256,512]{2,1,0:T(8,128)(2,1)S(1)} %get-tuple-element.101.mine), channel_id=1, source_target_pairs={{0,1},{1,0},{2,3},{3,2},{4,5},{5,4},{6,7},{7,6},{8,9},{9,8},{10,11... | collective-permute-start | bytes 1572872 | tf_op jit(solution)/shard_map/ppermute | solution.py:15
  120.0 3.1 %collective-permute-start.19 = (bf16[2,256,512]{2,1,0:T(8,128)(2,1)S(1)}, bf16[2,256,512]{2,1,0:T(8,128)(2,1)S(1)}, u32[]{:S(2)}, u32[]{:S(2)}) collective-permute-start(bf16[2,256,512]{2,1,0:T(8,128)(2,1)S(1)} %get-tuple-element.102.theirs), channel_id=1, source_target_pairs={{0,1},{1,0},{2,3},{3,2},{4,5},{5,4},{6,7},{7,6},{8,9},{9,8},{10,11... | collective-permute-start | bytes 1572872 | tf_op jit(solution)/shard_map/ppermute | solution.py:15
  120.5 14.8 %collective-permute-start.20 = (bf16[512,512]{1,0:T(8,128)(2,1)S(1)}, bf16[512,512]{1,0:T(8,128)(2,1)S(1)}, u32[]{:S(2)}, u32[]{:S(2)}) collective-permute-start(bf16[512,512]{1,0:T(8,128)(2,1)S(1)} %shard_map.88.own), channel_id=1, source_target_pairs={{0,2},{2,0},{1,3},{3,1},{4,6},{6,4},{5,7},{7,5},{8,10},{10,8},{9,1... | collective-permute-start | bytes 1572872 | tf_op jit(solution)/shard_map/ppermute | solution.py:15
  126.9 9.4 %collective-permute-start.21 = (bf16[2,256,512]{2,1,0:T(8,128)(2,1)S(1)}, bf16[2,256,512]{2,1,0:T(8,128)(2,1)S(1)}, u32[]{:S(2)}, u32[]{:S(2)}) collective-permute-start(bf16[2,256,512]{2,1,0:T(8,128)(2,1)S(1)} %get-tuple-element.110.mine), channel_id=1, source_target_pairs={{0,1},{1,0},{2,3},{3,2},{4,5},{5,4},{6,7},{7,6},{8,9},{9,8},{10,11... | collective-permute-start | bytes 1572872 | tf_op jit(solution)/shard_map/ppermute | solution.py:15
  126.9 9.4 %collective-permute-start.22 = (bf16[2,256,512]{2,1,0:T(8,128)(2,1)S(1)}, bf16[2,256,512]{2,1,0:T(8,128)(2,1)S(1)}, u32[]{:S(2)}, u32[]{:S(2)}) collective-permute-start(bf16[2,256,512]{2,1,0:T(8,128)(2,1)S(1)} %get-tuple-element.111.theirs), channel_id=1, source_target_pairs={{0,1},{1,0},{2,3},{3,2},{4,5},{5,4},{6,7},{7,6},{8,9},{9,8},{10,11... | collective-permute-start | bytes 1572872 | tf_op jit(solution)/shard_map/ppermute | solution.py:15
  128.7 17.8 %collective-permute-start.23 = (bf16[2,256,512]{2,1,0:T(8,128)(2,1)S(1)}, bf16[2,256,512]{2,1,0:T(8,128)(2,1)S(1)}, u32[]{:S(2)}, u32[]{:S(2)}) collective-permute-start(bf16[2,256,512]{2,1,0:T(8,128)(2,1)S(1)} %shard_map.91.mine), channel_id=1, source_target_pairs={{0,2},{2,0},{1,3},{3,1},{4,6},{6,4},{5,7},{7,5},{8,10},{10,8},{9,1... | collective-permute-start | bytes 1572872 | tf_op jit(solution)/shard_map/ppermute | solution.py:15
  140.1 6.5 %collective-permute-start.24 = (bf16[2,256,512]{2,1,0:T(8,128)(2,1)S(1)}, bf16[2,256,512]{2,1,0:T(8,128)(2,1)S(1)}, u32[]{:S(2)}, u32[]{:S(2)}) collective-permute-start(bf16[2,256,512]{2,1,0:T(8,128)(2,1)S(1)} %get-tuple-element.117.mine), channel_id=1, source_target_pairs={{0,1},{1,0},{2,3},{3,2},{4,5},{5,4},{6,7},{7,6},{8,9},{9,8},{10,11... | collective-permute-start | bytes 1572872 | tf_op jit(solution)/shard_map/ppermute | solution.py:15
  140.1 6.5 %collective-permute-start.25 = (bf16[2,256,512]{2,1,0:T(8,128)(2,1)S(1)}, bf16[2,256,512]{2,1,0:T(8,128)(2,1)S(1)}, u32[]{:S(2)}, u32[]{:S(2)}) collective-permute-start(bf16[2,256,512]{2,1,0:T(8,128)(2,1)S(1)} %get-tuple-element.118.theirs), channel_id=1, source_target_pairs={{0,1},{1,0},{2,3},{3,2},{4,5},{5,4},{6,7},{7,6},{8,9},{9,8},{10,11... | collective-permute-start | bytes 1572872 | tf_op jit(solution)/shard_map/ppermute | solution.py:15
  141.1 16.7 %collective-permute-start.26 = (bf16[2,256,512]{2,1,0:T(8,128)(2,1)S(1)}, bf16[2,256,512]{2,1,0:T(8,128)(2,1)S(1)}, u32[]{:S(2)}, u32[]{:S(2)}) collective-permute-start(bf16[2,256,512]{2,1,0:T(8,128)(2,1)S(1)} %shard_map.94.mine), channel_id=1, source_target_pairs={{0,2},{2,0},{1,3},{3,1},{4,6},{6,4},{5,7},{7,5},{8,10},{10,8},{9,1... | collective-permute-start | bytes 1572872 | tf_op jit(solution)/shard_map/ppermute | solution.py:15
  150.3 7.5 %collective-permute-start.27 = (bf16[2,256,512]{2,1,0:T(8,128)(2,1)S(1)}, bf16[2,256,512]{2,1,0:T(8,128)(2,1)S(1)}, u32[]{:S(2)}, u32[]{:S(2)}) collective-permute-start(bf16[2,256,512]{2,1,0:T(8,128)(2,1)S(1)} %shard_map.91.mine), channel_id=1, source_target_pairs={{0,1},{1,0},{2,3},{3,2},{4,5},{5,4},{6,7},{7,6},{8,9},{9,8},{10,11... | collective-permute-start | bytes 1572872 | tf_op jit(solution)/shard_map/ppermute | solution.py:15
  150.3 7.5 %collective-permute-start.28 = (bf16[2,256,512]{2,1,0:T(8,128)(2,1)S(1)}, bf16[2,256,512]{2,1,0:T(8,128)(2,1)S(1)}, u32[]{:S(2)}, u32[]{:S(2)}) collective-permute-start(bf16[2,256,512]{2,1,0:T(8,128)(2,1)S(1)} %collective-permute-done.23.theirs), channel_id=1, source_target_pairs={{0,1},{1,0},{2,3},{3,2},{4,5},{5,4},{6,7},{7,6},{8,9},{9,8},{10,11... | collective-permute-start | bytes 1572872 | tf_op jit(solution)/shard_map/ppermute | solution.py:15
  151.4 16.7 %collective-permute-start.29 = (bf16[2,256,512]{2,1,0:T(8,128)(2,1)S(1)}, bf16[2,256,512]{2,1,0:T(8,128)(2,1)S(1)}, u32[]{:S(2)}, u32[]{:S(2)}) collective-permute-start(bf16[2,256,512]{2,1,0:T(8,128)(2,1)S(1)} %shard_map.96.mine), channel_id=1, source_target_pairs={{0,2},{2,0},{1,3},{3,1},{4,6},{6,4},{5,7},{7,5},{8,10},{10,8},{9,1... | collective-permute-start | bytes 1572872 | tf_op jit(solution)/shard_map/ppermute | solution.py:15
  161.5 7.1 %collective-permute-start.30 = (bf16[2,256,512]{2,1,0:T(8,128)(2,1)S(1)}, bf16[2,256,512]{2,1,0:T(8,128)(2,1)S(1)}, u32[]{:S(2)}, u32[]{:S(2)}) collective-permute-start(bf16[2,256,512]{2,1,0:T(8,128)(2,1)S(1)} %shard_map.94.mine), channel_id=1, source_target_pairs={{0,1},{1,0},{2,3},{3,2},{4,5},{5,4},{6,7},{7,6},{8,9},{9,8},{10,11... | collective-permute-start | bytes 1572872 | tf_op jit(solution)/shard_map/ppermute | solution.py:15
  161.5 7.1 %collective-permute-start.31 = (bf16[2,256,512]{2,1,0:T(8,128)(2,1)S(1)}, bf16[2,256,512]{2,1,0:T(8,128)(2,1)S(1)}, u32[]{:S(2)}, u32[]{:S(2)}) collective-permute-start(bf16[2,256,512]{2,1,0:T(8,128)(2,1)S(1)} %collective-permute-done.26.theirs), channel_id=1, source_target_pairs={{0,1},{1,0},{2,3},{3,2},{4,5},{5,4},{6,7},{7,6},{8,9},{9,8},{10,11... | collective-permute-start | bytes 1572872 | tf_op jit(solution)/shard_map/ppermute | solution.py:15
  168.1 4.3 %collective-permute-start.32 = (bf16[2,256,512]{2,1,0:T(8,128)(2,1)S(1)}, bf16[2,256,512]{2,1,0:T(8,128)(2,1)S(1)}, u32[]{:S(2)}, u32[]{:S(2)}) collective-permute-start(bf16[2,256,512]{2,1,0:T(8,128)(2,1)S(1)} %shard_map.96.mine), channel_id=1, source_target_pairs={{0,1},{1,0},{2,3},{3,2},{4,5},{5,4},{6,7},{7,6},{8,9},{9,8},{10,11... | collective-permute-start | bytes 1572872 | tf_op jit(solution)/shard_map/ppermute | solution.py:15
  168.1 4.3 %collective-permute-start.33 = (bf16[2,256,512]{2,1,0:T(8,128)(2,1)S(1)}, bf16[2,256,512]{2,1,0:T(8,128)(2,1)S(1)}, u32[]{:S(2)}, u32[]{:S(2)}) collective-permute-start(bf16[2,256,512]{2,1,0:T(8,128)(2,1)S(1)} %collective-permute-done.29.theirs), channel_id=1, source_target_pairs={{0,1},{1,0},{2,3},{3,2},{4,5},{5,4},{6,7},{7,6},{8,9},{9,8},{10,11... | collective-permute-start | bytes 1572872 | tf_op jit(solution)/shard_map/ppermute | solution.py:15

commit v3 on v2

--- a/solution.py
+++ b/solution.py
@@ -7,7 +7,7 @@
 from jax.experimental.pallas import tpu as pltpu
 from jax.sharding import PartitionSpec as P
 
-VMEM_LIMIT = 24 * 1024 * 1024
+VMEM_LIMIT = 40 * 1024 * 1024
 LANES = 256
 
 
@@ -45,34 +45,6 @@
     )(*operands)
 
 
-def scale_kernel(block_side, first_block, codes, scales, weight):
-    feature_rows, lanes = codes.shape
-    base = first_block + pl.program_id(0) * (lanes // block_side)
-    for i in range(feature_rows // block_side):
-        for j in range(lanes // block_side):
-            rows = slice(i * block_side, (i + 1) * block_side)
-            cols = slice(j * block_side, (j + 1) * block_side)
-            scaled = codes[rows, cols].astype(jnp.float32) * scales[i, base + j]
-            weight[0, rows, cols] = scaled.astype(jnp.bfloat16)
-
-
-def scaled_weight(codes, scales, start, width):
-    features = codes.shape[0]
-    block_side = features // scales.shape[0]
-    offset = start // LANES
-    return call(
-        functools.partial(scale_kernel, block_side, start // block_side),
-        (width // LANES,),
-        [
-            pl.BlockSpec((features, LANES), lambda i: (0, offset + i)),
-            pl.BlockSpec(memory_space=pltpu.SMEM),
-        ],
-        pl.BlockSpec((1, features, LANES), lambda i: (i, 0, 0)),
-        jax.ShapeDtypeStruct((width // LANES, features, LANES), jnp.bfloat16),
-        [codes, scales],
-    )
-
-
 def arrange_kernel(places, own, buddy, across, middle, outward, out):
     for k, shard in enumerate((own, buddy, across)):
         out[:, pl.ds(places[k], 1)] = shard[...][:, None]
@@ -100,9 +72,18 @@
     )
 
 
-def partial_kernel(parts, grads, weight, *outs):
+def partial_kernel(parts, block_side, first_block, grads, codes, scales, *refs):
+    weight, outs = refs[-1], refs[:-1]
     step = pl.program_id(0)
-    product = jnp.dot(grads[...], weight[0], preferred_element_type=jnp.float32)
+    features, lanes = codes.shape
+    base = first_block + step * (lanes // block_side)
+    for i in range(features // block_side):
+        for j in range(lanes // block_side):
+            rows = slice(i * block_side, (i + 1) * block_side)
+            cols = slice(j * block_side, (j + 1) * block_side)
+            scaled = codes[rows, cols].astype(jnp.float32) * scales[i, base + j]
+            weight[rows, cols] = scaled.astype(jnp.bfloat16)
+    product = jnp.dot(grads[...], weight[...], preferred_element_type=jnp.float32)
     product = product.astype(jnp.bfloat16)
     first = 0
     for count, split in parts:
@@ -117,8 +98,10 @@
         first += count
 
 
-def partial_products(grads, weight, parts):
+def partial_products(grads, codes, scales, start, parts):
     tokens, features = grads.shape
+    block_side = features // scales.shape[0]
+    offset = start // LANES
     outs, out_specs, first = [], [], 0
     for count, split in parts:
         rows = tokens // (1 + split)
@@ -130,15 +113,17 @@
         out_specs += [pl.BlockSpec((rows, LANES), place)] * (1 + split)
         first += count
     return call(
-        functools.partial(partial_kernel, parts),
+        functools.partial(partial_kernel, parts, block_side, start // block_side),
         (first,),
         [
             pl.BlockSpec((tokens, features), lambda i: (0, 0)),
-            pl.BlockSpec((1, features, LANES), lambda i: (i, 0, 0)),
+            pl.BlockSpec((features, LANES), lambda i: (0, offset + i)),
+            pl.BlockSpec(memory_space=pltpu.SMEM),
         ],
         out_specs,
         outs,
-        [grads, weight],
+        [grads, codes, scales],
+        scratch=[pltpu.VMEM((features, LANES), jnp.bfloat16)],
     )
 
 
@@ -279,30 +264,29 @@
         across = lax.ppermute(shard, "row", [(0, 3), (3, 0), (1, 2), (2, 1)])
         return buddy, across
 
-    def gather_far(buddy, across):
-        outward = lax.ppermute(across, "row", [(1, 0), (2, 3)])
-        middle = lax.ppermute(buddy, "row", [(1, 2), (2, 1)])
-        return middle, outward
+    def send_outward(across):
+        return lax.ppermute(across, "row", [(1, 0), (2, 3)])
+
+    def send_middle(buddy):
+        return lax.ppermute(buddy, "row", [(1, 2), (2, 1)])
 
     is_inner = jnp.logical_or(row == 1, row == 2).astype(jnp.int32)
     shards = [row, row ^ 1, 3 - row, (3 - row) ^ 1]
     places = jnp.stack([*(lax.rem(s + 4 - 2 * col, 4) for s in shards), is_inner])
     places = places.astype(jnp.int32)
 
-    near = gather_near(out_grad)
-    lead = 2 * unit
-    first_weight = scaled_weight(down_codes, down_scales, 0, lead)
-    chain.done(first_weight)
-    far = gather_far(*(chain(part) for part in near))
-    weight = scaled_weight(chain(down_codes), down_scales, lead, hidden - lead)
-    chain.done(weight)
+    buddy, across = gather_near(out_grad)
+    middle = send_middle(buddy)
+    across = lax.optimization_barrier((across, buddy))[0]
+    outward = send_outward(across)
 
     keep = lax.dynamic_slice_in_dim(layer_input, depth * half_features, half_features, 2)
     send = lax.dynamic_slice_in_dim(layer_input, (1 - depth) * half_features, half_features, 2)
     both = jnp.concatenate([keep, swap_neighbours(send, "depth")], axis=0)
-
-    outward = lax.optimization_barrier((far[1], other_gates, other_ups))[0]
-    grads = arranged(chain(places), [out_grad, *near, far[0], outward])
+    across = lax.optimization_barrier((across, both))[0]
+
+    outward = lax.optimization_barrier((outward, other_gates, other_ups))[0]
+    grads = arranged(chain(places), [out_grad, buddy, across, middle, outward])
     chain.done(grads)
     grads = grads.reshape(4 * shard_tokens, features)
 
@@ -345,20 +329,26 @@
         return outs
 
     outs = None
-    kept, sent = partial_products(chain(grads), first_weight, [(2 * blocks, True)])
+    kept, sent = partial_products(
+        chain(grads), down_codes, down_scales, 0, [(2 * blocks, True)]
+    )
     chain.done(sent)
     send_step(["p0", "p1"], kept, sent)
-    kept, sent, *rest = partial_products(
-        chain(grads), weight, [(2 * blocks, True)] + [(blocks, False)] * 3
+    input_near = gather_near(chain(both))
+    kept, sent = partial_products(
+        chain(grads), down_codes, down_scales, 2 * unit, [(2 * blocks, True)]
     )
     chain.done(sent)
     send_step(["p2", "p3"], kept, sent)
+    rest = partial_products(
+        chain(grads), down_codes, down_scales, shared, [(blocks, False)] * 3
+    )
+    chain.done(rest[0])
     shared_parts = {f"s{k}": part for k, part in enumerate(rest)}
-    input_near = gather_near(chain(both))
     activation_step("p0")
+    input_far = send_middle(chain(input_near[0])), send_outward(chain(input_near[1]))
     chain.wait(other_part["p2"])
     touch_step("s0")
-    input_far = gather_far(*(chain(part) for part in input_near))
     far_step("p0")
     chain.wait(theirs["p0"])
     touch_step("s1")

time: 177 us -> 164 us (0.927)
  local copies, waits for them, and re-layouts: 29.4 us -> 7.72 us
  waiting for transfers between devices: 62 us -> 68.6 us
  starting transfers between devices: 30.5 us -> 33 us
    unnamed x26 -> x8, local copies, waits for them, and re-layouts: 23.9 us -> 1.75 us
    ppermute x26, waiting for transfers between devices: 37.7 us -> 47.2 us  [swap_neighbours(): lax.ppermute(value, axis, [(i, i ^ 1) for i in range(lax.axis_size(axis))])]
    ppermute x4, waiting for transfers between devices: 5.32 us -> 0.01 us  [the longest x2 0.01 us: send_outward(): return lax.ppermute(across, 'row', [(1, 0), (2, 3)])]
    ppermute x2, waiting for transfers between devices: 12.6 us -> 17.4 us  [gather_near(): across = lax.ppermute(shard, 'row', [(0, 3), (3, 0), (1, 2), (2, 1)])]
    ppermute x2, starting transfers between devices: 2.32 us -> 6.83 us  [gather_near(): buddy = lax.ppermute(shard, 'row', [(0, 1), (1, 0), (2, 3), (3, 2)])]
    ppermute x2, starting transfers between devices: 7.41 us -> 3.82 us  [gather_near(): across = lax.ppermute(shard, 'row', [(0, 3), (3, 0), (1, 2), (2, 1)])]
    ppermute x2, waiting for transfers between devices: 6.4 us -> 4.02 us  [gather_near(): buddy = lax.ppermute(shard, 'row', [(0, 1), (1, 0), (2, 3), (3, 2)])]
    pallas_call x23 -> x22, Pallas kernels: 53.2 us -> 51.6 us  [call(): pl.pallas_call(kernel, grid_spec=pltpu.PrefetchScalarGridSpec(num_scalar_...]
  transfers between devices with their start and end apart: 34 -> 34, of which waited for: 11 -> 13; matrix products, arithmetic and copies ran while one was open for 3% -> 4% of each run, Pallas kernels for 25% -> 25%
where the time goes in v3:
time: 164 us; the launch traced here: 163 us
  waiting for transfers between devices  68.6 us (42%)
  Pallas kernels  51.6 us (31%)
  starting transfers between devices  33 us (20%)
  local copies, waits for them, and re-layouts  7.72 us (5%)
    pallas_call x22, Pallas kernels, call(): pl.pallas_call(kernel, grid_spec=pltpu.PrefetchScalarGridSpec(num_scalar_...  51.6 us
    ppermute x26, waiting for transfers between devices, swap_neighbours(): lax.ppermute(value, axis, [(i, i ^ 1) for i in range(lax.axis_size(axis))])  47.2 us
    ppermute x26, starting transfers between devices, swap_neighbours(): lax.ppermute(value, axis, [(i, i ^ 1) for i in range(lax.axis_size(axis))])  17.6 us
    ppermute x2, waiting for transfers between devices, gather_near(): across = lax.ppermute(shard, 'row', [(0, 3), (3, 0), (1, 2), (2, 1)])  17.4 us
    ppermute x2, starting transfers between devices, gather_near(): buddy = lax.ppermute(shard, 'row', [(0, 1), (1, 0), (2, 3), (3, 2)])  6.83 us
    ppermute x2, waiting for transfers between devices, gather_near(): buddy = lax.ppermute(shard, 'row', [(0, 1), (1, 0), (2, 3), (3, 2)])  4.02 us
    ppermute x2, starting transfers between devices, gather_near(): across = lax.ppermute(shard, 'row', [(0, 3), (3, 0), (1, 2), (2, 1)])  3.82 us
  transfers between devices with their start and end apart: 34, of which 13 were waited for; matrix products, arithmetic and copies ran while one was open for 4% of the time, Pallas kernels for 25%

profile of v3, /device:TPU:0, one launch (start us, length us, event | category | flops | bytes accessed | tf_op | source)
XLA Modules:
  0.0 162.9 jit_solution(16293891238892047353)
XLA Ops:
  0.6 3.1 %collective-permute-start = (bf16[1,128,2048]{2,1,0:T(8,128)(2,1)}, bf16[1,128,2048]{2,1,0:T(8,128)(2,1)S(1)}, u32[]{:S(2)}, u32[]{:S(2)}) collective-permute-start(bf16[1,128,2048]{2,1,0:T(8,128)(2,1)} %own.1), channel_id=1, source_target_pairs={{0,4},{4,0},{8,12},{12,8},{1,5},{5,1},{9,13},{13,9},{2,6},{6,2},{1... | collective-permute-start | bytes 1572872 | tf_op jit(solution)/shard_map/ppermute | solution.py:263
  3.7 2.5 %collective-permute-start.1 = (bf16[1,128,2048]{2,1,0:T(8,128)(2,1)}, bf16[1,128,2048]{2,1,0:T(8,128)(2,1)S(1)}, u32[]{:S(2)}, u32[]{:S(2)}) collective-permute-start(bf16[1,128,2048]{2,1,0:T(8,128)(2,1)} %own.1), channel_id=1, source_target_pairs={{0,12},{12,0},{4,8},{8,4},{1,13},{13,1},{5,9},{9,5},{2,14},{14,2},... | collective-permute-start | bytes 1572872 | tf_op jit(solution)/shard_map/ppermute | solution.py:264
  6.2 2.1 %slice.6 = bf16[1,256,1536]{2,1,0:T(8,128)(2,1)} slice(bf16[1,256,3584]{2,1,0:T(8,128)(2,1)} %gates.13), slice={[0:1], [0:256], [2048:3584]} | slice | bytes 1572864 | tf_op jit(solution)/shard_map/slice | solution.py:259
  8.3 1.5 collective-permute-start.5
  9.7 2.1 %slice.7 = bf16[1,256,1536]{2,1,0:T(8,128)(2,1)} slice(bf16[1,256,3584]{2,1,0:T(8,128)(2,1)} %ups.13), slice={[0:1], [0:256], [2048:3584]} | slice | bytes 1572864 | tf_op jit(solution)/shard_map/slice | solution.py:260
  12.3 4.0 %collective-permute-done.buddy = bf16[1,128,2048]{2,1,0:T(8,128)(2,1)S(1)} collective-permute-done((bf16[1,128,2048]{2,1,0:T(8,128)(2,1)}, bf16[1,128,2048]{2,1,0:T(8,128)(2,1)S(1)}, u32[]{:S(2)}, u32[]{:S(2)}) %collective-permute-start) | collective-permute-done | bytes 524320 | tf_op jit(solution)/shard_map/ppermute | solution.py:263
  16.4 13.0 %collective-permute-done.1.across = bf16[1,128,2048]{2,1,0:T(8,128)(2,1)S(1)} collective-permute-done((bf16[1,128,2048]{2,1,0:T(8,128)(2,1)}, bf16[1,128,2048]{2,1,0:T(8,128)(2,1)S(1)}, u32[]{:S(2)}, u32[]{:S(2)}) %collective-permute-start.1) | collective-permute-done | bytes 524320 | tf_op jit(solution)/shard_map/ppermute | solution.py:264
  29.4 1.3 collective-permute-start.4
  30.7 1.5 collective-permute-start.3
  32.1 1.8 %constant_dynamic-slice_fusion.1 = (bf16[1,128,1024]{2,1,0:T(8,128)(2,1)S(1)}, bf16[1,128,1024]{2,1,0:T(8,128)(2,1)}) fusion(bf16[1,128,2048]{2,1,0:T(8,128)(2,1)} %param.6, s32[]{:T(128)S(6)} %select_n.6, s32[]{:T(128)S(6)} %select_n.7), kind=kLoop, calls=%fused_computation.2 | loop fusion | bytes 1048584 | tf_op jit(solution)/shard_map/dynamic_slice | solution.py:283
  34.0 1.8 %collective-permute-done.2 = bf16[1,128,1024]{2,1,0:T(8,128)(2,1)} collective-permute-done((bf16[1,128,1024]{2,1,0:T(8,128)(2,1)}, bf16[1,128,1024]{2,1,0:T(8,128)(2,1)}, u32[]{:S(2)}, u32[]{:S(2)}) %collective-permute-start.2) | collective-permute-done | bytes 262176 | tf_op jit(solution)/shard_map/ppermute | solution.py:15
  35.8 1.0 pad_maximum_fusion.own
  36.8 7.2 %collective-permute-done.6.other_ups = bf16[1,256,1536]{2,1,0:T(8,128)(2,1)S(1)} collective-permute-done((bf16[1,256,1536]{2,1,0:T(8,128)(2,1)}, bf16[1,256,1536]{2,1,0:T(8,128)(2,1)S(1)}, u32[]{:S(2)}, u32[]{:S(2)}) %collective-permute-start.6) | collective-permute-done | bytes 786464 | tf_op jit(solution)/shard_map/ppermute | solution.py:15
  44.1 1.0 copy-done.2
  45.1 1.7 %shard_map.77 = bf16[1,4,128,2048]{3,2,1,0:T(8,128)(2,1)S(1)} custom-call(s32[5]{0:T(128)S(1)} %stack.27.places, bf16[1,128,2048]{2,1,0:T(8,128)(2,1)S(1)} %copy-done.2, bf16[1,128,2048]{2,1,0:T(8,128)(2,1)S(1)} %collective-permute-done.buddy, bf16[1,128,2048]{2,1,0:T(8,128)(2,1)S(1)} %collective-permute-done.1.across, ...), custom_call_target="tpu_custom_call" | custom-call | flops 1 | bytes 1 | tf_op jit(solution)/shard_map/pallas_call | solution.py:32
  47.5 5.2 %shard_map.78 = (bf16[256,1024]{1,0:T(8,128)(2,1)S(1)}, bf16[256,1024]{1,0:T(8,128)(2,1)S(1)}) custom-call(bf16[512,2048]{1,0:T(8,128)(2,1)S(1)} %bitcast.14, bf16[2048,3584]{1,0:T(8,128)(2,1)} %codes.5, f32[16,28]{1,0:T(8,128)S(1)} %copy-done.3), custom_call_target="tpu_custom_call" | custom-call | flops 1 | bytes 1 | tf_op jit(solution)/shard_map/pallas_call | solution.py:32
  52.7 1.6 collective-permute-start.7
  54.3 5.2 %shard_map.79 = (bf16[256,1024]{1,0:T(8,128)(2,1)S(1)}, bf16[256,1024]{1,0:T(8,128)(2,1)S(1)}) custom-call(bf16[512,2048]{1,0:T(8,128)(2,1)S(1)} %bitcast.15, bf16[2048,3584]{1,0:T(8,128)(2,1)} %codes.5, f32[16,28]{1,0:T(8,128)S(1)} %copy-done.3), custom_call_target="tpu_custom_call" | custom-call | flops 1 | bytes 1 | tf_op jit(solution)/shard_map/pallas_call | solution.py:32
  59.5 0.9 collective-permute-start.8
  60.4 3.7 %collective-permute-start.11 = (bf16[2,128,1024]{2,1,0:T(8,128)(2,1)S(1)}, bf16[2,128,1024]{2,1,0:T(8,128)(2,1)S(1)}, u32[]{:S(2)}, u32[]{:S(2)}) collective-permute-start(bf16[2,128,1024]{2,1,0:T(8,128)(2,1)S(1)} %pad_maximum_fusion.own), channel_id=1, source_target_pairs={{0,4},{4,0},{8,12},{12,8},{1,5},{5,1},{9,13},{13,9},{2,6},{6,2},{1... | collective-permute-start | bytes 1572872 | tf_op jit(solution)/shard_map/ppermute | solution.py:263
  64.1 1.3 collective-permute-start.12
  65.5 7.5 %shard_map.80 = (bf16[512,512]{1,0:T(8,128)(2,1)S(1)}, bf16[512,512]{1,0:T(8,128)(2,1)S(1)}, bf16[512,512]{1,0:T(8,128)(2,1)S(1)}) custom-call(bf16[512,2048]{1,0:T(8,128)(2,1)S(1)} %bitcast.16, bf16[2048,3584]{1,0:T(8,128)(2,1)} %codes.5, f32[16,28]{1,0:T(8,128)S(1)} %copy-done.3), custom_call_target="tpu_custom_call" | custom-call | flops 1 | bytes 1 | tf_op jit(solution)/shard_map/pallas_call | solution.py:32
  73.5 1.3 collective-permute-start.9
  74.8 4.1 %collective-permute-done.8.other = bf16[256,1024]{1,0:T(8,128)(2,1)S(1)} collective-permute-done((bf16[256,1024]{1,0:T(8,128)(2,1)S(1)}, bf16[256,1024]{1,0:T(8,128)(2,1)S(1)}, u32[]{:S(2)}, u32[]{:S(2)}) %collective-permute-start.8) | collective-permute-done | bytes 524320 | tf_op jit(solution)/shard_map/ppermute | solution.py:15
  78.9 1.5 collective-permute-start.10
  81.1 4.4 %collective-permute-done.12.across = bf16[2,128,1024]{2,1,0:T(8,128)(2,1)S(1)} collective-permute-done((bf16[2,128,1024]{2,1,0:T(8,128)(2,1)S(1)}, bf16[2,128,1024]{2,1,0:T(8,128)(2,1)S(1)}, u32[]{:S(2)}, u32[]{:S(2)}) %collective-permute-start.12) | collective-permute-done | bytes 524320 | tf_op jit(solution)/shard_map/ppermute | solution.py:264
  85.5 1.3 collective-permute-start.14
  86.9 3.3 %collective-permute-done.9.theirs = bf16[2,256,512]{2,1,0:T(8,128)(2,1)S(1)} collective-permute-done((bf16[2,256,512]{2,1,0:T(8,128)(2,1)S(1)}, bf16[2,256,512]{2,1,0:T(8,128)(2,1)S(1)}, u32[]{:S(2)}, u32[]{:S(2)}) %collective-permute-start.9) | collective-permute-done | bytes 524320 | tf_op jit(solution)/shard_map/ppermute | solution.py:15
  90.1 8.5 %collective-permute-done.10.other = bf16[512,512]{1,0:T(8,128)(2,1)S(1)} collective-permute-done((bf16[512,512]{1,0:T(8,128)(2,1)S(1)}, bf16[512,512]{1,0:T(8,128)(2,1)S(1)}, u32[]{:S(2)}, u32[]{:S(2)}) %collective-permute-start.10) | collective-permute-done | bytes 524320 | tf_op jit(solution)/shard_map/ppermute | solution.py:15
  98.7 1.5 collective-permute-start.17
  100.2 0.9 shard_map.84
  102.1 3.7 %shard_map.86 = (f32[3584,1024]{1,0:T(8,128)}, f32[3584,1024]{1,0:T(8,128)}) custom-call(bf16[1024,1024]{1,0:T(8,128)(2,1)S(1)} %bitcast.7, bf16[2,256,512]{2,1,0:T(8,128)(2,1)S(1)} %shard_map.81.mine, bf16[2,256,512]{2,1,0:T(8,128)(2,1)S(1)} %collective-permute-done.9.theirs, bf16[2,256,512]{2,1,0:T(8,128)(2,1)S(1)} %collective-permute-done.15.mine_far, ...), custom_call_target="tpu_custom_call" | custom-call | flops 1 | bytes 1 | tf_op jit(solution)/shard_map/pallas_call | solution.py:32
  106.8 4.1 %collective-permute-done.17.other = bf16[512,512]{1,0:T(8,128)(2,1)S(1)} collective-permute-done((bf16[512,512]{1,0:T(8,128)(2,1)S(1)}, bf16[512,512]{1,0:T(8,128)(2,1)S(1)}, u32[]{:S(2)}, u32[]{:S(2)}) %collective-permute-start.17) | collective-permute-done | bytes 524320 | tf_op jit(solution)/shard_map/ppermute | solution.py:15
  110.9 1.0 shard_map.88
  111.9 3.7 %shard_map.89 = (f32[3584,1024]{1,0:T(8,128)}, f32[3584,1024]{1,0:T(8,128)}) custom-call(bf16[1024,1024]{1,0:T(8,128)(2,1)S(1)} %bitcast.8, bf16[2,256,512]{2,1,0:T(8,128)(2,1)S(1)} %get-tuple-element.99.mine, bf16[2,256,512]{2,1,0:T(8,128)(2,1)S(1)} %get-tuple-element.100.theirs, ...), custom_call_target="tpu_custom_call", output_to_operand_aliasing={{0}: (5, {}), {1}: (6, {})} | custom-call | flops 1 | bytes 1 | tf_op jit(solution)/shard_map/pallas_call | solution.py:32
  116.7 2.5 %collective-permute-start.23 = (bf16[2,256,512]{2,1,0:T(8,128)(2,1)S(1)}, bf16[2,256,512]{2,1,0:T(8,128)(2,1)S(1)}, u32[]{:S(2)}, u32[]{:S(2)}) collective-permute-start(bf16[2,256,512]{2,1,0:T(8,128)(2,1)S(1)} %shard_map.90.mine), channel_id=1, source_target_pairs={{0,2},{2,0},{1,3},{3,1},{4,6},{6,4},{5,7},{7,5},{8,10},{10,8},{9,1... | collective-permute-start | bytes 1572872 | tf_op jit(solution)/shard_map/ppermute | solution.py:15
  119.2 2.9 %collective-permute-done.20.other = bf16[512,512]{1,0:T(8,128)(2,1)S(1)} collective-permute-done((bf16[512,512]{1,0:T(8,128)(2,1)S(1)}, bf16[512,512]{1,0:T(8,128)(2,1)S(1)}, u32[]{:S(2)}, u32[]{:S(2)}) %collective-permute-start.20) | collective-permute-done | bytes 524320 | tf_op jit(solution)/shard_map/ppermute | solution.py:15
  122.2 1.0 shard_map.91
  123.1 3.7 %shard_map.92 = (f32[3584,1024]{1,0:T(8,128)}, f32[3584,1024]{1,0:T(8,128)}) custom-call(bf16[1024,1024]{1,0:T(8,128)(2,1)S(1)} %bitcast.9, bf16[2,256,512]{2,1,0:T(8,128)(2,1)S(1)} %get-tuple-element.108.mine, bf16[2,256,512]{2,1,0:T(8,128)(2,1)S(1)} %get-tuple-element.109.theirs, ...), custom_call_target="tpu_custom_call", output_to_operand_aliasing={{0}: (5, {}), {1}: (6, {})} | custom-call | flops 1 | bytes 1 | tf_op jit(solution)/shard_map/pallas_call | solution.py:32
  128.0 1.4 collective-permute-start.26
  129.3 4.1 %collective-permute-done.23.theirs = bf16[2,256,512]{2,1,0:T(8,128)(2,1)S(1)} collective-permute-done((bf16[2,256,512]{2,1,0:T(8,128)(2,1)S(1)}, bf16[2,256,512]{2,1,0:T(8,128)(2,1)S(1)}, u32[]{:S(2)}, u32[]{:S(2)}) %collective-permute-start.23) | collective-permute-done | bytes 524320 | tf_op jit(solution)/shard_map/ppermute | solution.py:15
  133.4 3.7 %shard_map.94 = (f32[3584,1024]{1,0:T(8,128)}, f32[3584,1024]{1,0:T(8,128)}) custom-call(bf16[1024,1024]{1,0:T(8,128)(2,1)S(1)} %bitcast.10, bf16[2,256,512]{2,1,0:T(8,128)(2,1)S(1)} %get-tuple-element.115.mine, bf16[2,256,512]{2,1,0:T(8,128)(2,1)S(1)} %get-tuple-element.116.theirs, ...), custom_call_target="tpu_custom_call", output_to_operand_aliasing={{0}: (5, {}), {1}: (6, {})} | custom-call | flops 1 | bytes 1 | tf_op jit(solution)/shard_map/pallas_call | solution.py:32
  138.2 1.4 collective-permute-start.29
  139.6 5.1 %collective-permute-done.26.theirs = bf16[2,256,512]{2,1,0:T(8,128)(2,1)S(1)} collective-permute-done((bf16[2,256,512]{2,1,0:T(8,128)(2,1)S(1)}, bf16[2,256,512]{2,1,0:T(8,128)(2,1)S(1)}, u32[]{:S(2)}, u32[]{:S(2)}) %collective-permute-start.26) | collective-permute-done | bytes 524320 | tf_op jit(solution)/shard_map/ppermute | solution.py:15
  144.6 3.7 %shard_map.96 = (f32[3584,1024]{1,0:T(8,128)}, f32[3584,1024]{1,0:T(8,128)}) custom-call(bf16[1024,1024]{1,0:T(8,128)(2,1)S(1)} %bitcast.11, bf16[2,256,512]{2,1,0:T(8,128)(2,1)S(1)} %shard_map.90.mine, bf16[2,256,512]{2,1,0:T(8,128)(2,1)S(1)} %collective-permute-done.23.theirs, ...), custom_call_target="tpu_custom_call", output_to_operand_aliasing={{0}: (5, {}), {1}: (6, {})} | custom-call | flops 1 | bytes 1 | tf_op jit(solution)/shard_map/pallas_call | solution.py:32
  148.9 6.0 %collective-permute-done.29.theirs = bf16[2,256,512]{2,1,0:T(8,128)(2,1)S(1)} collective-permute-done((bf16[2,256,512]{2,1,0:T(8,128)(2,1)S(1)}, bf16[2,256,512]{2,1,0:T(8,128)(2,1)S(1)}, u32[]{:S(2)}, u32[]{:S(2)}) %collective-permute-start.29) | collective-permute-done | bytes 524320 | tf_op jit(solution)/shard_map/ppermute | solution.py:15
  155.4 3.7 %shard_map.97 = (f32[3584,1024]{1,0:T(8,128)}, f32[3584,1024]{1,0:T(8,128)}) custom-call(bf16[1024,1024]{1,0:T(8,128)(2,1)S(1)} %bitcast.12, bf16[2,256,512]{2,1,0:T(8,128)(2,1)S(1)} %shard_map.93.mine, bf16[2,256,512]{2,1,0:T(8,128)(2,1)S(1)} %collective-permute-done.26.theirs, ...), custom_call_target="tpu_custom_call", output_to_operand_aliasing={{0}: (5, {}), {1}: (6, {})} | custom-call | flops 1 | bytes 1 | tf_op jit(solution)/shard_map/pallas_call | solution.py:32
  159.1 3.7 %shard_map.98 = (f32[3584,1024]{1,0:T(8,128)}, f32[3584,1024]{1,0:T(8,128)}) custom-call(bf16[1024,1024]{1,0:T(8,128)(2,1)S(1)} %bitcast.13, bf16[2,256,512]{2,1,0:T(8,128)(2,1)S(1)} %shard_map.95.mine, bf16[2,256,512]{2,1,0:T(8,128)(2,1)S(1)} %collective-permute-done.29.theirs, ...), custom_call_target="tpu_custom_call", output_to_operand_aliasing={{0}: (5, {}), {1}: (6, {})} | custom-call | flops 1 | bytes 1 | tf_op jit(solution)/shard_map/pallas_call | solution.py:32
  (55 shorter events, 8.8 us)
Async XLA Ops:
  0.6 15.7 %collective-permute-start = (bf16[1,128,2048]{2,1,0:T(8,128)(2,1)}, bf16[1,128,2048]{2,1,0:T(8,128)(2,1)S(1)}, u32[]{:S(2)}, u32[]{:S(2)}) collective-permute-start(bf16[1,128,2048]{2,1,0:T(8,128)(2,1)} %own.1), channel_id=1, source_target_pairs={{0,4},{4,0},{8,12},{12,8},{1,5},{5,1},{9,13},{13,9},{2,6},{6,2},{1... | collective-permute-start | bytes 1572872 | tf_op jit(solution)/shard_map/ppermute | solution.py:263
  3.7 25.7 %collective-permute-start.1 = (bf16[1,128,2048]{2,1,0:T(8,128)(2,1)}, bf16[1,128,2048]{2,1,0:T(8,128)(2,1)S(1)}, u32[]{:S(2)}, u32[]{:S(2)}) collective-permute-start(bf16[1,128,2048]{2,1,0:T(8,128)(2,1)} %own.1), channel_id=1, source_target_pairs={{0,12},{12,0},{4,8},{8,4},{1,13},{13,1},{5,9},{9,5},{2,14},{14,2},... | collective-permute-start | bytes 1572872 | tf_op jit(solution)/shard_map/ppermute | solution.py:264
  8.3 28.5 %collective-permute-start.5 = (bf16[1,256,1536]{2,1,0:T(8,128)(2,1)}, bf16[1,256,1536]{2,1,0:T(8,128)(2,1)S(1)}, u32[]{:S(2)}, u32[]{:S(2)}) collective-permute-start(bf16[1,256,1536]{2,1,0:T(8,128)(2,1)} %slice.6), channel_id=1, source_target_pairs={{0,2},{2,0},{1,3},{3,1},{4,6},{6,4},{5,7},{7,5},{8,10},{10,8},{9,1... | collective-permute-start | bytes 2359304 | tf_op jit(solution)/shard_map/ppermute | solution.py:15
  11.8 32.2 %collective-permute-start.6 = (bf16[1,256,1536]{2,1,0:T(8,128)(2,1)}, bf16[1,256,1536]{2,1,0:T(8,128)(2,1)S(1)}, u32[]{:S(2)}, u32[]{:S(2)}) collective-permute-start(bf16[1,256,1536]{2,1,0:T(8,128)(2,1)} %slice.7), channel_id=1, source_target_pairs={{0,2},{2,0},{1,3},{3,1},{4,6},{6,4},{5,7},{7,5},{8,10},{10,8},{9,1... | collective-permute-start | bytes 2359304 | tf_op jit(solution)/shard_map/ppermute | solution.py:15
  29.4 14.7 %collective-permute-start.4 = (bf16[1,128,2048]{2,1,0:T(8,128)(2,1)S(1)}, bf16[1,128,2048]{2,1,0:T(8,128)(2,1)S(1)}, u32[]{:S(2)}, u32[]{:S(2)}) collective-permute-start(bf16[1,128,2048]{2,1,0:T(8,128)(2,1)S(1)} %collective-permute-done.1.across), channel_id=1, source_target_pairs={{4,0},{8,12},{5,1},{9,13},{6,2},{10,14},{7,3},{11,15},{20,16},{24,... | collective-permute-start | bytes 1572872 | tf_op jit(solution)/shard_map/ppermute | solution.py:268
  30.7 13.4 %collective-permute-start.3 = (bf16[1,128,2048]{2,1,0:T(8,128)(2,1)S(1)}, bf16[1,128,2048]{2,1,0:T(8,128)(2,1)}, u32[]{:S(2)}, u32[]{:S(2)}) collective-permute-start(bf16[1,128,2048]{2,1,0:T(8,128)(2,1)S(1)} %collective-permute-done.buddy), channel_id=1, source_target_pairs={{4,8},{8,4},{5,9},{9,5},{6,10},{10,6},{7,11},{11,7},{20,24},{24,20... | collective-permute-start | bytes 1572872 | tf_op jit(solution)/shard_map/ppermute | solution.py:271
  33.9 1.9 %collective-permute-start.2 = (bf16[1,128,1024]{2,1,0:T(8,128)(2,1)}, bf16[1,128,1024]{2,1,0:T(8,128)(2,1)}, u32[]{:S(2)}, u32[]{:S(2)}) collective-permute-start(bf16[1,128,1024]{2,1,0:T(8,128)(2,1)} %get-tuple-element.135), channel_id=1, source_target_pairs={{0,1},{1,0},{2,3},{3,2},{4,5},{5,4},{6,7},{7,6},{8,9},{9,8},{10,11... | collective-permute-start | bytes 786440 | tf_op jit(solution)/shard_map/ppermute | solution.py:15
  44.0 1.0 copy-start.2
  46.8 0.7 copy-start.3
  52.7 20.2 %copy-start = (bf16[1,256,3584]{2,1,0:T(8,128)(2,1)S(1)}, bf16[1,256,3584]{2,1,0:T(8,128)(2,1)}, u32[]{:S(2)}) copy-start(bf16[1,256,3584]{2,1,0:T(8,128)(2,1)} %gates.13) | copy-start | bytes 5505028
  52.7 20.2 %copy-start.1 = (bf16[1,256,3584]{2,1,0:T(8,128)(2,1)S(1)}, bf16[1,256,3584]{2,1,0:T(8,128)(2,1)}, u32[]{:S(2)}) copy-start(bf16[1,256,3584]{2,1,0:T(8,128)(2,1)} %ups.13) | copy-start | bytes 5505028
  52.7 20.2 %collective-permute-start.7 = (bf16[256,1024]{1,0:T(8,128)(2,1)S(1)}, bf16[256,1024]{1,0:T(8,128)(2,1)S(1)}, u32[]{:S(2)}, u32[]{:S(2)}) collective-permute-start(bf16[256,1024]{1,0:T(8,128)(2,1)S(1)} %get-tuple-element.72), channel_id=1, source_target_pairs={{0,2},{2,0},{1,3},{3,1},{4,6},{6,4},{5,7},{7,5},{8,10},{10,8},{9,1... | collective-permute-start | bytes 1572872 | tf_op jit(solution)/shard_map/ppermute | solution.py:15
  59.5 19.4 %collective-permute-start.8 = (bf16[256,1024]{1,0:T(8,128)(2,1)S(1)}, bf16[256,1024]{1,0:T(8,128)(2,1)S(1)}, u32[]{:S(2)}, u32[]{:S(2)}) collective-permute-start(bf16[256,1024]{1,0:T(8,128)(2,1)S(1)} %get-tuple-element.74), channel_id=1, source_target_pairs={{0,2},{2,0},{1,3},{3,1},{4,6},{6,4},{5,7},{7,5},{8,10},{10,8},{9,1... | collective-permute-start | bytes 1572872 | tf_op jit(solution)/shard_map/ppermute | solution.py:15
  60.4 20.0 %collective-permute-start.11 = (bf16[2,128,1024]{2,1,0:T(8,128)(2,1)S(1)}, bf16[2,128,1024]{2,1,0:T(8,128)(2,1)S(1)}, u32[]{:S(2)}, u32[]{:S(2)}) collective-permute-start(bf16[2,128,1024]{2,1,0:T(8,128)(2,1)S(1)} %pad_maximum_fusion.own), channel_id=1, source_target_pairs={{0,4},{4,0},{8,12},{12,8},{1,5},{5,1},{9,13},{13,9},{2,6},{6,2},{1... | collective-permute-start | bytes 1572872 | tf_op jit(solution)/shard_map/ppermute | solution.py:263
  64.1 21.4 %collective-permute-start.12 = (bf16[2,128,1024]{2,1,0:T(8,128)(2,1)S(1)}, bf16[2,128,1024]{2,1,0:T(8,128)(2,1)S(1)}, u32[]{:S(2)}, u32[]{:S(2)}) collective-permute-start(bf16[2,128,1024]{2,1,0:T(8,128)(2,1)S(1)} %pad_maximum_fusion.own), channel_id=1, source_target_pairs={{0,12},{12,0},{4,8},{8,4},{1,13},{13,1},{5,9},{9,5},{2,14},{14,2},... | collective-permute-start | bytes 1572872 | tf_op jit(solution)/shard_map/ppermute | solution.py:264
  73.5 16.6 %collective-permute-start.9 = (bf16[2,256,512]{2,1,0:T(8,128)(2,1)S(1)}, bf16[2,256,512]{2,1,0:T(8,128)(2,1)S(1)}, u32[]{:S(2)}, u32[]{:S(2)}) collective-permute-start(bf16[2,256,512]{2,1,0:T(8,128)(2,1)S(1)} %shard_map.81.mine), channel_id=1, source_target_pairs={{0,2},{2,0},{1,3},{3,1},{4,6},{6,4},{5,7},{7,5},{8,10},{10,8},{9,1... | collective-permute-start | bytes 1572872 | tf_op jit(solution)/shard_map/ppermute | solution.py:15
  78.9 19.8 %collective-permute-start.10 = (bf16[512,512]{1,0:T(8,128)(2,1)S(1)}, bf16[512,512]{1,0:T(8,128)(2,1)S(1)}, u32[]{:S(2)}, u32[]{:S(2)}) collective-permute-start(bf16[512,512]{1,0:T(8,128)(2,1)S(1)} %shard_map.82.own), channel_id=1, source_target_pairs={{0,2},{2,0},{1,3},{3,1},{4,6},{6,4},{5,7},{7,5},{8,10},{10,8},{9,1... | collective-permute-start | bytes 1572872 | tf_op jit(solution)/shard_map/ppermute | solution.py:15
  80.4 20.7 %collective-permute-start.13 = (bf16[2,128,1024]{2,1,0:T(8,128)(2,1)S(1)}, bf16[2,128,1024]{2,1,0:T(8,128)(2,1)S(1)}, u32[]{:S(2)}, u32[]{:S(2)}) collective-permute-start(bf16[2,128,1024]{2,1,0:T(8,128)(2,1)S(1)} %collective-permute-done.11.buddy), channel_id=1, source_target_pairs={{4,8},{8,4},{5,9},{9,5},{6,10},{10,6},{7,11},{11,7},{20,24},{24,20... | collective-permute-start | bytes 1572872 | tf_op jit(solution)/shard_map/ppermute | solution.py:271
  85.5 15.6 %collective-permute-start.14 = (bf16[2,128,1024]{2,1,0:T(8,128)(2,1)S(1)}, bf16[2,128,1024]{2,1,0:T(8,128)(2,1)S(1)}, u32[]{:S(2)}, u32[]{:S(2)}) collective-permute-start(bf16[2,128,1024]{2,1,0:T(8,128)(2,1)S(1)} %collective-permute-done.12.across), channel_id=1, source_target_pairs={{4,0},{8,12},{5,1},{9,13},{6,2},{10,14},{7,3},{11,15},{20,16},{24,... | collective-permute-start | bytes 1572872 | tf_op jit(solution)/shard_map/ppermute | solution.py:268
  86.8 15.2 %collective-permute-start.15 = (bf16[2,256,512]{2,1,0:T(8,128)(2,1)S(1)}, bf16[2,256,512]{2,1,0:T(8,128)(2,1)S(1)}, u32[]{:S(2)}, u32[]{:S(2)}) collective-permute-start(bf16[2,256,512]{2,1,0:T(8,128)(2,1)S(1)} %shard_map.81.mine), channel_id=1, source_target_pairs={{0,1},{1,0},{2,3},{3,2},{4,5},{5,4},{6,7},{7,6},{8,9},{9,8},{10,11... | collective-permute-start | bytes 1572872 | tf_op jit(solution)/shard_map/ppermute | solution.py:15
  90.1 11.9 %collective-permute-start.16 = (bf16[2,256,512]{2,1,0:T(8,128)(2,1)S(1)}, bf16[2,256,512]{2,1,0:T(8,128)(2,1)S(1)}, u32[]{:S(2)}, u32[]{:S(2)}) collective-permute-start(bf16[2,256,512]{2,1,0:T(8,128)(2,1)S(1)} %collective-permute-done.9.theirs), channel_id=1, source_target_pairs={{0,1},{1,0},{2,3},{3,2},{4,5},{5,4},{6,7},{7,6},{8,9},{9,8},{10,11... | collective-permute-start | bytes 1572872 | tf_op jit(solution)/shard_map/ppermute | solution.py:15
  98.7 12.2 %collective-permute-start.17 = (bf16[512,512]{1,0:T(8,128)(2,1)S(1)}, bf16[512,512]{1,0:T(8,128)(2,1)S(1)}, u32[]{:S(2)}, u32[]{:S(2)}) collective-permute-start(bf16[512,512]{1,0:T(8,128)(2,1)S(1)} %shard_map.83.own), channel_id=1, source_target_pairs={{0,2},{2,0},{1,3},{3,1},{4,6},{6,4},{5,7},{7,5},{8,10},{10,8},{9,1... | collective-permute-start | bytes 1572872 | tf_op jit(solution)/shard_map/ppermute | solution.py:15
  105.8 6.1 %collective-permute-start.18 = (bf16[2,256,512]{2,1,0:T(8,128)(2,1)S(1)}, bf16[2,256,512]{2,1,0:T(8,128)(2,1)S(1)}, u32[]{:S(2)}, u32[]{:S(2)}) collective-permute-start(bf16[2,256,512]{2,1,0:T(8,128)(2,1)S(1)} %get-tuple-element.99.mine), channel_id=1, source_target_pairs={{0,1},{1,0},{2,3},{3,2},{4,5},{5,4},{6,7},{7,6},{8,9},{9,8},{10,11... | collective-permute-start | bytes 1572872 | tf_op jit(solution)/shard_map/ppermute | solution.py:15
  105.8 6.1 %collective-permute-start.19 = (bf16[2,256,512]{2,1,0:T(8,128)(2,1)S(1)}, bf16[2,256,512]{2,1,0:T(8,128)(2,1)S(1)}, u32[]{:S(2)}, u32[]{:S(2)}) collective-permute-start(bf16[2,256,512]{2,1,0:T(8,128)(2,1)S(1)} %get-tuple-element.100.theirs), channel_id=1, source_target_pairs={{0,1},{1,0},{2,3},{3,2},{4,5},{5,4},{6,7},{7,6},{8,9},{9,8},{10,11... | collective-permute-start | bytes 1572872 | tf_op jit(solution)/shard_map/ppermute | solution.py:15
  106.3 15.9 %collective-permute-start.20 = (bf16[512,512]{1,0:T(8,128)(2,1)S(1)}, bf16[512,512]{1,0:T(8,128)(2,1)S(1)}, u32[]{:S(2)}, u32[]{:S(2)}) collective-permute-start(bf16[512,512]{1,0:T(8,128)(2,1)S(1)} %shard_map.87.own), channel_id=1, source_target_pairs={{0,2},{2,0},{1,3},{3,1},{4,6},{6,4},{5,7},{7,5},{8,10},{10,8},{9,1... | collective-permute-start | bytes 1572872 | tf_op jit(solution)/shard_map/ppermute | solution.py:15
  115.7 7.5 %collective-permute-start.21 = (bf16[2,256,512]{2,1,0:T(8,128)(2,1)S(1)}, bf16[2,256,512]{2,1,0:T(8,128)(2,1)S(1)}, u32[]{:S(2)}, u32[]{:S(2)}) collective-permute-start(bf16[2,256,512]{2,1,0:T(8,128)(2,1)S(1)} %get-tuple-element.108.mine), channel_id=1, source_target_pairs={{0,1},{1,0},{2,3},{3,2},{4,5},{5,4},{6,7},{7,6},{8,9},{9,8},{10,11... | collective-permute-start | bytes 1572872 | tf_op jit(solution)/shard_map/ppermute | solution.py:15
  115.7 7.5 %collective-permute-start.22 = (bf16[2,256,512]{2,1,0:T(8,128)(2,1)S(1)}, bf16[2,256,512]{2,1,0:T(8,128)(2,1)S(1)}, u32[]{:S(2)}, u32[]{:S(2)}) collective-permute-start(bf16[2,256,512]{2,1,0:T(8,128)(2,1)S(1)} %get-tuple-element.109.theirs), channel_id=1, source_target_pairs={{0,1},{1,0},{2,3},{3,2},{4,5},{5,4},{6,7},{7,6},{8,9},{9,8},{10,11... | collective-permute-start | bytes 1572872 | tf_op jit(solution)/shard_map/ppermute | solution.py:15
  116.7 16.7 %collective-permute-start.23 = (bf16[2,256,512]{2,1,0:T(8,128)(2,1)S(1)}, bf16[2,256,512]{2,1,0:T(8,128)(2,1)S(1)}, u32[]{:S(2)}, u32[]{:S(2)}) collective-permute-start(bf16[2,256,512]{2,1,0:T(8,128)(2,1)S(1)} %shard_map.90.mine), channel_id=1, source_target_pairs={{0,2},{2,0},{1,3},{3,1},{4,6},{6,4},{5,7},{7,5},{8,10},{10,8},{9,1... | collective-permute-start | bytes 1572872 | tf_op jit(solution)/shard_map/ppermute | solution.py:15
  126.9 6.5 %collective-permute-start.24 = (bf16[2,256,512]{2,1,0:T(8,128)(2,1)S(1)}, bf16[2,256,512]{2,1,0:T(8,128)(2,1)S(1)}, u32[]{:S(2)}, u32[]{:S(2)}) collective-permute-start(bf16[2,256,512]{2,1,0:T(8,128)(2,1)S(1)} %get-tuple-element.115.mine), channel_id=1, source_target_pairs={{0,1},{1,0},{2,3},{3,2},{4,5},{5,4},{6,7},{7,6},{8,9},{9,8},{10,11... | collective-permute-start | bytes 1572872 | tf_op jit(solution)/shard_map/ppermute | solution.py:15
  126.9 6.5 %collective-permute-start.25 = (bf16[2,256,512]{2,1,0:T(8,128)(2,1)S(1)}, bf16[2,256,512]{2,1,0:T(8,128)(2,1)S(1)}, u32[]{:S(2)}, u32[]{:S(2)}) collective-permute-start(bf16[2,256,512]{2,1,0:T(8,128)(2,1)S(1)} %get-tuple-element.116.theirs), channel_id=1, source_target_pairs={{0,1},{1,0},{2,3},{3,2},{4,5},{5,4},{6,7},{7,6},{8,9},{9,8},{10,11... | collective-permute-start | bytes 1572872 | tf_op jit(solution)/shard_map/ppermute | solution.py:15
  128.0 16.7 %collective-permute-start.26 = (bf16[2,256,512]{2,1,0:T(8,128)(2,1)S(1)}, bf16[2,256,512]{2,1,0:T(8,128)(2,1)S(1)}, u32[]{:S(2)}, u32[]{:S(2)}) collective-permute-start(bf16[2,256,512]{2,1,0:T(8,128)(2,1)S(1)} %shard_map.93.mine), channel_id=1, source_target_pairs={{0,2},{2,0},{1,3},{3,1},{4,6},{6,4},{5,7},{7,5},{8,10},{10,8},{9,1... | collective-permute-start | bytes 1572872 | tf_op jit(solution)/shard_map/ppermute | solution.py:15
  137.1 7.5 %collective-permute-start.27 = (bf16[2,256,512]{2,1,0:T(8,128)(2,1)S(1)}, bf16[2,256,512]{2,1,0:T(8,128)(2,1)S(1)}, u32[]{:S(2)}, u32[]{:S(2)}) collective-permute-start(bf16[2,256,512]{2,1,0:T(8,128)(2,1)S(1)} %shard_map.90.mine), channel_id=1, source_target_pairs={{0,1},{1,0},{2,3},{3,2},{4,5},{5,4},{6,7},{7,6},{8,9},{9,8},{10,11... | collective-permute-start | bytes 1572872 | tf_op jit(solution)/shard_map/ppermute | solution.py:15
  137.1 7.5 %collective-permute-start.28 = (bf16[2,256,512]{2,1,0:T(8,128)(2,1)S(1)}, bf16[2,256,512]{2,1,0:T(8,128)(2,1)S(1)}, u32[]{:S(2)}, u32[]{:S(2)}) collective-permute-start(bf16[2,256,512]{2,1,0:T(8,128)(2,1)S(1)} %collective-permute-done.23.theirs), channel_id=1, source_target_pairs={{0,1},{1,0},{2,3},{3,2},{4,5},{5,4},{6,7},{7,6},{8,9},{9,8},{10,11... | collective-permute-start | bytes 1572872 | tf_op jit(solution)/shard_map/ppermute | solution.py:15
  138.2 16.7 %collective-permute-start.29 = (bf16[2,256,512]{2,1,0:T(8,128)(2,1)S(1)}, bf16[2,256,512]{2,1,0:T(8,128)(2,1)S(1)}, u32[]{:S(2)}, u32[]{:S(2)}) collective-permute-start(bf16[2,256,512]{2,1,0:T(8,128)(2,1)S(1)} %shard_map.95.mine), channel_id=1, source_target_pairs={{0,2},{2,0},{1,3},{3,1},{4,6},{6,4},{5,7},{7,5},{8,10},{10,8},{9,1... | collective-permute-start | bytes 1572872 | tf_op jit(solution)/shard_map/ppermute | solution.py:15
  148.4 7.0 %collective-permute-start.30 = (bf16[2,256,512]{2,1,0:T(8,128)(2,1)S(1)}, bf16[2,256,512]{2,1,0:T(8,128)(2,1)S(1)}, u32[]{:S(2)}, u32[]{:S(2)}) collective-permute-start(bf16[2,256,512]{2,1,0:T(8,128)(2,1)S(1)} %shard_map.93.mine), channel_id=1, source_target_pairs={{0,1},{1,0},{2,3},{3,2},{4,5},{5,4},{6,7},{7,6},{8,9},{9,8},{10,11... | collective-permute-start | bytes 1572872 | tf_op jit(solution)/shard_map/ppermute | solution.py:15
  148.4 7.0 %collective-permute-start.31 = (bf16[2,256,512]{2,1,0:T(8,128)(2,1)S(1)}, bf16[2,256,512]{2,1,0:T(8,128)(2,1)S(1)}, u32[]{:S(2)}, u32[]{:S(2)}) collective-permute-start(bf16[2,256,512]{2,1,0:T(8,128)(2,1)S(1)} %collective-permute-done.26.theirs), channel_id=1, source_target_pairs={{0,1},{1,0},{2,3},{3,2},{4,5},{5,4},{6,7},{7,6},{8,9},{9,8},{10,11... | collective-permute-start | bytes 1572872 | tf_op jit(solution)/shard_map/ppermute | solution.py:15
  154.9 4.2 %collective-permute-start.32 = (bf16[2,256,512]{2,1,0:T(8,128)(2,1)S(1)}, bf16[2,256,512]{2,1,0:T(8,128)(2,1)S(1)}, u32[]{:S(2)}, u32[]{:S(2)}) collective-permute-start(bf16[2,256,512]{2,1,0:T(8,128)(2,1)S(1)} %shard_map.95.mine), channel_id=1, source_target_pairs={{0,1},{1,0},{2,3},{3,2},{4,5},{5,4},{6,7},{7,6},{8,9},{9,8},{10,11... | collective-permute-start | bytes 1572872 | tf_op jit(solution)/shard_map/ppermute | solution.py:15
  154.9 4.2 %collective-permute-start.33 = (bf16[2,256,512]{2,1,0:T(8,128)(2,1)S(1)}, bf16[2,256,512]{2,1,0:T(8,128)(2,1)S(1)}, u32[]{:S(2)}, u32[]{:S(2)}) collective-permute-start(bf16[2,256,512]{2,1,0:T(8,128)(2,1)S(1)} %collective-permute-done.29.theirs), channel_id=1, source_target_pairs={{0,1},{1,0},{2,3},{3,2},{4,5},{5,4},{6,7},{7,6},{8,9},{9,8},{10,11... | collective-permute-start | bytes 1572872 | tf_op jit(solution)/shard_map/ppermute | solution.py:15

commit v4 on v3

--- a/solution.py
+++ b/solution.py
@@ -7,7 +7,7 @@
 from jax.experimental.pallas import tpu as pltpu
 from jax.sharding import PartitionSpec as P
 
-VMEM_LIMIT = 40 * 1024 * 1024
+VMEM_LIMIT = 48 * 1024 * 1024
 LANES = 256
 
 
@@ -45,6 +45,26 @@
     )(*operands)
 
 
+def pack_kernel(gates, ups, out):
+    out[0] = gates[0]
+    out[1] = ups[0]
+
+
+def packed(gate_pre, up_pre, start, width):
+    tokens = gate_pre.shape[1]
+    lanes = 2 * LANES
+    offset = start // lanes
+    piece = pl.BlockSpec((1, tokens, lanes), lambda i: (0, 0, offset + i))
+    return call(
+        pack_kernel,
+        (width // lanes,),
+        [piece, piece],
+        pl.BlockSpec((2, tokens, lanes), lambda i: (0, 0, i)),
+        jax.ShapeDtypeStruct((2, tokens, width), gate_pre.dtype),
+        [gate_pre, up_pre],
+    )
+
+
 def arrange_kernel(places, own, buddy, across, middle, outward, out):
     for k, shard in enumerate((own, buddy, across)):
         out[:, pl.ds(places[k], 1)] = shard[...][:, None]
@@ -168,35 +188,35 @@
     )
 
 
-def both_kernel(own, other, gates, ups, other_gates, other_ups, mine, theirs):
+def both_kernel(own, other, gates, ups, other_saved, mine, theirs):
     half = gates.shape[1]
-    for k, (gate, up, out) in enumerate(((gates, ups, mine), (other_gates, other_ups, theirs))):
+    for k, (gate, up, out) in enumerate(((gates[0], ups[0], mine), (other_saved[0], other_saved[1], theirs))):
         here = slice(k * half, (k + 1) * half)
         there = slice((1 - k) * half, (2 - k) * half)
         hidden_grad = own[here].astype(jnp.float32) + other[there].astype(jnp.float32)
         d_gate, d_up = d_gate_and_up(
-            hidden_grad, gate[0].astype(jnp.float32), up[0].astype(jnp.float32)
+            hidden_grad, gate.astype(jnp.float32), up.astype(jnp.float32)
         )
         out[0] = d_gate
         out[1] = d_up
 
 
-def both_activation_grads(own, other, gate_pre, up_pre, other_gates, other_ups, start, inner):
+def both_activation_grads(own, other, gate_pre, up_pre, other_saved, start, inner):
     tokens, width = own.shape
     offset = start // LANES
     inner = inner // LANES
     piece = pl.BlockSpec((tokens, LANES), lambda i: (0, i))
     saved = pl.BlockSpec((1, tokens // 2, LANES), lambda i: (0, 0, offset + i))
-    swapped = pl.BlockSpec((1, tokens // 2, LANES), lambda i: (0, 0, inner + i))
+    swapped = pl.BlockSpec((2, tokens // 2, LANES), lambda i: (0, 0, inner + i))
     out = jax.ShapeDtypeStruct((2, tokens // 2, width), jnp.bfloat16)
     out_spec = pl.BlockSpec((2, tokens // 2, LANES), lambda i: (0, 0, i))
     return call(
         both_kernel,
         (width // LANES,),
-        [piece, piece, saved, saved, swapped, swapped],
+        [piece, piece, saved, saved, swapped],
         [out_spec, out_spec],
         [out, out],
-        [own, other, gate_pre, up_pre, other_gates, other_ups],
+        [own, other, gate_pre, up_pre, other_saved],
     )
 
 
@@ -255,9 +275,8 @@
     half_features = features // 2
     chain = Chain()
 
-    shared = 4 * unit
-    other_gates = swap_neighbours(gate_pre[:, :, shared:], "col")
-    other_ups = swap_neighbours(up_pre[:, :, shared:], "col")
+    shared = 3 * unit
+    other_saved = swap_neighbours(packed(gate_pre, up_pre, shared, hidden - shared), "col")
 
     def gather_near(shard):
         buddy = lax.ppermute(shard, "row", [(0, 1), (1, 0), (2, 3), (3, 2)])
@@ -276,22 +295,19 @@
     places = places.astype(jnp.int32)
 
     buddy, across = gather_near(out_grad)
-    middle = send_middle(buddy)
-    across = lax.optimization_barrier((across, buddy))[0]
-    outward = send_outward(across)
-
     keep = lax.dynamic_slice_in_dim(layer_input, depth * half_features, half_features, 2)
     send = lax.dynamic_slice_in_dim(layer_input, (1 - depth) * half_features, half_features, 2)
+    send = lax.optimization_barrier((send, buddy))[0]
     both = jnp.concatenate([keep, swap_neighbours(send, "depth")], axis=0)
-    across = lax.optimization_barrier((across, both))[0]
-
-    outward = lax.optimization_barrier((outward, other_gates, other_ups))[0]
+    middle = send_middle(lax.optimization_barrier((buddy, both))[0])
+    outward = send_outward(lax.optimization_barrier((across, both))[0])
+
     grads = arranged(chain(places), [out_grad, buddy, across, middle, outward])
     chain.done(grads)
     grads = grads.reshape(4 * shard_tokens, features)
 
-    starts = {f"p{k}": k * unit for k in range(4)}
-    starts.update({f"s{k}": shared + k * unit for k in range(3)})
+    starts = {f"p{k}": k * unit for k in range(3)}
+    starts.update({f"s{k}": shared + k * unit for k in range(4)})
     own_part, other_part, mine, theirs, mine_far, theirs_far = {}, {}, {}, {}, {}, {}
     blocks = unit // LANES
 
@@ -314,7 +330,7 @@
             theirs[name] = swap_neighbours(mine[name], "col")
         else:
             mine[name], theirs[name] = both_activation_grads(
-                *operands, other_gates, other_ups, starts[name], starts[name] - shared
+                *operands, other_saved, starts[name], starts[name] - shared
             )
         chain.done(mine[name])
 
@@ -330,54 +346,48 @@
 
     outs = None
     kept, sent = partial_products(
-        chain(grads), down_codes, down_scales, 0, [(2 * blocks, True)]
+        chain(grads), down_codes, down_scales, 0, [(3 * blocks, True)]
     )
     chain.done(sent)
-    send_step(["p0", "p1"], kept, sent)
+    send_step(["p0", "p1", "p2"], kept, sent)
     input_near = gather_near(chain(both))
-    kept, sent = partial_products(
-        chain(grads), down_codes, down_scales, 2 * unit, [(2 * blocks, True)]
-    )
-    chain.done(sent)
-    send_step(["p2", "p3"], kept, sent)
     rest = partial_products(
-        chain(grads), down_codes, down_scales, shared, [(blocks, False)] * 3
+        chain(grads), down_codes, down_scales, shared, [(blocks, False)] * 4
     )
     chain.done(rest[0])
     shared_parts = {f"s{k}": part for k, part in enumerate(rest)}
+    touch_step("s0")
     activation_step("p0")
     input_far = send_middle(chain(input_near[0])), send_outward(chain(input_near[1]))
-    chain.wait(other_part["p2"])
-    touch_step("s0")
-    far_step("p0")
+    activation_step("s0")
+    far_step("s0")
+    touch_step("s1")
     chain.wait(theirs["p0"])
-    touch_step("s1")
-    activation_step("s0")
     inputs = arranged(chain(places), [both, *input_near, *input_far])
     chain.done(inputs)
     inputs = inputs.reshape(-1, half_features)
-    outs = weight_step("p0", outs)
-    far_step("s0")
+    outs = weight_step("s0", outs)
+    far_step("p0")
     touch_step("s2")
     activation_step("s1")
-    outs = weight_step("s0", outs)
+    outs = weight_step("p0", outs)
     far_step("s1")
-    activation_step("p1")
+    touch_step("s3")
     activation_step("s2")
     outs = weight_step("s1", outs)
     far_step("s2")
+    activation_step("p1")
+    activation_step("s3")
+    outs = weight_step("s2", outs)
+    far_step("s3")
     activation_step("p2")
     chain.wait(theirs["p1"])
-    outs = weight_step("s2", outs)
+    outs = weight_step("s3", outs)
     far_step("p1")
-    activation_step("p3")
     chain.wait(theirs["p2"])
+    far_step("p2")
     outs = weight_step("p1", outs)
-    far_step("p2")
-    chain.wait(theirs["p3"])
-    far_step("p3")
     outs = weight_step("p2", outs)
-    outs = weight_step("p3", outs)
     return tuple(outs)
 
 

time: 164 us -> 163 us (level)
  starting transfers between devices: 33 us -> 23.8 us
  waiting for transfers between devices: 68.6 us -> 75.6 us
  Pallas kernels: 51.6 us -> 56.2 us
  local copies, waits for them, and re-layouts: 7.72 us -> 5.91 us
    ppermute x2, waiting for transfers between devices: 0.01 us -> 16.3 us  [send_outward(): return lax.ppermute(across, 'row', [(1, 0), (2, 3)])]
    ppermute x26 -> x24, starting transfers between devices: 17.6 us -> 9.72 us  [swap_neighbours(): lax.ppermute(value, axis, [(i, i ^ 1) for i in range(lax.axis_size(axis))])]
    ppermute x26 -> x24, waiting for transfers between devices: 47.2 us -> 39.8 us  [swap_neighbours(): lax.ppermute(value, axis, [(i, i ^ 1) for i in range(lax.axis_size(axis))])]
    pallas_call x22 -> x23, Pallas kernels: 51.6 us -> 56.2 us  [call(): pl.pallas_call(kernel, grid_spec=pltpu.PrefetchScalarGridSpec(num_scalar_...]
    slice x2 -> x0, local copies, waits for them, and re-layouts: 4.12 us -> none  [the longest x1 2.06 us: on_pairs(): other_gates = swap_neighbours(gate_pre[:, :, shared:], 'col')]
    ppermute x2, starting transfers between devices: 6.83 us -> 3.09 us  [gather_near(): buddy = lax.ppermute(shard, 'row', [(0, 1), (1, 0), (2, 3), (3, 2)])]
    unnamed x8 -> x22, local copies, waits for them, and re-layouts: 1.75 us -> 4.76 us
    ppermute x2, starting transfers between devices: 3.82 us -> 6.31 us  [gather_near(): across = lax.ppermute(shard, 'row', [(0, 3), (3, 0), (1, 2), (2, 1)])]
  transfers between devices with their start and end apart: 34 -> 32, of which waited for: 13 -> 13; matrix products, arithmetic and copies ran while one was open for 4% -> 1% of each run, Pallas kernels for 25% -> 32%
where the time goes in v4:
time: 163 us; the launch traced here: 162 us
  waiting for transfers between devices  75.6 us (46%)
  Pallas kernels  56.2 us (34%)
  starting transfers between devices  23.8 us (15%)
  local copies, waits for them, and re-layouts  5.91 us (4%)
    pallas_call x23, Pallas kernels, call(): pl.pallas_call(kernel, grid_spec=pltpu.PrefetchScalarGridSpec(num_scalar_...  56.2 us
    ppermute x24, waiting for transfers between devices, swap_neighbours(): lax.ppermute(value, axis, [(i, i ^ 1) for i in range(lax.axis_size(axis))])  39.8 us
    ppermute x2, waiting for transfers between devices, send_outward(): return lax.ppermute(across, 'row', [(1, 0), (2, 3)])  16.3 us
    ppermute x2, waiting for transfers between devices, gather_near(): across = lax.ppermute(shard, 'row', [(0, 3), (3, 0), (1, 2), (2, 1)])  15.5 us
    ppermute x24, starting transfers between devices, swap_neighbours(): lax.ppermute(value, axis, [(i, i ^ 1) for i in range(lax.axis_size(axis))])  9.72 us
    ppermute x2, starting transfers between devices, gather_near(): across = lax.ppermute(shard, 'row', [(0, 3), (3, 0), (1, 2), (2, 1)])  6.31 us
    unnamed x22, local copies, waits for them, and re-layouts  4.76 us
    ppermute x2, waiting for transfers between devices, gather_near(): buddy = lax.ppermute(shard, 'row', [(0, 1), (1, 0), (2, 3), (3, 2)])  4.02 us
  transfers between devices with their start and end apart: 32, of which 13 were waited for; matrix products, arithmetic and copies ran while one was open for 1% of the time, Pallas kernels for 32%

profile of v4, /device:TPU:0, one launch (start us, length us, event | category | flops | bytes accessed | tf_op | source)
XLA Modules:
  0.0 162.5 jit_solution(9097695606906790968)
XLA Ops:
  0.6 3.1 %collective-permute-start = (bf16[1,128,2048]{2,1,0:T(8,128)(2,1)}, bf16[1,128,2048]{2,1,0:T(8,128)(2,1)S(1)}, u32[]{:S(2)}, u32[]{:S(2)}) collective-permute-start(bf16[1,128,2048]{2,1,0:T(8,128)(2,1)} %own.1), channel_id=1, source_target_pairs={{0,4},{4,0},{8,12},{12,8},{1,5},{5,1},{9,13},{13,9},{2,6},{6,2},{1... | collective-permute-start | bytes 1572872 | tf_op jit(solution)/shard_map/ppermute | solution.py:282
  3.7 1.5 copy-done
  5.2 1.5 copy-done.2
  6.7 0.5 shard_map.82
  7.2 1.6 collective-permute-start.7
  8.8 2.5 %collective-permute-start.1 = (bf16[1,128,2048]{2,1,0:T(8,128)(2,1)}, bf16[1,128,2048]{2,1,0:T(8,128)(2,1)}, u32[]{:S(2)}, u32[]{:S(2)}) collective-permute-start(bf16[1,128,2048]{2,1,0:T(8,128)(2,1)} %own.1), channel_id=1, source_target_pairs={{0,12},{12,0},{4,8},{8,4},{1,13},{13,1},{5,9},{9,5},{2,14},{14,2},... | collective-permute-start | bytes 1572872 | tf_op jit(solution)/shard_map/ppermute | solution.py:283
  11.3 1.1 constant_dynamic-slice_fusion.1
  12.3 4.0 %collective-permute-done.buddy = bf16[1,128,2048]{2,1,0:T(8,128)(2,1)S(1)} collective-permute-done((bf16[1,128,2048]{2,1,0:T(8,128)(2,1)}, bf16[1,128,2048]{2,1,0:T(8,128)(2,1)S(1)}, u32[]{:S(2)}, u32[]{:S(2)}) %collective-permute-start) | collective-permute-done | bytes 524320 | tf_op jit(solution)/shard_map/ppermute | solution.py:282
  16.4 1.5 collective-permute-done.2
  18.0 1.4 collective-permute-start.3
  19.4 10.1 %collective-permute-done.1.across = bf16[1,128,2048]{2,1,0:T(8,128)(2,1)} collective-permute-done((bf16[1,128,2048]{2,1,0:T(8,128)(2,1)}, bf16[1,128,2048]{2,1,0:T(8,128)(2,1)}, u32[]{:S(2)}, u32[]{:S(2)}) %collective-permute-start.1) | collective-permute-done | bytes 524320 | tf_op jit(solution)/shard_map/ppermute | solution.py:283
  29.5 1.3 collective-permute-start.4
  30.9 16.3 %collective-permute-done.4.outward = bf16[1,128,2048]{2,1,0:T(8,128)(2,1)} collective-permute-done((bf16[1,128,2048]{2,1,0:T(8,128)(2,1)}, bf16[1,128,2048]{2,1,0:T(8,128)(2,1)}, u32[]{:S(2)}, u32[]{:S(2)}) %collective-permute-start.4) | collective-permute-done | bytes 524320 | tf_op jit(solution)/shard_map/ppermute | solution.py:287
  47.2 1.0 copy-done.8
  48.2 2.0 %shard_map.77 = bf16[1,4,128,2048]{3,2,1,0:T(8,128)(2,1)S(1)} custom-call(s32[5]{0:T(128)S(1)} %stack.27.places, bf16[1,128,2048]{2,1,0:T(8,128)(2,1)S(1)} %copy-done.8, bf16[1,128,2048]{2,1,0:T(8,128)(2,1)S(1)} %collective-permute-done.buddy, bf16[1,128,2048]{2,1,0:T(8,128)(2,1)} %collective-permute-done.1.across, ...), custom_call_target="tpu_custom_call" | custom-call | flops 1 | bytes 1 | tf_op jit(solution)/shard_map/pallas_call | solution.py:32
  50.3 0.7 copy-done.9
  51.0 7.5 %shard_map.78 = (bf16[256,1536]{1,0:T(8,128)(2,1)S(1)}, bf16[256,1536]{1,0:T(8,128)(2,1)S(1)}) custom-call(bf16[512,2048]{1,0:T(8,128)(2,1)S(1)} %bitcast.14, bf16[2048,3584]{1,0:T(8,128)(2,1)} %codes.3, f32[16,28]{1,0:T(8,128)S(1)} %copy-done.9), custom_call_target="tpu_custom_call" | custom-call | flops 1 | bytes 1 | tf_op jit(solution)/shard_map/pallas_call | solution.py:32
  58.5 0.6 collective-permute-start.5
  59.1 3.8 %collective-permute-start.10 = (bf16[2,128,1024]{2,1,0:T(8,128)(2,1)S(1)}, bf16[2,128,1024]{2,1,0:T(8,128)(2,1)S(1)}, u32[]{:S(2)}, u32[]{:S(2)}) collective-permute-start(bf16[2,128,1024]{2,1,0:T(8,128)(2,1)S(1)} %pad_maximum_fusion.own), channel_id=1, source_target_pairs={{0,12},{12,0},{4,8},{8,4},{1,13},{13,1},{5,9},{9,5},{2,14},{14,2},... | collective-permute-start | bytes 1572872 | tf_op jit(solution)/shard_map/ppermute | solution.py:283
  62.9 10.4 %shard_map.79 = (bf16[512,512]{1,0:T(8,128)(2,1)S(1)}, bf16[512,512]{1,0:T(8,128)(2,1)}, bf16[512,512]{1,0:T(8,128)(2,1)S(1)}, bf16[512,512]{1,0:T(8,128)(2,1)S(1)}) custom-call(bf16[512,2048]{1,0:T(8,128)(2,1)S(1)} %bitcast.15, bf16[2048,3584]{1,0:T(8,128)(2,1)} %codes.3, f32[16,28]{1,0:T(8,128)S(1)} %copy-done.10), custom_call_target="tpu_custom_call" | custom-call | flops 1 | bytes 1 | tf_op jit(solution)/shard_map/pallas_call | solution.py:32
  73.3 0.5 collective-permute-start.6
  73.8 2.4 %collective-permute-done.5.other = bf16[256,1536]{1,0:T(8,128)(2,1)S(1)} collective-permute-done((bf16[256,1536]{1,0:T(8,128)(2,1)S(1)}, bf16[256,1536]{1,0:T(8,128)(2,1)S(1)}, u32[]{:S(2)}, u32[]{:S(2)}) %collective-permute-start.5) | collective-permute-done | bytes 786464 | tf_op jit(solution)/shard_map/ppermute | solution.py:15
  76.7 0.7 collective-permute-start.8
  77.4 0.7 collective-permute-start.11
  78.1 5.4 %collective-permute-done.10.across = bf16[2,128,1024]{2,1,0:T(8,128)(2,1)S(1)} collective-permute-done((bf16[2,128,1024]{2,1,0:T(8,128)(2,1)S(1)}, bf16[2,128,1024]{2,1,0:T(8,128)(2,1)S(1)}, u32[]{:S(2)}, u32[]{:S(2)}) %collective-permute-start.10) | collective-permute-done | bytes 524320 | tf_op jit(solution)/shard_map/ppermute | solution.py:283
  83.5 1.3 collective-permute-start.12
  84.8 3.3 %collective-permute-done.6.other = bf16[512,512]{1,0:T(8,128)(2,1)S(1)} collective-permute-done((bf16[512,512]{1,0:T(8,128)(2,1)S(1)}, bf16[512,512]{1,0:T(8,128)(2,1)S(1)}, u32[]{:S(2)}, u32[]{:S(2)}) %collective-permute-start.6) | collective-permute-done | bytes 524320 | tf_op jit(solution)/shard_map/ppermute | solution.py:15
  88.1 1.8 %shard_map.83 = (bf16[2,256,512]{2,1,0:T(8,128)(2,1)S(1)}, bf16[2,256,512]{2,1,0:T(8,128)(2,1)S(1)}) custom-call(bf16[512,512]{1,0:T(8,128)(2,1)S(1)} %shard_map.80.own, bf16[512,512]{1,0:T(8,128)(2,1)S(1)} %collective-permute-done.6.other, bf16[1,256,3584]{2,1,0:T(8,128)(2,1)S(1)} %copy-done.1, bf16[1,256,3584]{2,1,0:T(8,128)(2,1)S(1)} %copy-done.3, ...), custom_call_target="tpu_custom_call" | custom-call | flops 1 | bytes 1 | tf_op jit(solution)/shard_map/pallas_call | solution.py:32
  90.6 6.4 %collective-permute-done.8.theirs = bf16[2,256,512]{2,1,0:T(8,128)(2,1)S(1)} collective-permute-done((bf16[2,256,512]{2,1,0:T(8,128)(2,1)S(1)}, bf16[2,256,512]{2,1,0:T(8,128)(2,1)S(1)}, u32[]{:S(2)}, u32[]{:S(2)}) %collective-permute-start.8) | collective-permute-done | bytes 524320 | tf_op jit(solution)/shard_map/ppermute | solution.py:15
  97.0 0.5 collective-permute-start.15
  97.5 0.9 shard_map.85
  98.4 3.7 %shard_map.86 = (f32[3584,1024]{1,0:T(8,128)}, f32[3584,1024]{1,0:T(8,128)}) custom-call(bf16[1024,1024]{1,0:T(8,128)(2,1)S(1)} %bitcast.7, bf16[2,256,512]{2,1,0:T(8,128)(2,1)S(1)} %get-tuple-element.89.mine, bf16[2,256,512]{2,1,0:T(8,128)(2,1)S(1)} %get-tuple-element.90.theirs, bf16[2,256,512]{2,1,0:T(8,128)(2,1)S(1)} %collective-permute-done.13.mine_far, ...), custom_call_target="tpu_custom_call" | custom-call | flops 1 | bytes 1 | tf_op jit(solution)/shard_map/pallas_call | solution.py:32
  102.7 1.5 collective-permute-start.18
  104.2 7.9 %collective-permute-done.15.other = bf16[512,512]{1,0:T(8,128)(2,1)S(1)} collective-permute-done((bf16[512,512]{1,0:T(8,128)(2,1)}, bf16[512,512]{1,0:T(8,128)(2,1)S(1)}, u32[]{:S(2)}, u32[]{:S(2)}) %collective-permute-start.15) | collective-permute-done | bytes 524320 | tf_op jit(solution)/shard_map/ppermute | solution.py:15
  112.1 1.8 %shard_map.88 = (bf16[2,256,512]{2,1,0:T(8,128)(2,1)S(1)}, bf16[2,256,512]{2,1,0:T(8,128)(2,1)S(1)}) custom-call(bf16[512,512]{1,0:T(8,128)(2,1)} %shard_map.84.own, bf16[512,512]{1,0:T(8,128)(2,1)S(1)} %collective-permute-done.15.other, bf16[1,256,3584]{2,1,0:T(8,128)(2,1)S(1)} %copy-done.1, bf16[1,256,3584]{2,1,0:T(8,128)(2,1)S(1)} %copy-done.3, ...), custom_call_target="tpu_custom_call" | custom-call | flops 1 | bytes 1 | tf_op jit(solution)/shard_map/pallas_call | solution.py:32
  113.9 3.7 %shard_map.89 = (f32[3584,1024]{1,0:T(8,128)}, f32[3584,1024]{1,0:T(8,128)}) custom-call(bf16[1024,1024]{1,0:T(8,128)(2,1)S(1)} %bitcast.8, bf16[2,256,512]{2,1,0:T(8,128)(2,1)S(1)} %shard_map.81.mine, bf16[2,256,512]{2,1,0:T(8,128)(2,1)S(1)} %collective-permute-done.8.theirs, ...), custom_call_target="tpu_custom_call", output_to_operand_aliasing={{0}: (5, {}), {1}: (6, {})} | custom-call | flops 1 | bytes 1 | tf_op jit(solution)/shard_map/pallas_call | solution.py:32
  118.2 1.8 %collective-permute-done.18.other = bf16[512,512]{1,0:T(8,128)(2,1)S(1)} collective-permute-done((bf16[512,512]{1,0:T(8,128)(2,1)S(1)}, bf16[512,512]{1,0:T(8,128)(2,1)S(1)}, u32[]{:S(2)}, u32[]{:S(2)}) %collective-permute-start.18) | collective-permute-done | bytes 524320 | tf_op jit(solution)/shard_map/ppermute | solution.py:15
  120.0 1.8 %shard_map.91 = (bf16[2,256,512]{2,1,0:T(8,128)(2,1)S(1)}, bf16[2,256,512]{2,1,0:T(8,128)(2,1)S(1)}) custom-call(bf16[512,512]{1,0:T(8,128)(2,1)S(1)} %shard_map.87.own, bf16[512,512]{1,0:T(8,128)(2,1)S(1)} %collective-permute-done.18.other, bf16[1,256,3584]{2,1,0:T(8,128)(2,1)S(1)} %copy-done.1, bf16[1,256,3584]{2,1,0:T(8,128)(2,1)S(1)} %copy-done.3, ...), custom_call_target="tpu_custom_call" | custom-call | flops 1 | bytes 1 | tf_op jit(solution)/shard_map/pallas_call | solution.py:32
  121.8 3.7 %shard_map.92 = (f32[3584,1024]{1,0:T(8,128)}, f32[3584,1024]{1,0:T(8,128)}) custom-call(bf16[1024,1024]{1,0:T(8,128)(2,1)S(1)} %bitcast.9, bf16[2,256,512]{2,1,0:T(8,128)(2,1)S(1)} %get-tuple-element.105.mine, bf16[2,256,512]{2,1,0:T(8,128)(2,1)S(1)} %get-tuple-element.106.theirs, ...), custom_call_target="tpu_custom_call", output_to_operand_aliasing={{0}: (5, {}), {1}: (6, {})} | custom-call | flops 1 | bytes 1 | tf_op jit(solution)/shard_map/pallas_call | solution.py:32
  126.6 0.6 collective-permute-start.24
  127.2 5.8 %collective-permute-done.21.other = bf16[512,512]{1,0:T(8,128)(2,1)S(1)} collective-permute-done((bf16[512,512]{1,0:T(8,128)(2,1)S(1)}, bf16[512,512]{1,0:T(8,128)(2,1)S(1)}, u32[]{:S(2)}, u32[]{:S(2)}) %collective-permute-start.21) | collective-permute-done | bytes 524320 | tf_op jit(solution)/shard_map/ppermute | solution.py:15
  133.0 1.8 %shard_map.94 = (bf16[2,256,512]{2,1,0:T(8,128)(2,1)S(1)}, bf16[2,256,512]{2,1,0:T(8,128)(2,1)S(1)}) custom-call(bf16[512,512]{1,0:T(8,128)(2,1)S(1)} %shard_map.90.own, bf16[512,512]{1,0:T(8,128)(2,1)S(1)} %collective-permute-done.21.other, bf16[1,256,3584]{2,1,0:T(8,128)(2,1)S(1)} %copy-done.1, bf16[1,256,3584]{2,1,0:T(8,128)(2,1)S(1)} %copy-done.3, ...), custom_call_target="tpu_custom_call" | custom-call | flops 1 | bytes 1 | tf_op jit(solution)/shard_map/pallas_call | solution.py:32
  134.8 3.7 %shard_map.95 = (f32[3584,1024]{1,0:T(8,128)}, f32[3584,1024]{1,0:T(8,128)}) custom-call(bf16[1024,1024]{1,0:T(8,128)(2,1)S(1)} %bitcast.10, bf16[2,256,512]{2,1,0:T(8,128)(2,1)S(1)} %get-tuple-element.114.mine, bf16[2,256,512]{2,1,0:T(8,128)(2,1)S(1)} %get-tuple-element.115.theirs, ...), custom_call_target="tpu_custom_call", output_to_operand_aliasing={{0}: (5, {}), {1}: (6, {})} | custom-call | flops 1 | bytes 1 | tf_op jit(solution)/shard_map/pallas_call | solution.py:32
  139.7 4.6 %collective-permute-done.24.theirs = bf16[2,256,512]{2,1,0:T(8,128)(2,1)S(1)} collective-permute-done((bf16[2,256,512]{2,1,0:T(8,128)(2,1)S(1)}, bf16[2,256,512]{2,1,0:T(8,128)(2,1)S(1)}, u32[]{:S(2)}, u32[]{:S(2)}) %collective-permute-start.24) | collective-permute-done | bytes 524320 | tf_op jit(solution)/shard_map/ppermute | solution.py:15
  144.2 3.7 %shard_map.97 = (f32[3584,1024]{1,0:T(8,128)}, f32[3584,1024]{1,0:T(8,128)}) custom-call(bf16[1024,1024]{1,0:T(8,128)(2,1)S(1)} %bitcast.11, bf16[2,256,512]{2,1,0:T(8,128)(2,1)S(1)} %get-tuple-element.121.mine, bf16[2,256,512]{2,1,0:T(8,128)(2,1)S(1)} %get-tuple-element.122.theirs, ...), custom_call_target="tpu_custom_call", output_to_operand_aliasing={{0}: (5, {}), {1}: (6, {})} | custom-call | flops 1 | bytes 1 | tf_op jit(solution)/shard_map/pallas_call | solution.py:32
  148.5 6.0 %collective-permute-done.27.theirs = bf16[2,256,512]{2,1,0:T(8,128)(2,1)S(1)} collective-permute-done((bf16[2,256,512]{2,1,0:T(8,128)(2,1)S(1)}, bf16[2,256,512]{2,1,0:T(8,128)(2,1)S(1)}, u32[]{:S(2)}, u32[]{:S(2)}) %collective-permute-start.27) | collective-permute-done | bytes 524320 | tf_op jit(solution)/shard_map/ppermute | solution.py:15
  155.0 3.7 %shard_map.98 = (f32[3584,1024]{1,0:T(8,128)}, f32[3584,1024]{1,0:T(8,128)}) custom-call(bf16[1024,1024]{1,0:T(8,128)(2,1)S(1)} %bitcast.12, bf16[2,256,512]{2,1,0:T(8,128)(2,1)S(1)} %shard_map.93.mine, bf16[2,256,512]{2,1,0:T(8,128)(2,1)S(1)} %collective-permute-done.24.theirs, ...), custom_call_target="tpu_custom_call", output_to_operand_aliasing={{0}: (5, {}), {1}: (6, {})} | custom-call | flops 1 | bytes 1 | tf_op jit(solution)/shard_map/pallas_call | solution.py:32
  158.7 3.7 %shard_map.99 = (f32[3584,1024]{1,0:T(8,128)}, f32[3584,1024]{1,0:T(8,128)}) custom-call(bf16[1024,1024]{1,0:T(8,128)(2,1)S(1)} %bitcast.13, bf16[2,256,512]{2,1,0:T(8,128)(2,1)S(1)} %shard_map.96.mine, bf16[2,256,512]{2,1,0:T(8,128)(2,1)S(1)} %collective-permute-done.27.theirs, ...), custom_call_target="tpu_custom_call", output_to_operand_aliasing={{0}: (5, {}), {1}: (6, {})} | custom-call | flops 1 | bytes 1 | tf_op jit(solution)/shard_map/pallas_call | solution.py:32
  (64 shorter events, 5.5 us)
Async XLA Ops:
  0.6 15.7 %collective-permute-start = (bf16[1,128,2048]{2,1,0:T(8,128)(2,1)}, bf16[1,128,2048]{2,1,0:T(8,128)(2,1)S(1)}, u32[]{:S(2)}, u32[]{:S(2)}) collective-permute-start(bf16[1,128,2048]{2,1,0:T(8,128)(2,1)} %own.1), channel_id=1, source_target_pairs={{0,4},{4,0},{8,12},{12,8},{1,5},{5,1},{9,13},{13,9},{2,6},{6,2},{1... | collective-permute-start | bytes 1572872 | tf_op jit(solution)/shard_map/ppermute | solution.py:282
  3.7 1.5 copy-start
  5.2 1.5 copy-start.2
  6.7 56.2 %copy-start.10 = (f32[16,28]{1,0:T(8,128)S(1)}, f32[16,28]{1,0:T(8,128)}, u32[]{:S(2)}) copy-start(f32[16,28]{1,0:T(8,128)} %scales.3) | copy-start | bytes 5380
  7.2 80.9 %collective-permute-start.7 = (bf16[2,256,2048]{2,1,0:T(8,128)(2,1)S(1)}, bf16[2,256,2048]{2,1,0:T(8,128)(2,1)}, u32[]{:S(2)}, u32[]{:S(2)}) collective-permute-start(bf16[2,256,2048]{2,1,0:T(8,128)(2,1)S(1)} %shard_map.82), channel_id=1, source_target_pairs={{0,2},{2,0},{1,3},{3,1},{4,6},{6,4},{5,7},{7,5},{8,10},{10,8},{9,1... | collective-permute-start | bytes 6291464 | tf_op jit(solution)/shard_map/ppermute | solution.py:15
  8.8 20.7 %collective-permute-start.1 = (bf16[1,128,2048]{2,1,0:T(8,128)(2,1)}, bf16[1,128,2048]{2,1,0:T(8,128)(2,1)}, u32[]{:S(2)}, u32[]{:S(2)}) collective-permute-start(bf16[1,128,2048]{2,1,0:T(8,128)(2,1)} %own.1), channel_id=1, source_target_pairs={{0,12},{12,0},{4,8},{8,4},{1,13},{13,1},{5,9},{9,5},{2,14},{14,2},... | collective-permute-start | bytes 1572872 | tf_op jit(solution)/shard_map/ppermute | solution.py:283
  16.4 1.5 collective-permute-start.2
  18.0 12.9 %collective-permute-start.3 = (bf16[1,128,2048]{2,1,0:T(8,128)(2,1)S(1)}, bf16[1,128,2048]{2,1,0:T(8,128)(2,1)}, u32[]{:S(2)}, u32[]{:S(2)}) collective-permute-start(bf16[1,128,2048]{2,1,0:T(8,128)(2,1)S(1)} %collective-permute-done.buddy), channel_id=1, source_target_pairs={{4,8},{8,4},{5,9},{9,5},{6,10},{10,6},{7,11},{11,7},{20,24},{24,20... | collective-permute-start | bytes 1572872 | tf_op jit(solution)/shard_map/ppermute | solution.py:290
  29.5 17.7 %collective-permute-start.4 = (bf16[1,128,2048]{2,1,0:T(8,128)(2,1)}, bf16[1,128,2048]{2,1,0:T(8,128)(2,1)}, u32[]{:S(2)}, u32[]{:S(2)}) collective-permute-start(bf16[1,128,2048]{2,1,0:T(8,128)(2,1)} %collective-permute-done.1.across), channel_id=1, source_target_pairs={{4,0},{8,12},{5,1},{9,13},{6,2},{10,14},{7,3},{11,15},{20,16},{24,... | collective-permute-start | bytes 1572872 | tf_op jit(solution)/shard_map/ppermute | solution.py:287
  47.2 1.0 copy-start.8
  50.3 0.7 copy-start.9
  51.0 25.2 %copy-start.1 = (bf16[1,256,3584]{2,1,0:T(8,128)(2,1)S(1)}, bf16[1,256,3584]{2,1,0:T(8,128)(2,1)}, u32[]{:S(2)}) copy-start(bf16[1,256,3584]{2,1,0:T(8,128)(2,1)} %gates.15) | copy-start | bytes 5505028
  51.0 25.2 %copy-start.3 = (bf16[1,256,3584]{2,1,0:T(8,128)(2,1)S(1)}, bf16[1,256,3584]{2,1,0:T(8,128)(2,1)}, u32[]{:S(2)}) copy-start(bf16[1,256,3584]{2,1,0:T(8,128)(2,1)} %ups.15) | copy-start | bytes 5505028
  58.5 17.7 %collective-permute-start.5 = (bf16[256,1536]{1,0:T(8,128)(2,1)S(1)}, bf16[256,1536]{1,0:T(8,128)(2,1)S(1)}, u32[]{:S(2)}, u32[]{:S(2)}) collective-permute-start(bf16[256,1536]{1,0:T(8,128)(2,1)S(1)} %get-tuple-element.72), channel_id=1, source_target_pairs={{0,2},{2,0},{1,3},{3,1},{4,6},{6,4},{5,7},{7,5},{8,10},{10,8},{9,1... | collective-permute-start | bytes 2359304 | tf_op jit(solution)/shard_map/ppermute | solution.py:15
  59.1 18.4 %collective-permute-start.9 = (bf16[2,128,1024]{2,1,0:T(8,128)(2,1)S(1)}, bf16[2,128,1024]{2,1,0:T(8,128)(2,1)S(1)}, u32[]{:S(2)}, u32[]{:S(2)}) collective-permute-start(bf16[2,128,1024]{2,1,0:T(8,128)(2,1)S(1)} %pad_maximum_fusion.own), channel_id=1, source_target_pairs={{0,4},{4,0},{8,12},{12,8},{1,5},{5,1},{9,13},{13,9},{2,6},{6,2},{1... | collective-permute-start | bytes 1572872 | tf_op jit(solution)/shard_map/ppermute | solution.py:282
  59.1 24.4 %collective-permute-start.10 = (bf16[2,128,1024]{2,1,0:T(8,128)(2,1)S(1)}, bf16[2,128,1024]{2,1,0:T(8,128)(2,1)S(1)}, u32[]{:S(2)}, u32[]{:S(2)}) collective-permute-start(bf16[2,128,1024]{2,1,0:T(8,128)(2,1)S(1)} %pad_maximum_fusion.own), channel_id=1, source_target_pairs={{0,12},{12,0},{4,8},{8,4},{1,13},{13,1},{5,9},{9,5},{2,14},{14,2},... | collective-permute-start | bytes 1572872 | tf_op jit(solution)/shard_map/ppermute | solution.py:283
  73.3 10.2 %copy-start.4 = (bf16[512,512]{1,0:T(8,128)(2,1)}, bf16[512,512]{1,0:T(8,128)(2,1)S(1)}, u32[]{:S(2)}) copy-start(bf16[512,512]{1,0:T(8,128)(2,1)S(1)} %get-tuple-element.100.value) | copy-start | bytes 1572868
  73.3 11.5 %copy-start.6 = (bf16[512,512]{1,0:T(8,128)(2,1)}, bf16[512,512]{1,0:T(8,128)(2,1)S(1)}, u32[]{:S(2)}) copy-start(bf16[512,512]{1,0:T(8,128)(2,1)S(1)} %get-tuple-element.92.value) | copy-start | bytes 1572868
  73.3 14.9 %collective-permute-start.6 = (bf16[512,512]{1,0:T(8,128)(2,1)S(1)}, bf16[512,512]{1,0:T(8,128)(2,1)S(1)}, u32[]{:S(2)}, u32[]{:S(2)}) collective-permute-start(bf16[512,512]{1,0:T(8,128)(2,1)S(1)} %shard_map.80.own), channel_id=1, source_target_pairs={{0,2},{2,0},{1,3},{3,1},{4,6},{6,4},{5,7},{7,5},{8,10},{10,8},{9,1... | collective-permute-start | bytes 1572872 | tf_op jit(solution)/shard_map/ppermute | solution.py:15
  76.7 20.3 %collective-permute-start.8 = (bf16[2,256,512]{2,1,0:T(8,128)(2,1)S(1)}, bf16[2,256,512]{2,1,0:T(8,128)(2,1)S(1)}, u32[]{:S(2)}, u32[]{:S(2)}) collective-permute-start(bf16[2,256,512]{2,1,0:T(8,128)(2,1)S(1)} %shard_map.81.mine), channel_id=1, source_target_pairs={{0,2},{2,0},{1,3},{3,1},{4,6},{6,4},{5,7},{7,5},{8,10},{10,8},{9,1... | collective-permute-start | bytes 1572872 | tf_op jit(solution)/shard_map/ppermute | solution.py:15
  77.4 20.1 %collective-permute-start.11 = (bf16[2,128,1024]{2,1,0:T(8,128)(2,1)S(1)}, bf16[2,128,1024]{2,1,0:T(8,128)(2,1)S(1)}, u32[]{:S(2)}, u32[]{:S(2)}) collective-permute-start(bf16[2,128,1024]{2,1,0:T(8,128)(2,1)S(1)} %collective-permute-done.9.buddy), channel_id=1, source_target_pairs={{4,8},{8,4},{5,9},{9,5},{6,10},{10,6},{7,11},{11,7},{20,24},{24,20... | collective-permute-start | bytes 1572872 | tf_op jit(solution)/shard_map/ppermute | solution.py:290
  83.5 14.0 %collective-permute-start.12 = (bf16[2,128,1024]{2,1,0:T(8,128)(2,1)S(1)}, bf16[2,128,1024]{2,1,0:T(8,128)(2,1)S(1)}, u32[]{:S(2)}, u32[]{:S(2)}) collective-permute-start(bf16[2,128,1024]{2,1,0:T(8,128)(2,1)S(1)} %collective-permute-done.10.across), channel_id=1, source_target_pairs={{4,0},{8,12},{5,1},{9,13},{6,2},{10,14},{7,3},{11,15},{20,16},{24,... | collective-permute-start | bytes 1572872 | tf_op jit(solution)/shard_map/ppermute | solution.py:287
  88.1 14.5 %copy-start.7 = (bf16[512,512]{1,0:T(8,128)(2,1)S(1)}, bf16[512,512]{1,0:T(8,128)(2,1)}, u32[]{:S(2)}) copy-start(bf16[512,512]{1,0:T(8,128)(2,1)} %copy-done.6) | copy-start | bytes 1572868
  90.0 8.4 %collective-permute-start.13 = (bf16[2,256,512]{2,1,0:T(8,128)(2,1)S(1)}, bf16[2,256,512]{2,1,0:T(8,128)(2,1)S(1)}, u32[]{:S(2)}, u32[]{:S(2)}) collective-permute-start(bf16[2,256,512]{2,1,0:T(8,128)(2,1)S(1)} %get-tuple-element.89.mine), channel_id=1, source_target_pairs={{0,1},{1,0},{2,3},{3,2},{4,5},{5,4},{6,7},{7,6},{8,9},{9,8},{10,11... | collective-permute-start | bytes 1572872 | tf_op jit(solution)/shard_map/ppermute | solution.py:15
  90.1 8.4 %collective-permute-start.14 = (bf16[2,256,512]{2,1,0:T(8,128)(2,1)S(1)}, bf16[2,256,512]{2,1,0:T(8,128)(2,1)S(1)}, u32[]{:S(2)}, u32[]{:S(2)}) collective-permute-start(bf16[2,256,512]{2,1,0:T(8,128)(2,1)S(1)} %get-tuple-element.90.theirs), channel_id=1, source_target_pairs={{0,1},{1,0},{2,3},{3,2},{4,5},{5,4},{6,7},{7,6},{8,9},{9,8},{10,11... | collective-permute-start | bytes 1572872 | tf_op jit(solution)/shard_map/ppermute | solution.py:15
  97.0 15.1 %collective-permute-start.15 = (bf16[512,512]{1,0:T(8,128)(2,1)}, bf16[512,512]{1,0:T(8,128)(2,1)S(1)}, u32[]{:S(2)}, u32[]{:S(2)}) collective-permute-start(bf16[512,512]{1,0:T(8,128)(2,1)} %shard_map.84.own), channel_id=1, source_target_pairs={{0,2},{2,0},{1,3},{3,1},{4,6},{6,4},{5,7},{7,5},{8,10},{10,8},{9,1... | collective-permute-start | bytes 1572872 | tf_op jit(solution)/shard_map/ppermute | solution.py:15
  102.2 11.7 %collective-permute-start.16 = (bf16[2,256,512]{2,1,0:T(8,128)(2,1)S(1)}, bf16[2,256,512]{2,1,0:T(8,128)(2,1)S(1)}, u32[]{:S(2)}, u32[]{:S(2)}) collective-permute-start(bf16[2,256,512]{2,1,0:T(8,128)(2,1)S(1)} %shard_map.81.mine), channel_id=1, source_target_pairs={{0,1},{1,0},{2,3},{3,2},{4,5},{5,4},{6,7},{7,6},{8,9},{9,8},{10,11... | collective-permute-start | bytes 1572872 | tf_op jit(solution)/shard_map/ppermute | solution.py:15
  102.2 11.7 %collective-permute-start.17 = (bf16[2,256,512]{2,1,0:T(8,128)(2,1)S(1)}, bf16[2,256,512]{2,1,0:T(8,128)(2,1)S(1)}, u32[]{:S(2)}, u32[]{:S(2)}) collective-permute-start(bf16[2,256,512]{2,1,0:T(8,128)(2,1)S(1)} %collective-permute-done.8.theirs), channel_id=1, source_target_pairs={{0,1},{1,0},{2,3},{3,2},{4,5},{5,4},{6,7},{7,6},{8,9},{9,8},{10,11... | collective-permute-start | bytes 1572872 | tf_op jit(solution)/shard_map/ppermute | solution.py:15
  102.7 17.3 %collective-permute-start.18 = (bf16[512,512]{1,0:T(8,128)(2,1)S(1)}, bf16[512,512]{1,0:T(8,128)(2,1)S(1)}, u32[]{:S(2)}, u32[]{:S(2)}) collective-permute-start(bf16[512,512]{1,0:T(8,128)(2,1)S(1)} %shard_map.87.own), channel_id=1, source_target_pairs={{0,2},{2,0},{1,3},{3,1},{4,6},{6,4},{5,7},{7,5},{8,10},{10,8},{9,1... | collective-permute-start | bytes 1572872 | tf_op jit(solution)/shard_map/ppermute | solution.py:15
  113.9 4.3 %copy-start.5 = (bf16[512,512]{1,0:T(8,128)(2,1)S(1)}, bf16[512,512]{1,0:T(8,128)(2,1)}, u32[]{:S(2)}) copy-start(bf16[512,512]{1,0:T(8,128)(2,1)} %copy-done.4) | copy-start | bytes 1572868
  117.7 4.1 %collective-permute-start.19 = (bf16[2,256,512]{2,1,0:T(8,128)(2,1)S(1)}, bf16[2,256,512]{2,1,0:T(8,128)(2,1)S(1)}, u32[]{:S(2)}, u32[]{:S(2)}) collective-permute-start(bf16[2,256,512]{2,1,0:T(8,128)(2,1)S(1)} %get-tuple-element.105.mine), channel_id=1, source_target_pairs={{0,1},{1,0},{2,3},{3,2},{4,5},{5,4},{6,7},{7,6},{8,9},{9,8},{10,11... | collective-permute-start | bytes 1572872 | tf_op jit(solution)/shard_map/ppermute | solution.py:15
  117.7 4.1 %collective-permute-start.20 = (bf16[2,256,512]{2,1,0:T(8,128)(2,1)S(1)}, bf16[2,256,512]{2,1,0:T(8,128)(2,1)S(1)}, u32[]{:S(2)}, u32[]{:S(2)}) collective-permute-start(bf16[2,256,512]{2,1,0:T(8,128)(2,1)S(1)} %get-tuple-element.106.theirs), channel_id=1, source_target_pairs={{0,1},{1,0},{2,3},{3,2},{4,5},{5,4},{6,7},{7,6},{8,9},{9,8},{10,11... | collective-permute-start | bytes 1572872 | tf_op jit(solution)/shard_map/ppermute | solution.py:15
  118.2 14.8 %collective-permute-start.21 = (bf16[512,512]{1,0:T(8,128)(2,1)S(1)}, bf16[512,512]{1,0:T(8,128)(2,1)S(1)}, u32[]{:S(2)}, u32[]{:S(2)}) collective-permute-start(bf16[512,512]{1,0:T(8,128)(2,1)S(1)} %shard_map.90.own), channel_id=1, source_target_pairs={{0,2},{2,0},{1,3},{3,1},{4,6},{6,4},{5,7},{7,5},{8,10},{10,8},{9,1... | collective-permute-start | bytes 1572872 | tf_op jit(solution)/shard_map/ppermute | solution.py:15
  125.6 9.2 %collective-permute-start.22 = (bf16[2,256,512]{2,1,0:T(8,128)(2,1)S(1)}, bf16[2,256,512]{2,1,0:T(8,128)(2,1)S(1)}, u32[]{:S(2)}, u32[]{:S(2)}) collective-permute-start(bf16[2,256,512]{2,1,0:T(8,128)(2,1)S(1)} %get-tuple-element.114.mine), channel_id=1, source_target_pairs={{0,1},{1,0},{2,3},{3,2},{4,5},{5,4},{6,7},{7,6},{8,9},{9,8},{10,11... | collective-permute-start | bytes 1572872 | tf_op jit(solution)/shard_map/ppermute | solution.py:15
  125.6 9.2 %collective-permute-start.23 = (bf16[2,256,512]{2,1,0:T(8,128)(2,1)S(1)}, bf16[2,256,512]{2,1,0:T(8,128)(2,1)S(1)}, u32[]{:S(2)}, u32[]{:S(2)}) collective-permute-start(bf16[2,256,512]{2,1,0:T(8,128)(2,1)S(1)} %get-tuple-element.115.theirs), channel_id=1, source_target_pairs={{0,1},{1,0},{2,3},{3,2},{4,5},{5,4},{6,7},{7,6},{8,9},{9,8},{10,11... | collective-permute-start | bytes 1572872 | tf_op jit(solution)/shard_map/ppermute | solution.py:15
  126.6 17.6 %collective-permute-start.24 = (bf16[2,256,512]{2,1,0:T(8,128)(2,1)S(1)}, bf16[2,256,512]{2,1,0:T(8,128)(2,1)S(1)}, u32[]{:S(2)}, u32[]{:S(2)}) collective-permute-start(bf16[2,256,512]{2,1,0:T(8,128)(2,1)S(1)} %shard_map.93.mine), channel_id=1, source_target_pairs={{0,2},{2,0},{1,3},{3,1},{4,6},{6,4},{5,7},{7,5},{8,10},{10,8},{9,1... | collective-permute-start | bytes 1572872 | tf_op jit(solution)/shard_map/ppermute | solution.py:15
  138.5 5.7 %collective-permute-start.25 = (bf16[2,256,512]{2,1,0:T(8,128)(2,1)S(1)}, bf16[2,256,512]{2,1,0:T(8,128)(2,1)S(1)}, u32[]{:S(2)}, u32[]{:S(2)}) collective-permute-start(bf16[2,256,512]{2,1,0:T(8,128)(2,1)S(1)} %get-tuple-element.121.mine), channel_id=1, source_target_pairs={{0,1},{1,0},{2,3},{3,2},{4,5},{5,4},{6,7},{7,6},{8,9},{9,8},{10,11... | collective-permute-start | bytes 1572872 | tf_op jit(solution)/shard_map/ppermute | solution.py:15
  138.6 5.7 %collective-permute-start.26 = (bf16[2,256,512]{2,1,0:T(8,128)(2,1)S(1)}, bf16[2,256,512]{2,1,0:T(8,128)(2,1)S(1)}, u32[]{:S(2)}, u32[]{:S(2)}) collective-permute-start(bf16[2,256,512]{2,1,0:T(8,128)(2,1)S(1)} %get-tuple-element.122.theirs), channel_id=1, source_target_pairs={{0,1},{1,0},{2,3},{3,2},{4,5},{5,4},{6,7},{7,6},{8,9},{9,8},{10,11... | collective-permute-start | bytes 1572872 | tf_op jit(solution)/shard_map/ppermute | solution.py:15
  139.6 14.9 %collective-permute-start.27 = (bf16[2,256,512]{2,1,0:T(8,128)(2,1)S(1)}, bf16[2,256,512]{2,1,0:T(8,128)(2,1)S(1)}, u32[]{:S(2)}, u32[]{:S(2)}) collective-permute-start(bf16[2,256,512]{2,1,0:T(8,128)(2,1)S(1)} %shard_map.96.mine), channel_id=1, source_target_pairs={{0,2},{2,0},{1,3},{3,1},{4,6},{6,4},{5,7},{7,5},{8,10},{10,8},{9,1... | collective-permute-start | bytes 1572872 | tf_op jit(solution)/shard_map/ppermute | solution.py:15
  148.0 7.0 %collective-permute-start.28 = (bf16[2,256,512]{2,1,0:T(8,128)(2,1)S(1)}, bf16[2,256,512]{2,1,0:T(8,128)(2,1)S(1)}, u32[]{:S(2)}, u32[]{:S(2)}) collective-permute-start(bf16[2,256,512]{2,1,0:T(8,128)(2,1)S(1)} %shard_map.93.mine), channel_id=1, source_target_pairs={{0,1},{1,0},{2,3},{3,2},{4,5},{5,4},{6,7},{7,6},{8,9},{9,8},{10,11... | collective-permute-start | bytes 1572872 | tf_op jit(solution)/shard_map/ppermute | solution.py:15
  148.0 7.0 %collective-permute-start.29 = (bf16[2,256,512]{2,1,0:T(8,128)(2,1)S(1)}, bf16[2,256,512]{2,1,0:T(8,128)(2,1)S(1)}, u32[]{:S(2)}, u32[]{:S(2)}) collective-permute-start(bf16[2,256,512]{2,1,0:T(8,128)(2,1)S(1)} %collective-permute-done.24.theirs), channel_id=1, source_target_pairs={{0,1},{1,0},{2,3},{3,2},{4,5},{5,4},{6,7},{7,6},{8,9},{9,8},{10,11... | collective-permute-start | bytes 1572872 | tf_op jit(solution)/shard_map/ppermute | solution.py:15
  154.5 4.3 %collective-permute-start.30 = (bf16[2,256,512]{2,1,0:T(8,128)(2,1)S(1)}, bf16[2,256,512]{2,1,0:T(8,128)(2,1)S(1)}, u32[]{:S(2)}, u32[]{:S(2)}) collective-permute-start(bf16[2,256,512]{2,1,0:T(8,128)(2,1)S(1)} %shard_map.96.mine), channel_id=1, source_target_pairs={{0,1},{1,0},{2,3},{3,2},{4,5},{5,4},{6,7},{7,6},{8,9},{9,8},{10,11... | collective-permute-start | bytes 1572872 | tf_op jit(solution)/shard_map/ppermute | solution.py:15
  154.5 4.3 %collective-permute-start.31 = (bf16[2,256,512]{2,1,0:T(8,128)(2,1)S(1)}, bf16[2,256,512]{2,1,0:T(8,128)(2,1)S(1)}, u32[]{:S(2)}, u32[]{:S(2)}) collective-permute-start(bf16[2,256,512]{2,1,0:T(8,128)(2,1)S(1)} %collective-permute-done.27.theirs), channel_id=1, source_target_pairs={{0,1},{1,0},{2,3},{3,2},{4,5},{5,4},{6,7},{7,6},{8,9},{9,8},{10,11... | collective-permute-start | bytes 1572872 | tf_op jit(solution)/shard_map/ppermute | solution.py:15
